TPU v7x, 32 devices: a whole 2x2x4 slice. The times are simulated.
32 devices in a mesh: grp: 4 (over y, x), pts: 8 (over z, core).
Axes of the slice: x: 2, y: 2, z: 4, core: 2. Of those that a mesh axis runs over, the one named last changes fastest.
Arguments:
- points: bfloat16 [32768, 512], P(('grp', 'pts')), may hold values from -16 to 16
- ball_ids: int32 [64, 512], P(('grp', 'pts')), may hold values from 0 to 3, never falling along the last dimension, each value on 1 to 256 neighbouring positions
- send_pick: int32 [32, 8], P(('grp', 'pts')), may hold values from 0 to 8, as said below
- recv_from: int32 [32, 8], P(('grp', 'pts')), may hold values from 0 to 7, as said below
- gain_one: float32 [512], replicated, may hold values from 0.1 to 1.9
- attn_in_one: bfloat16 [512, 1536], replicated, may hold values from -2 to 2
- attn_out_one: bfloat16 [512, 512], replicated, may hold values from -0.25 to 0.25
- gain_two: float32 [512], replicated, may hold values from 0.1 to 1.9
- mlp_up: bfloat16 [512, 2048], replicated, may hold values from -0.25 to 0.25
- mlp_down: bfloat16 [2048, 512], replicated, may hold values from -0.125 to 0.125
- gain_three: float32 [512], replicated, may hold values from 0.1 to 1.9
- compress_proj: bfloat16 [512, 1024], replicated, may hold values from -2 to 2
- attn_in_two: bfloat16 [512, 1536], replicated, may hold values from -2 to 2
- attn_out_two: bfloat16 [512, 512], replicated, may hold values from -0.25 to 0.25
Outputs:
- second: bfloat16 [32768, 512], P(('grp', 'pts'))
Inputs may be any that keep to these rules, and one draw needn't show every extreme that they name: `send_pick`: slot q + c of device d goes to the device of pts index q in d's grp row; an entry is the local leaf block sent there, or 8 for an empty slot; each of a device's 8 blocks stands in exactly one slot, and every device receives exactly 8 blocks. `recv_from`: entry j of row d is the received slot p + c (p the sender's pts index in d's grp row, c its slot toward d) that fills rotated position j; a row's entries are distinct and are exactly the non-empty slots that device d receives according to send_pick.
All inputs are finite; a program needn't handle non-finite values.
Results may differ from a plain program's by a relative error of at most 0.017.
The roundings to bfloat16 on the way count: a program that leaves them out, or rounds other values in their place, can miss the bound.
Values may be sent and summed in bfloat16 or wider, within the bound.
No kernel may reach another device: no remote copies, remote signals or barrier semaphores. Data moves between devices by JAX's collectives and lax.ppermute only.
A program may use at most 128 MiB of HBM per device.

v0:
```python
from functools import partial

import jax
import jax.numpy as jnp
from jax import lax
from jax.sharding import PartitionSpec as P

D = 512
HEADS = 8
HEAD = 64
LEAF = 128
BALL = 512
CMP = 256


def norm_rows(values, gain):
    wide = values.astype(jnp.float32)
    return wide * lax.rsqrt(jnp.mean(wide * wide, axis=-1, keepdims=True) + 1e-06) * gain


def softmax_rows(scores):
    top = jnp.max(scores, axis=-1, keepdims=True)
    expo = jnp.exp(scores - top)
    return expo / jnp.sum(expo, axis=-1, keepdims=True)


def first_ball(packed):
    rows, member = packed
    scores = jnp.einsum(
        "qhd,khd->hqk", rows[:, 0], rows[:, 1], preferred_element_type=jnp.float32
    ) * HEAD ** (-0.5)
    same_ball = member[:, None] == member[None, :]
    scores = jnp.where(same_ball[None], scores, -1e30)
    weights = softmax_rows(scores).astype(jnp.bfloat16)
    mixed = jnp.einsum("hqk,khd->qhd", weights, rows[:, 2], preferred_element_type=jnp.float32)
    return mixed.astype(jnp.bfloat16).reshape(rows.shape[0], D)


def second_ball(rows, comp_keys, comp_values):
    queries = rows[:, 0]
    scores = jnp.einsum(
        "qhd,khd->hqk", queries, rows[:, 1], preferred_element_type=jnp.float32
    ) * HEAD ** (-0.5)
    weights = softmax_rows(scores).astype(jnp.bfloat16)
    local_out = jnp.einsum("hqk,khd->qhd", weights, rows[:, 2], preferred_element_type=jnp.float32)
    comp_scores = jnp.einsum(
        "qhd,khd->hqk", queries, comp_keys, preferred_element_type=jnp.float32
    ) * HEAD ** (-0.5)
    comp_weights = softmax_rows(comp_scores).astype(jnp.bfloat16)
    comp_out = jnp.einsum(
        "hqk,khd->qhd", comp_weights, comp_values, preferred_element_type=jnp.float32
    )
    return (local_out + comp_out).astype(jnp.bfloat16).reshape(rows.shape[0], D)


def shards(
    points,
    ball_ids,
    send_pick,
    recv_from,
    gain_one,
    attn_in_one,
    attn_out_one,
    gain_two,
    mlp_up,
    mlp_down,
    gain_three,
    compress_proj,
    attn_in_two,
    attn_out_two,
):
    count = points.shape[0]
    blocks_total = recv_from.shape[1]
    slots_total = send_pick.shape[1]
    normed = norm_rows(points, gain_one).astype(jnp.bfloat16)
    proj = jnp.dot(normed, attn_in_one, preferred_element_type=jnp.float32).astype(jnp.bfloat16)
    proj = proj.reshape(count // BALL, BALL, 3, HEADS, HEAD)
    mixed = lax.map(first_ball, (proj, ball_ids)).reshape(count, D)
    middle = (
        points.astype(jnp.float32)
        + jnp.dot(mixed, attn_out_one, preferred_element_type=jnp.float32)
    ).astype(jnp.bfloat16)
    inner = norm_rows(middle, gain_two).astype(jnp.bfloat16)
    hidden = jax.nn.gelu(jnp.dot(inner, mlp_up, preferred_element_type=jnp.float32)).astype(
        jnp.bfloat16
    )
    layer_one = (
        middle.astype(jnp.float32) + jnp.dot(hidden, mlp_down, preferred_element_type=jnp.float32)
    ).astype(jnp.bfloat16)
    normed_two = norm_rows(layer_one, gain_three).astype(jnp.bfloat16)
    pooled = (
        jnp.sum(normed_two.reshape(count // CMP, CMP, D), axis=1, dtype=jnp.float32) * CMP ** (-0.5)
    ).astype(jnp.bfloat16)
    local_comp = jnp.dot(pooled, compress_proj, preferred_element_type=jnp.float32).astype(
        jnp.bfloat16
    )
    comp = lax.all_gather(local_comp, ("grp", "pts"), axis=0, tiled=True)
    comp_keys = comp[:, :D].reshape(-1, HEADS, HEAD)
    comp_values = comp[:, D:].reshape(-1, HEADS, HEAD)
    empty_block = jnp.zeros((1, LEAF, D), jnp.bfloat16)
    padded = jnp.concatenate([normed_two.reshape(blocks_total, LEAF, D), empty_block], axis=0)
    arrived = lax.all_to_all(padded[send_pick[0]], "pts", split_axis=0, concat_axis=0, tiled=True)
    rotated = arrived[recv_from[0]].reshape(count, D)
    proj_two = jnp.dot(rotated, attn_in_two, preferred_element_type=jnp.float32).astype(
        jnp.bfloat16
    )
    proj_two = proj_two.reshape(count // BALL, BALL, 3, HEADS, HEAD)
    branch = lax.map(
        partial(second_ball, comp_keys=comp_keys, comp_values=comp_values), proj_two
    ).reshape(count, D)
    slot_index = jnp.arange(slots_total, dtype=jnp.int32)
    block_index = jnp.arange(blocks_total, dtype=jnp.int32)
    matches = recv_from[0][None, :] == slot_index[:, None]
    filled = jnp.any(matches, axis=1).astype(jnp.int32)
    source_pos = jnp.sum(jnp.where(matches, block_index[None, :], 0), axis=1) + blocks_total * (
        1 - filled
    )
    result_pad = jnp.concatenate([branch.reshape(blocks_total, LEAF, D), empty_block], axis=0)
    returning = lax.all_to_all(
        result_pad[source_pos], "pts", split_axis=0, concat_axis=0, tiled=True
    )
    homes = send_pick[0][None, :] == block_index[:, None]
    home_slot = jnp.sum(jnp.where(homes, slot_index[None, :], 0), axis=1)
    back = returning[home_slot].reshape(count, D)
    return (
        layer_one.astype(jnp.float32)
        + jnp.dot(back, attn_out_two, preferred_element_type=jnp.float32)
    ).astype(jnp.bfloat16)


def solution(mesh):
    placed = (
        P(("grp", "pts"), None),
        P(("grp", "pts"), None),
        P(("grp", "pts"), None),
        P(("grp", "pts"), None),
        P(),
        P(),
        P(),
        P(),
        P(),
        P(),
        P(),
        P(),
        P(),
        P(),
    )
    return jax.shard_map(
        shards, mesh=mesh, in_specs=placed, out_specs=P(("grp", "pts"), None), check_vma=False
    )
```

profile of v0, /device:TPU:0, one launch (start us, length us, event | category | flops | bytes accessed | tf_op | source)
XLA Modules:
  0.0 225.6 jit_solution(7809991669911405485)
XLA Ops:
  1.7 5.3 %convolution_convert_fusion.1 = bf16[1024,1536]{1,0:T(8,128)(2,1)} fusion(bf16[512,1536]{1,0:T(8,128)(2,1)} %param.23, bf16[1024,512]{1,0:T(8,128)(2,1)} %param.18, f32[512]{0:T(512)} %param.22, f32[1024]{0:T(1024)S(1)} %add_rsqrt_fusion.2), kind=kOutput, calls=%fused_computation.63 | convolution fusion | flops 1614282752 | bytes 5773312 | tf_op jit(solution)/shard_map/dot_general | solution.py:76
  7.0 8.9 %reshape.242 = bf16[2,512,3,8,64]{4,3,2,1,0:T(8,128)(2,1)} reshape(bf16[1024,1536]{1,0:T(8,128)(2,1)} %convolution_convert_fusion.1) | data formatting | bytes 6291456 | tf_op jit(solution)/shard_map/reshape | solution.py:77
  15.8 7.6 %copy.48 = bf16[2,512,3,8,64]{1,4,3,2,0:T(8,128)(2,1)} copy(bf16[2,512,3,8,64]{4,3,2,1,0:T(8,128)(2,1)} %reshape.242) | data formatting | bytes 6291456 | tf_op jit(solution)/shard_map/while | solution.py:78
  24.5 32.0 %while.20 = (s32[]{:T(128)}, bf16[2,512,512]{2,1,0:T(8,128)(2,1)}, bf16[2,512,3,8,64]{1,4,3,2,0:T(8,128)(2,1)}, s32[2,512]{1,0:T(2,128)S(1)}, s32[]{:T(128)}) while((s32[]{:T(128)}, bf16[2,512,512]{2,1,0:T(8,128)(2,1)}, bf16[2,512,3,8,64]{1,4,3,2,0:T(8,128)(2,1)}, s32[2,512]{1,0:T(2,128)S(1)}, s32[]{:T(128)}) %tuple.60), condition=%wide.region_4.5_spmd, body=%wide.region_1.4_spmd.sunk | while | flops 549978624 | bytes 24681028 | solution.py:78
  24.5 2.7 %dynamic-slice_bitcast_fusion.4 = bf16[512,3,8,64]{0,3,2,1:T(8,128)(2,1)} fusion(bf16[2,512,3,8,64]{1,4,3,2,0:T(8,128)(2,1)} %get-tuple-element.204, s32[]{:T(128)} %get-tuple-element.197), kind=kLoop, calls=%fused_computation.13.clone.1 | loop fusion | bytes 3145732 | tf_op jit(solution)/shard_map/while/body/jit(dynamic_index_in_dim)/squeeze | solution.py:78
  27.5 7.6 %fusion.104 = (f32[8,512]{1,0:T(8,128)S(1)}, f32[8,512,512]{1,2,0:T(8,128)}) fusion(pred[512,512]{0,1:T(8,128)(4,1)S(1)} %broadcast_compare_fusion.2, bf16[512,3,8,64]{0,3,2,1:T(8,128)(2,1)} %dynamic-slice_bitcast_fusion.4), kind=kOutput, calls=%fused_computation.120.clone.1 | convolution fusion | flops 276824576 | bytes 9715712 | tf_op jit(solution)/shard_map/while/body/eval_jaxpr/sub | solution.py:23
  35.0 4.4 %fusion.105 = bf16[8,64,512]{2,1,0:T(8,128)(2,1)S(1)} fusion(f32[8,512,512]{1,2,0:T(8,128)} %get-tuple-element.181, f32[8,512]{1,0:T(8,128)S(1)} %get-tuple-element.182, bf16[512,3,8,64]{0,3,2,1:T(8,128)(2,1)} %dynamic-slice_bitcast_fusion.4), kind=kOutput, calls=%fused_computation.14.clone.1 | convolution fusion | flops 272891904 | bytes 9453568 | tf_op jit(solution)/shard_map/while/body/eval_jaxpr/hqk,khd->qhd/dot_general | solution.py:35
  43.5 7.6 %fusion.104 = (f32[8,512]{1,0:T(8,128)S(1)}, f32[8,512,512]{1,2,0:T(8,128)}) fusion(pred[512,512]{0,1:T(8,128)(4,1)S(1)} %broadcast_compare_fusion.2, bf16[512,3,8,64]{0,3,2,1:T(8,128)(2,1)} %dynamic-slice_bitcast_fusion.4), kind=kOutput, calls=%fused_computation.120.clone.1 | convolution fusion | flops 276824576 | bytes 9715712 | tf_op jit(solution)/shard_map/while/body/eval_jaxpr/sub | solution.py:23
  51.1 4.4 %fusion.105 = bf16[8,64,512]{2,1,0:T(8,128)(2,1)S(1)} fusion(f32[8,512,512]{1,2,0:T(8,128)} %get-tuple-element.181, f32[8,512]{1,0:T(8,128)S(1)} %get-tuple-element.182, bf16[512,3,8,64]{0,3,2,1:T(8,128)(2,1)} %dynamic-slice_bitcast_fusion.4), kind=kOutput, calls=%fused_computation.14.clone.1 | convolution fusion | flops 272891904 | bytes 9453568 | tf_op jit(solution)/shard_map/while/body/eval_jaxpr/hqk,khd->qhd/dot_general | solution.py:35
  56.5 3.4 %fusion.44 = (f32[1024]{0:T(1024)S(1)}, bf16[1024,512]{1,0:T(8,128)(2,1)}) fusion(bf16[1024,512]{1,0:T(8,128)(2,1)} %bitcast.156, bf16[512,512]{1,0:T(8,128)(2,1)} %param.24, bf16[1024,512]{1,0:T(8,128)(2,1)} %param.18), kind=kOutput, calls=%fused_computation.77 | convolution fusion | flops 540015616 | bytes 3674112 | tf_op jit(solution)/shard_map/dot_general | solution.py:81
  60.0 7.1 %fusion.48 = (f32[1024]{0:T(1024)S(1)}, bf16[1024,512]{1,0:T(8,128)(2,1)S(1)}) fusion(bf16[2048,512]{1,0:T(8,128)(2,1)S(1)} %copy-done, bf16[512,2048]{1,0:T(8,128)(2,1)} %param.26, bf16[1024,512]{1,0:T(8,128)(2,1)} %get-tuple-element.121, f32[512]{0:T(512)S(1)} %copy-done.6, f32[1024]{0:T(1024)S(1)} %add_rsqrt_fusion.1), kind=kOutput, calls=%fused_computation.81 | convolution fusion | flops 4319083520 | bytes 6301696 | tf_op jit(solution)/shard_map/dot_general | solution.py:88
  69.7 6.5 %all-to-all-start = ((bf16[8,128,512]{2,1,0:T(8,128)(2,1)}), bf16[8,128,512]{2,1,0:T(8,128)(2,1)S(1)}, u32[]{:S(2)}, u32[]{:S(2)}) async-start(bf16[8,128,512]{2,1,0:T(8,128)(2,1)} %gather_fusion), calls=%async_computation | async-start | bytes 2097152 | tf_op jit(solution)/shard_map/all_to_all | solution.py:102
  76.4 56.8 %all-gather = bf16[32,4,1024]{2,1,0:T(4,128)(2,1)S(1)} all-gather(bf16[1,4,1024]{2,1,0:T(4,128)(2,1)S(1)} %fusion.56), channel_id=1, replica_groups=mesh['grp'=4,'pts'=8] {'grp','pts'}, dimensions={0}, use_global_device_ids=true | all-gather | bytes 270336 | tf_op jit(solution)/shard_map/all_gather | solution.py:97
  134.4 4.9 %convolution_convert_fusion = bf16[1024,1536]{1,0:T(8,128)(2,1)} fusion(bf16[1024,512]{1,0:T(8,128)(2,1)S(1)} %bitcast.155, bf16[512,1536]{1,0:T(8,128)(2,1)} %param.30), kind=kOutput, calls=%fused_computation.62 | convolution fusion | flops 1612185600 | bytes 5767168 | tf_op jit(solution)/shard_map/dot_general | solution.py:104
  139.3 8.9 %reshape.243 = bf16[2,512,3,8,64]{4,3,2,1,0:T(8,128)(2,1)} reshape(bf16[1024,1536]{1,0:T(8,128)(2,1)} %convolution_convert_fusion) | data formatting | bytes 6291456 | tf_op jit(solution)/shard_map/reshape | solution.py:107
  148.2 7.6 %copy.53 = bf16[2,512,3,8,64]{1,4,3,2,0:T(8,128)(2,1)} copy(bf16[2,512,3,8,64]{4,3,2,1,0:T(8,128)(2,1)} %reshape.243) | data formatting | bytes 6291456 | tf_op jit(solution)/shard_map/while | solution.py:108
  155.9 32.9 %while.21 = (s32[]{:T(128)}, bf16[2,512,512]{2,1,0:T(8,128)(2,1)S(1)}, bf16[2,512,3,8,64]{1,4,3,2,0:T(8,128)(2,1)}, bf16[128,8,64]{0,2,1:T(8,128)(2,1)S(1)}, bf16[128,8,64]{0,2,1:T(8,128)(2,1)S(1)}, /*index=5*/s32[]{:T(128)}) while((s32[]{:T(128)}, bf16[2,512,512]{2,1,0:T(8,128)(2,1)S(1)}, bf16[2,512,3,8,64]{1,4,3,2,0:T(8,128)(2,1)}, ...), condition=%wide.region_13.14_spmd, body=%wide.region_8.13_spmd.sunk | while | flops 684720768 | bytes 31260748 | solution.py:108
  157.5 5.1 %fusion.108 = (f32[8,512]{1,0:T(8,128)S(1)}, f32[8,512,512]{1,2,0:T(8,128)}) fusion(bf16[512,3,8,64]{0,3,2,1:T(8,128)(2,1)S(1)} %dynamic-slice_bitcast_fusion.5), kind=kOutput, calls=%fused_computation.121.clone.1 | convolution fusion | flops 274727424 | bytes 9453568 | tf_op jit(solution)/shard_map/while/body/eval_jaxpr/sub | solution.py:23
  162.5 5.2 %fusion.109 = f32[512,8,64]{0,2,1:T(8,128)} fusion(f32[8,512,512]{1,2,0:T(8,128)} %get-tuple-element.188, f32[8,512]{1,0:T(8,128)S(1)} %get-tuple-element.189, bf16[512,3,8,64]{0,3,2,1:T(8,128)(2,1)S(1)} %dynamic-slice_bitcast_fusion.5), kind=kOutput, calls=%fused_computation.38.clone.1 | convolution fusion | flops 272629760 | bytes 9977856 | tf_op jit(solution)/shard_map/while/body/eval_jaxpr/hqk,khd->qhd/dot_general | solution.py:45
  173.9 5.1 %fusion.108 = (f32[8,512]{1,0:T(8,128)S(1)}, f32[8,512,512]{1,2,0:T(8,128)}) fusion(bf16[512,3,8,64]{0,3,2,1:T(8,128)(2,1)S(1)} %dynamic-slice_bitcast_fusion.5), kind=kOutput, calls=%fused_computation.121.clone.1 | convolution fusion | flops 274727424 | bytes 9453568 | tf_op jit(solution)/shard_map/while/body/eval_jaxpr/sub | solution.py:23
  179.0 5.2 %fusion.109 = f32[512,8,64]{0,2,1:T(8,128)} fusion(f32[8,512,512]{1,2,0:T(8,128)} %get-tuple-element.188, f32[8,512]{1,0:T(8,128)S(1)} %get-tuple-element.189, bf16[512,3,8,64]{0,3,2,1:T(8,128)(2,1)S(1)} %dynamic-slice_bitcast_fusion.5), kind=kOutput, calls=%fused_computation.38.clone.1 | convolution fusion | flops 272629760 | bytes 9977856 | tf_op jit(solution)/shard_map/while/body/eval_jaxpr/hqk,khd->qhd/dot_general | solution.py:45
  190.5 3.6 %all-to-all-start.1 = ((bf16[8,128,512]{2,1,0:T(8,128)(2,1)}), bf16[8,128,512]{2,1,0:T(8,128)(2,1)S(1)}, u32[]{:S(2)}, u32[]{:S(2)}) async-start(bf16[8,128,512]{2,1,0:T(8,128)(2,1)} %gather_fusion.2), calls=%async_computation.1 | async-start | bytes 2097152 | tf_op jit(solution)/shard_map/all_to_all | solution.py:119
  194.2 26.4 %all-to-all-done.1 = bf16[8,128,512]{2,1,0:T(8,128)(2,1)S(1)} async-done(((bf16[8,128,512]{2,1,0:T(8,128)(2,1)}), bf16[8,128,512]{2,1,0:T(8,128)(2,1)S(1)}, u32[]{:S(2)}, u32[]{:S(2)}) %all-to-all-start.1) | async-done | bytes 1048608 | tf_op jit(solution)/shard_map/all_to_all | solution.py:119
  222.2 3.4 %fusion.51 = bf16[1024,512]{1,0:T(8,128)(2,1)} fusion(bf16[1024,512]{1,0:T(8,128)(2,1)} %copy-done.2, bf16[1024,512]{1,0:T(8,128)(2,1)} %bitcast.154, bf16[512,512]{1,0:T(8,128)(2,1)} %param.31), kind=kOutput, calls=%fused_computation.84 | convolution fusion | flops 538443776 | bytes 3670016 | tf_op jit(solution)/shard_map/dot_general | solution.py:127
  (67 shorter events, 27.8 us)
Async XLA Ops:
  0.0 60.0 %copy-start = (bf16[2048,512]{1,0:T(8,128)(2,1)S(1)}, bf16[2048,512]{1,0:T(8,128)(2,1)}, u32[]{:S(2)}) copy-start(bf16[2048,512]{1,0:T(8,128)(2,1)} %param.27) | copy-start | bytes 6291460
  15.8 8.7 %copy-start.4 = (s32[2,512]{1,0:T(2,128)S(1)}, s32[2,512]{1,0:T(2,128)}, u32[]{:S(2)}) copy-start(s32[2,512]{1,0:T(2,128)} %param.19) | copy-start | bytes 12292
  56.5 3.5 %copy-start.6 = (f32[512]{0:T(512)S(1)}, f32[512]{0:T(512)}, u32[]{:S(2)}) copy-start(f32[512]{0:T(512)} %param.25) | copy-start | bytes 6148
  60.0 7.2 %copy-start.8 = (s32[1,8]{1,0:T(1,128)S(1)}, s32[1,8]{1,0:T(1,128)}, u32[]{:S(2)}) copy-start(s32[1,8]{1,0:T(1,128)} %param.20) | copy-start | bytes 100
  60.0 7.2 %copy-start.5 = (f32[512]{0:T(512)S(1)}, f32[512]{0:T(512)}, u32[]{:S(2)}) copy-start(f32[512]{0:T(512)} %param.28) | copy-start | bytes 6148
  67.1 1.0 copy-start.2
  69.7 6.5 %copy-start.3 = (bf16[512,1024]{1,0:T(8,128)(2,1)S(1)}, bf16[512,1024]{1,0:T(8,128)(2,1)}, u32[]{:S(2)}) copy-start(bf16[512,1024]{1,0:T(8,128)(2,1)} %param.29) | copy-start | bytes 3145732
  69.7 63.8 %copy-start.7 = (s32[1,8]{1,0:T(1,128)S(1)}, s32[1,8]{1,0:T(1,128)}, u32[]{:S(2)}) copy-start(s32[1,8]{1,0:T(1,128)} %param.21) | copy-start | bytes 100
  69.7 64.1 %all-to-all-start = ((bf16[8,128,512]{2,1,0:T(8,128)(2,1)}), bf16[8,128,512]{2,1,0:T(8,128)(2,1)S(1)}, u32[]{:S(2)}, u32[]{:S(2)}) async-start(bf16[8,128,512]{2,1,0:T(8,128)(2,1)} %gather_fusion), calls=%async_computation | async-start | bytes 2097152 | tf_op jit(solution)/shard_map/all_to_all | solution.py:102
  190.5 30.1 %all-to-all-start.1 = ((bf16[8,128,512]{2,1,0:T(8,128)(2,1)}), bf16[8,128,512]{2,1,0:T(8,128)(2,1)S(1)}, u32[]{:S(2)}, u32[]{:S(2)}) async-start(bf16[8,128,512]{2,1,0:T(8,128)(2,1)} %gather_fusion.2), calls=%async_computation.1 | async-start | bytes 2097152 | tf_op jit(solution)/shard_map/all_to_all | solution.py:119
  220.6 5.0 %copy-start.1 = (bf16[2048,512]{1,0:T(8,128)(2,1)S(1)}, bf16[2048,512]{1,0:T(8,128)(2,1)}, u32[]{:S(2)}) copy-start(bf16[2048,512]{1,0:T(8,128)(2,1)} %param.27) | copy-start | bytes 6291460
where the time goes:
time: 227 us; the launch traced here: 226 us
  matrix products  77.5 us (34%)
  blocking collectives  56.8 us (25%)
  local copies, waits for them, and re-layouts  51.7 us (23%)
  waiting for transfers between devices  26.4 us (12%)
  starting transfers between devices  10 us (4%)
  other arithmetic  2.89 us (1%)
    all_gather x1, blocking collectives, shards(): comp = lax.all_gather(local_comp, ('grp', 'pts'), axis=0, tiled=True)  56.8 us
    sub x6, matrix products, softmax_rows(): expo = jnp.exp(scores - top)  29.6 us
    all_to_all x1, waiting for transfers between devices, shards(): lax.all_to_all(result_pad[source_pos], 'pts', split_axis=0, concat_axis=0...  26.4 us
    dot_general x2, matrix products, second_ball(): jnp.einsum('hqk,khd->qhd', weights, rows[:, 2], preferred_element_type=jn...  10.4 us
    reshape x1, local copies, waits for them, and re-layouts, shards(): proj = proj.reshape(count // BALL, BALL, 3, HEADS, HEAD)  8.86 us
    reshape x1, local copies, waits for them, and re-layouts, shards(): proj_two = proj_two.reshape(count // BALL, BALL, 3, HEADS, HEAD)  8.86 us
    dot_general x2, matrix products, first_ball(): jnp.einsum('hqk,khd->qhd', weights, rows[:, 2], preferred_element_type=jn...  8.83 us
    squeeze x4, local copies, waits for them, and re-layouts, shards(): mixed = lax.map(first_ball, (proj, ball_ids)).reshape(count, D)  8.59 us
  transfers between devices with their start and end apart: 2, of which 1 were waited for; matrix products, arithmetic and copies ran while one was open for 0% of the time, Pallas kernels for 0%

commit v1 on v0

v1 whole, which is shorter than its diff:
```python
from functools import partial
import math

import jax
import jax.numpy as jnp
from jax import lax
from jax.experimental import pallas as pl
from jax.experimental.pallas import tpu as pltpu
from jax.sharding import PartitionSpec as P

HEAD = 64
LEAF = 128
BALL = 512
CMP = 256
PAIR = 2 * HEAD
AUG = HEAD + 16
HIDE = 512
MIB = 1 << 20
F32 = jnp.float32
BF16 = jnp.bfloat16
SCALE = HEAD ** (-0.5) * math.log2(math.e)

ANY = pl.BlockSpec(memory_space=pl.ANY)
VMEM = pl.BlockSpec(memory_space=pltpu.VMEM)
SMEM = pl.BlockSpec(memory_space=pltpu.SMEM)


def norm(values, gain):
    wide = values.astype(F32)
    return wide * lax.rsqrt(jnp.mean(wide * wide, axis=-1, keepdims=True) + 1e-06) * gain


def gelu(x):
    c = math.sqrt(2.0 / math.pi)
    t = jnp.tanh(x * (c + (c * 0.044715) * (x * x)))
    return x * (0.5 + 0.5 * t)


def dot(a, b):
    return jnp.dot(a, b, preferred_element_type=F32)


def dot_t(a, b):
    return lax.dot_general(a, b, (((1,), (1,)), ((), ())), preferred_element_type=F32)


def aligned(index, size):
    return pl.ds(pl.multiple_of(index * size, size), size)


def head_keys(keys, half):
    lane = lax.broadcasted_iota(jnp.int32, keys.shape, 1)
    return jnp.where((lane >= HEAD) == bool(half), keys, jnp.zeros_like(keys))


def softmax_mix(scores, values_aug):
    top = jnp.max(scores, axis=0, keepdims=True)
    expo = jnp.exp2(scores - top).astype(BF16)
    mixed = dot(values_aug, expo)
    return mixed[:HEAD] * (1.0 / mixed[HEAD : HEAD + 1])


def send_to(me, s, peers):
    return me ^ s if peers & (peers - 1) == 0 else (me + s) % peers


def got_from(me, s, peers):
    return me ^ s if peers & (peers - 1) == 0 else (me + peers - s) % peers


def layer_one_kernel(peers, cap, slots, late, *refs):
    n_in = 13 if late else 12
    ins, rest = refs[:n_in], refs[n_in:]
    me_ref, pick_ref, points, ids, gain1, w_in, w_out, gain2, w_up, w_down, gain3 = ins[:11]
    lead = ins[11]
    h_first = ins[12] if late else None
    z_out, pool_out = rest[:2]
    n_send = len(slots)
    sends = rest[2 : 2 + n_send]
    rest = rest[2 + n_send :]
    if not late:
        h_out = rest[0]
        rest = rest[1:]
    (x_s, win_s, wout_s, wup_s, wdown_s, q_s, k_s, va_s, bias_s, mix_s, y_s, h_s, sem) = rest
    per = BALL // LEAF
    first = lead[0]
    ball = (1 - first) if late else first
    rows = aligned(ball, BALL)
    copies = [
        pltpu.make_async_copy(points.at[rows, :], x_s, sem.at[0]),
        pltpu.make_async_copy(w_in, win_s, sem.at[1]),
        pltpu.make_async_copy(w_out, wout_s, sem.at[2]),
        pltpu.make_async_copy(w_up, wup_s, sem.at[3]),
        pltpu.make_async_copy(w_down, wdown_s, sem.at[4]),
    ]
    for copy in copies:
        copy.start()
    width = x_s.shape[1]
    heads = width // HEAD

    own = ids[pl.ds(ball, 1), :]
    across = jnp.broadcast_to(own, (LEAF, BALL)).astype(F32)
    down = across.T
    for c in range(BALL // LEAF):
        cols = slice(c * LEAF, (c + 1) * LEAF)
        bias_s[:, cols] = jnp.where(down == across[:1, cols], 0.0, -1e30)
    for h in range(heads):
        va_s[h, HEAD:, :] = jnp.ones((AUG - HEAD, BALL), BF16)

    copies[0].wait()
    h1 = norm(x_s[...], gain1[...]).astype(BF16)
    copies[1].wait()
    q_s[...] = (dot(h1, win_s[:, :width]) * SCALE).astype(BF16)
    k_s[...] = dot(h1, win_s[:, width : 2 * width]).astype(BF16)
    values = dot(h1, win_s[:, 2 * width :]).astype(BF16).T
    for h in range(heads):
        va_s[h, :HEAD, :] = values[h * HEAD : (h + 1) * HEAD]

    @pl.loop(0, heads // 2)
    def _(pair):
        cols = aligned(pair, PAIR)
        q, k = q_s[:, cols], k_s[:, cols]
        for half in range(2):
            scores = dot_t(head_keys(k, half), q) + bias_s[...]
            out = softmax_mix(scores, va_s[2 * pair + half])
            mix_s[aligned(2 * pair + half, HEAD), :] = out.astype(BF16)

    copies[2].wait()
    y = (x_s[...].astype(F32) + dot(mix_s[...].T, wout_s[...])).astype(BF16)
    y_s[...] = y
    inner = norm(y, gain2[...]).astype(BF16)
    copies[3].wait()
    copies[4].wait()
    total = jnp.zeros((BALL, width), F32)
    for c in range(wup_s.shape[1] // HIDE):
        cols = slice(c * HIDE, (c + 1) * HIDE)
        hidden = gelu(dot(inner, wup_s[:, cols])).astype(BF16)
        total = total + dot(hidden, wdown_s[cols, :])
    z = (y_s[...].astype(F32) + total).astype(BF16)
    z_out[...] = z
    h3 = norm(z, gain3[...]).astype(BF16)
    h_s[...] = h3
    wide = h3.astype(F32)
    for c in range(BALL // CMP):
        part = jnp.sum(wide[c * CMP : (c + 1) * CMP], axis=0, keepdims=True) * CMP ** (-0.5)
        pool_out[c : c + 1, :] = part.astype(BF16)
    if not late:
        h_out[...] = h3
    me = me_ref[0]
    for s, send in zip(slots, sends):
        for c in range(cap):
            block = jnp.minimum(pick_ref[0, send_to(me, s, peers) * cap + c], 2 * per - 1)
            place = aligned(lax.rem(block, per), LEAF)
            at = slice(c * LEAF, (c + 1) * LEAF)
            if late:
                here = block // per == ball

                @pl.when(here)
                def _():
                    send[at, :] = h_s[place, :]

                @pl.when(jnp.logical_not(here))
                def _():
                    send[at, :] = h_first[place, :]

            else:
                send[at, :] = h_s[place, :]


def layer_one(peers, cap, slots, late, me, pick, points, ids, weights, lead, h_first=None):
    width = points.shape[1]
    hidden = weights[4].shape[1]
    half = jax.ShapeDtypeStruct((BALL, width), BF16)
    block = jax.ShapeDtypeStruct((cap * LEAF, width), BF16)
    outs = [half, jax.ShapeDtypeStruct((BALL // CMP, width), BF16)] + [block] * len(slots)
    specs = [SMEM, SMEM, ANY, VMEM, VMEM, ANY, ANY, VMEM, ANY, ANY, VMEM, SMEM]
    args = [me, pick, points, ids, *weights, lead]
    if late:
        specs.append(VMEM)
        args.append(h_first)
    else:
        outs.append(half)
    heads = width // HEAD
    return pl.pallas_call(
        partial(layer_one_kernel, peers, cap, slots, late),
        out_shape=outs,
        in_specs=specs,
        out_specs=[VMEM] * len(outs),
        scratch_shapes=[
            pltpu.VMEM((BALL, width), BF16),
            pltpu.VMEM((width, 3 * width), BF16),
            pltpu.VMEM((width, width), BF16),
            pltpu.VMEM((width, hidden), BF16),
            pltpu.VMEM((hidden, width), BF16),
            pltpu.VMEM((BALL, width), BF16),
            pltpu.VMEM((BALL, width), BF16),
            pltpu.VMEM((heads, AUG, BALL), BF16),
            pltpu.VMEM((BALL, BALL), F32),
            pltpu.VMEM((width, BALL), BF16),
            pltpu.VMEM((BALL, width), BF16),
            pltpu.VMEM((BALL, width), BF16),
            pltpu.SemaphoreType.DMA((5,)),
        ],
        compiler_params=pltpu.CompilerParams(vmem_limit_bytes=32 * MIB),
        cost_estimate=pl.CostEstimate(
            flops=2 * BALL * width * (4 * width + 2 * hidden) + 16 * BALL * BALL * width,
            bytes_accessed=8 * MIB,
            transcendentals=heads * BALL * BALL,
        ),
        name="layer_one_late" if late else "layer_one_lead",
    )(*args)


def place_of(recv_ref, slot, blocks):
    place, found = jnp.int32(0), jnp.int32(0)
    for j in range(blocks):
        hit = (recv_ref[0, j] == slot).astype(jnp.int32)
        place = place + j * hit
        found = found + hit
    return place, found > 0


def layer_two_kernel(peers, cap, blocks, *refs):
    me_ref, recv_ref = refs[:2]
    arrived = refs[2 : 2 + peers]
    pooled, w_comp, w_in = refs[2 + peers : 5 + peers]
    outs = refs[5 + peers : 5 + 2 * peers]
    q_s, k_s, va_s, ck_s, cv_s, mix_s, a_s = refs[5 + 2 * peers :]
    width = q_s.shape[1]
    heads = width // HEAD
    me = me_ref[0]
    comp = pooled.shape[0]
    for h in range(heads):
        va_s[h, HEAD:, :] = jnp.ones((AUG - HEAD, va_s.shape[2]), BF16)
        cv_s[h, HEAD:, :] = jnp.ones((AUG - HEAD, comp), BF16)
    ck_s[...] = dot(pooled[...], w_comp[:, :width]).astype(BF16)
    values = dot(pooled[...], w_comp[:, width:]).astype(BF16).T
    for h in range(heads):
        cv_s[h, :HEAD, :] = values[h * HEAD : (h + 1) * HEAD]
    for s in range(peers):
        for c in range(cap):
            place, found = place_of(recv_ref, got_from(me, s, peers) * cap + c, blocks)

            @pl.when(found)
            def _():
                block = arrived[s][c * LEAF : (c + 1) * LEAF, :]
                rows = aligned(place, LEAF)
                q_s[rows, :] = (dot(block, w_in[:, :width]) * SCALE).astype(BF16)
                k_s[rows, :] = dot(block, w_in[:, width : 2 * width]).astype(BF16)
                values = dot(block, w_in[:, 2 * width :]).astype(BF16).T
                for h in range(heads):
                    va_s[h, :HEAD, rows] = values[h * HEAD : (h + 1) * HEAD]

    for ball in range(blocks * LEAF // BALL):
        rows = slice(ball * BALL, (ball + 1) * BALL)

        @pl.loop(0, heads // 2)
        def _(pair):
            cols = aligned(pair, PAIR)
            q, k, ck = q_s[rows, cols], k_s[rows, cols], ck_s[:, cols]
            for half in range(2):
                h = 2 * pair + half
                out = softmax_mix(dot_t(head_keys(k, half), q), va_s[h, :, rows])
                far = softmax_mix(dot_t(head_keys(ck, half), q), cv_s[h])
                mix_s[aligned(h, HEAD), :] = (out + far).astype(BF16)

        a_s[rows, :] = mix_s[...].T
    for s in range(peers):
        for c in range(cap):
            place, _ = place_of(recv_ref, got_from(me, s, peers) * cap + c, blocks)
            outs[s][c * LEAF : (c + 1) * LEAF, :] = a_s[aligned(place, LEAF), :]


def layer_two(peers, cap, me, recv, arrived, pooled, w_comp, w_in):
    blocks = recv.shape[1]
    width = w_in.shape[0]
    heads = width // HEAD
    rows = blocks * LEAF
    comp = pooled.shape[0]
    block = jax.ShapeDtypeStruct((cap * LEAF, width), BF16)
    return pl.pallas_call(
        partial(layer_two_kernel, peers, cap, blocks),
        out_shape=[block] * peers,
        in_specs=[SMEM, SMEM] + [VMEM] * (peers + 3),
        out_specs=[VMEM] * peers,
        scratch_shapes=[
            pltpu.VMEM((rows, width), BF16),
            pltpu.VMEM((rows, width), BF16),
            pltpu.VMEM((heads, AUG, rows), BF16),
            pltpu.VMEM((comp, width), BF16),
            pltpu.VMEM((heads, AUG, comp), BF16),
            pltpu.VMEM((width, BALL), BF16),
            pltpu.VMEM((rows, width), BF16),
        ],
        compiler_params=pltpu.CompilerParams(vmem_limit_bytes=32 * MIB),
        name="layer_two",
    )(me, recv, *arrived, pooled, w_comp, w_in)


def final_kernel(peers, cap, me_ref, pick_ref, lead, *refs):
    back = refs[:peers]
    w_out, z_first, z_late, out = refs[peers:]
    per = BALL // LEAF
    me = me_ref[0]
    for s in range(peers):
        for c in range(cap):
            block = pick_ref[0, send_to(me, s, peers) * cap + c]

            @pl.when(block < 2 * per)
            def _():
                place = aligned(lax.rem(block, per), LEAF)
                early = block // per == lead[0]
                z = jnp.where(early, z_first[place, :], z_late[place, :]).astype(F32)
                gain = dot(back[s][c * LEAF : (c + 1) * LEAF, :], w_out[...])
                out[aligned(block, LEAF), :] = (z + gain).astype(BF16)


def final(peers, cap, me, pick, lead, back, w_out, z_first, z_late):
    rows = 2 * z_first.shape[0]
    return pl.pallas_call(
        partial(final_kernel, peers, cap),
        out_shape=jax.ShapeDtypeStruct((rows, z_first.shape[1]), BF16),
        in_specs=[SMEM] * 3 + [VMEM] * (peers + 3),
        out_specs=VMEM,
        compiler_params=pltpu.CompilerParams(vmem_limit_bytes=24 * MIB),
        name="last_product",
    )(me, pick, lead, *back, w_out, z_first, z_late)


def gather_all(rows, axes):
    for axis, size in axes:
        if size & (size - 1):
            rows = lax.all_gather(rows, axis, axis=0, tiled=True)
            continue
        bit = 1
        while bit < size:
            pattern = [(i, i ^ bit) for i in range(size)]
            rows = jnp.concatenate([rows, lax.ppermute(rows, axis, pattern)])
            bit *= 2
    return rows


def shards(
    axes,
    points,
    ball_ids,
    send_pick,
    recv_from,
    gain_one,
    attn_in_one,
    attn_out_one,
    gain_two,
    mlp_up,
    mlp_down,
    gain_three,
    compress_proj,
    attn_in_two,
    attn_out_two,
):
    peers = axes[1][1]
    cap = send_pick.shape[1] // peers
    per = BALL // LEAF
    me = lax.axis_index("pts").astype(jnp.int32)
    far = peers - 1
    target = send_to(me, far, peers)
    lead_slot = lax.dynamic_slice(send_pick[0], (target * cap,), (1,))
    lead = jnp.minimum(lead_slot // per, ball_ids.shape[0] - 1).astype(jnp.int32)
    me1 = me.reshape(1)
    weights = (
        gain_one.reshape(1, -1),
        attn_in_one,
        attn_out_one,
        gain_two.reshape(1, -1),
        mlp_up,
        mlp_down,
        gain_three.reshape(1, -1),
    )
    one = partial(layer_one, peers, cap)
    early = [far] if cap == 1 else []
    z_first, pool_first, *lead_sends, h_first = one(
        early, False, me1, send_pick, points, ball_ids, weights, lead
    )
    order = [s for s in range(peers - 1, -1, -1) if s not in early]
    z_late, pool_late, *late_sends = one(
        order, True, me1, send_pick, points, ball_ids, weights, lead, h_first
    )
    sends = dict(zip(early + order, lead_sends + late_sends))

    def travel(blocks, s, home):
        if s == 0:
            return blocks
        pattern = [(i, send_to(i, s, peers)) for i in range(peers)]
        if home:
            pattern = [(b, a) for a, b in pattern]
        return lax.ppermute(blocks, "pts", pattern)

    arrived = {s: travel(sends[s], s, False) for s in early + order}
    pooled = gather_all(jnp.concatenate([pool_first, pool_late]), axes)
    mixed = layer_two(
        peers, cap, me1, recv_from, [arrived[s] for s in range(peers)], pooled, compress_proj, attn_in_two
    )
    back = {s: travel(mixed[s], s, True) for s in range(peers - 1, -1, -1)}
    return final(
        peers,
        cap,
        me1,
        send_pick,
        lead,
        [back[s] for s in range(peers)],
        attn_out_two,
        z_first,
        z_late,
    )


def solution(mesh):
    rows = P(("grp", "pts"), None)
    axes = (("grp", mesh.shape["grp"]), ("pts", mesh.shape["pts"]))
    return jax.shard_map(
        partial(shards, axes),
        mesh=mesh,
        in_specs=(rows,) * 4 + (P(),) * 10,
        out_specs=rows,
        check_vma=False,
    )
```

time: 227 us -> 139 us (0.61)
  the two profiles are of different devices: /device:TPU:0 before, /device:TPU:11 now
where the time goes in v1:
time: 139 us; the launch traced here: 138 us
  Pallas kernels  44.9 us (32%)
  waiting for transfers between devices  31.8 us (23%)
  local copies, waits for them, and re-layouts  29.3 us (21%)
  starting transfers between devices  29.3 us (21%)
  between operations  2.8 us (2%)
    ppermute x14, waiting for transfers between devices, travel(): return lax.ppermute(blocks, 'pts', pattern)  27.1 us
    pallas_call x2, Pallas kernels, layer_one(): pl.pallas_call(partial(layer_one_kernel, peers, cap, slots, late), out_sh...  23 us
    ppermute x14, starting transfers between devices, travel(): return lax.ppermute(blocks, 'pts', pattern)  22.9 us
    pallas_call x1, Pallas kernels, layer_two(): pl.pallas_call(partial(layer_two_kernel, peers, cap, blocks), out_shape=[...  18.5 us
    unnamed x68, local copies, waits for them, and re-layouts  17.3 us
    concatenate x3, local copies, waits for them, and re-layouts, gather_all(): rows = jnp.concatenate([rows, lax.ppermute(rows, axis, pattern)])  10.8 us
    ppermute x5, starting transfers between devices, gather_all(): rows = jnp.concatenate([rows, lax.ppermute(rows, axis, pattern)])  6.4 us
    ppermute x5, waiting for transfers between devices, gather_all(): rows = jnp.concatenate([rows, lax.ppermute(rows, axis, pattern)])  4.66 us
  transfers between devices with their start and end apart: 19, of which 10 were waited for; matrix products, arithmetic and copies ran while one was open for 8% of the time, Pallas kernels for 0%

profile of v1, /device:TPU:11, one launch (start us, length us, event | category | flops | bytes accessed | tf_op | source)
XLA Modules:
  0.0 138.1 jit_solution(7984136366722118605)
XLA Ops:
  4.5 1.6 %copy-done.12 = bf16[512,2048]{1,0:T(8,128)(2,1)S(1)} copy-done((bf16[512,2048]{1,0:T(8,128)(2,1)S(1)}, bf16[512,2048]{1,0:T(8,128)(2,1)}, u32[]{:S(2)}) %copy-start.12) | copy-done | bytes 2097176
  14.1 11.3 %layer_one_lead.1 = (bf16[512,512]{1,0:T(8,128)(2,1)S(1)}, bf16[2,512]{1,0:T(2,128)(2,1)S(1)}, bf16[128,512]{1,0:T(8,128)(2,1)}, bf16[512,512]{1,0:T(8,128)(2,1)S(1)}) custom-call(s32[1]{0:T(128)} %bitcast.refs_0_.me_ref, s32[1,8]{1,0:T(1,128)S(1)} %copy-done.10, bf16[1024,512]{1,0:T(8,128)(2,1)S(1)} %copy-done.15, s32[2,512]{1,0:T(2,128)S(1)} %copy-done.22, ...), custom_call_target="tpu_custom_call" | custom-call | flops 5368709120 | bytes 8388608 | tf_op jit(solution)/shard_map/layer_one_lead/pallas_call | solution.py:184
  26.3 11.7 %layer_one_late.1 = (bf16[512,512]{1,0:T(8,128)(2,1)S(1)}, bf16[2,512]{1,0:T(2,128)(2,1)S(1)}, bf16[128,512]{1,0:T(8,128)(2,1)S(1)}, bf16[128,512]{1,0:T(8,128)(...) custom-call(s32[1]{0:T(128)} %bitcast.refs_0_.me_ref, ...), custom_call_target="tpu_custom_call" | custom-call | flops 5368709120 | bytes 8388608 | tf_op jit(solution)/shard_map/layer_one_late/pallas_call | solution.py:184
  42.3 2.2 %collective-permute-done.7 = bf16[4,512]{1,0:T(4,128)(2,1)S(1)} collective-permute-done((bf16[4,512]{1,0:T(4,128)(2,1)S(1)}, bf16[4,512]{1,0:T(4,128)(2,1)S(1)}, u32[]{:S(2)}, u32[]{:S(2)}) %collective-permute-start.7) | collective-permute-done | bytes 4128 | tf_op jit(solution)/shard_map/ppermute | solution.py:338
  45.8 3.3 %collective-permute-start.6 = (bf16[128,512]{1,0:T(8,128)(2,1)}, bf16[128,512]{1,0:T(8,128)(2,1)S(1)}, u32[]{:S(2)}, u32[]{:S(2)}) collective-permute-start(bf16[128,512]{1,0:T(8,128)(2,1)} %get-tuple-element.34), channel_id=1, source_target_pairs={{0,7},{1,6},{2,5},{3,4},{4,3},{5,2},{6,1},{7,0},{8,15},{9,14},{10,... | collective-permute-start | bytes 393224 | tf_op jit(solution)/shard_map/ppermute | solution.py:395
  51.6 1.8 %concatenate.26 = bf16[32,512]{1,0:T(8,128)(2,1)} concatenate(bf16[2,512]{1,0:T(2,128)(2,1)S(1)} %get-tuple-element.35, bf16[2,512]{1,0:T(2,128)(2,1)S(1)} %get-tuple-element.36, bf16[4,512]{1,0:T(4,128)(2,1)S(1)} %collective-permute-done.7, bf16[8,512]{1,0:T(8,128)(2,1)S(1)} %collective-permute-done.8, bf16[16,512]{1,0:T(8,128)(2,1)S(1)} %collective-permute-done.9), dimensions={0} | concatenate | bytes 65536 | tf_op jit(solution)/shard_map/concatenate | solution.py:338
  53.4 1.8 %collective-permute-start.10 = (bf16[32,512]{1,0:T(8,128)(2,1)}, bf16[32,512]{1,0:T(8,128)(2,1)}, u32[]{:S(2)}, u32[]{:S(2)}) collective-permute-start(bf16[32,512]{1,0:T(8,128)(2,1)} %concatenate.26), channel_id=1, source_target_pairs={{0,2},{1,3},{2,0},{3,1},{4,6},{5,7},{6,4},{7,5},{8,10},{9,11},{10,... | collective-permute-start | bytes 98312 | tf_op jit(solution)/shard_map/ppermute | solution.py:338
  55.2 1.6 %collective-permute-done.10 = bf16[32,512]{1,0:T(8,128)(2,1)} collective-permute-done((bf16[32,512]{1,0:T(8,128)(2,1)}, bf16[32,512]{1,0:T(8,128)(2,1)}, u32[]{:S(2)}, u32[]{:S(2)}) %collective-permute-start.10) | collective-permute-done | bytes 32800 | tf_op jit(solution)/shard_map/ppermute | solution.py:338
  56.8 5.2 %concatenate.27 = bf16[64,512]{1,0:T(8,128)(2,1)} concatenate(bf16[2,512]{1,0:T(2,128)(2,1)S(1)} %get-tuple-element.35, bf16[2,512]{1,0:T(2,128)(2,1)S(1)} %get-tuple-element.36, bf16[4,512]{1,0:T(4,128)(2,1)} %copy-done.32, bf16[8,512]{1,0:T(8,128)(2,1)} %copy-done.31, bf16[16,512]{1,0:T(8,128)(2,1)} %copy-done.30, bf16[32,512]{1,0:T(8,128)(2,1)} %collective-permute-done.10), dimensions={0} | concatenate | bytes 131072 | tf_op jit(solution)/shard_map/concatenate | solution.py:338
  62.1 2.0 %collective-permute-start.11 = (bf16[64,512]{1,0:T(8,128)(2,1)}, bf16[64,512]{1,0:T(8,128)(2,1)S(1)}, u32[]{:S(2)}, u32[]{:S(2)}) collective-permute-start(bf16[64,512]{1,0:T(8,128)(2,1)} %concatenate.27), channel_id=1, source_target_pairs={{0,4},{1,5},{2,6},{3,7},{4,0},{5,1},{6,2},{7,3},{8,12},{9,13},{10,... | collective-permute-start | bytes 196616 | tf_op jit(solution)/shard_map/ppermute | solution.py:338
  64.2 3.2 %collective-permute-start.2 = (bf16[128,512]{1,0:T(8,128)(2,1)}, bf16[128,512]{1,0:T(8,128)(2,1)}, u32[]{:S(2)}, u32[]{:S(2)}) collective-permute-start(bf16[128,512]{1,0:T(8,128)(2,1)} %copy-done.20), channel_id=1, source_target_pairs={{0,3},{1,2},{2,1},{3,0},{4,7},{5,6},{6,5},{7,4},{8,11},{9,10},{10,... | collective-permute-start | bytes 393224 | tf_op jit(solution)/shard_map/ppermute | solution.py:395
  69.0 2.9 %collective-permute-start.4 = (bf16[128,512]{1,0:T(8,128)(2,1)}, bf16[128,512]{1,0:T(8,128)(2,1)}, u32[]{:S(2)}, u32[]{:S(2)}) collective-permute-start(bf16[128,512]{1,0:T(8,128)(2,1)} %copy-done.18), channel_id=1, source_target_pairs={{0,5},{1,4},{2,7},{3,6},{4,1},{5,0},{6,3},{7,2},{8,13},{9,12},{10,... | collective-permute-start | bytes 393224 | tf_op jit(solution)/shard_map/ppermute | solution.py:395
  73.8 3.7 %concatenate.28.refs_10_ = bf16[128,512]{1,0:T(8,128)(2,1)S(1)} concatenate(bf16[2,512]{1,0:T(2,128)(2,1)S(1)} %get-tuple-element.35, bf16[2,512]{1,0:T(2,128)(2,1)S(1)} %get-tuple-element.36, bf16[4,512]{1,0:T(4,128)(2,1)} %copy-done.32, bf16[8,512]{1,0:T(8,128)(2,1)} %copy-done.31, bf16[16,512]{1,0:T(8,128)(2,1)} %copy-done.30, bf16[32,512]{1,0:T(8,128)(2,1)} %collective-permute-done.10, ...), dimensions={0} | concatenate | bytes 262144 | tf_op jit(solution)/shard_map/concatenate | solution.py:338
  77.5 5.4 %collective-permute-done.4.refs_7_ = bf16[128,512]{1,0:T(8,128)(2,1)} collective-permute-done((bf16[128,512]{1,0:T(8,128)(2,1)}, bf16[128,512]{1,0:T(8,128)(2,1)}, u32[]{:S(2)}, u32[]{:S(2)}) %collective-permute-start.4) | collective-permute-done | bytes 131104 | tf_op jit(solution)/shard_map/ppermute | solution.py:395
  82.9 4.6 %collective-permute-done.5.refs_8_ = bf16[128,512]{1,0:T(8,128)(2,1)} collective-permute-done((bf16[128,512]{1,0:T(8,128)(2,1)}, bf16[128,512]{1,0:T(8,128)(2,1)}, u32[]{:S(2)}, u32[]{:S(2)}) %collective-permute-start.5) | collective-permute-done | bytes 131104 | tf_op jit(solution)/shard_map/ppermute | solution.py:395
  88.4 18.5 %layer_two.1 = (bf16[128,512]{1,0:T(8,128)(2,1)S(1)}, bf16[128,512]{1,0:T(8,128)(2,1)S(1)}, bf16[128,512]{1,0:T(8,128)(2,1)S(1)}, bf16[128,512]{1,0:T(8,128)(2,1...) custom-call(s32[1]{0:T(128)} %bitcast.refs_0_.me_ref, ...), custom_call_target="tpu_custom_call" | custom-call | tf_op jit(solution)/shard_map/layer_two/pallas_call | solution.py:281
  108.5 1.7 %collective-permute-start.14 = (bf16[128,512]{1,0:T(8,128)(2,1)S(1)}, bf16[128,512]{1,0:T(8,128)(2,1)S(1)}, u32[]{:S(2)}, u32[]{:S(2)}) collective-permute-start(bf16[128,512]{1,0:T(8,128)(2,1)S(1)} %get-tuple-element.40), channel_id=1, source_target_pairs={{3,0},{2,1},{1,2},{0,3},{7,4},{6,5},{5,6},{4,7},{11,8},{10,9},{9,1... | collective-permute-start | bytes 393224 | tf_op jit(solution)/shard_map/ppermute | solution.py:395
  110.5 2.3 %collective-permute-start.16 = (bf16[128,512]{1,0:T(8,128)(2,1)S(1)}, bf16[128,512]{1,0:T(8,128)(2,1)S(1)}, u32[]{:S(2)}, u32[]{:S(2)}) collective-permute-start(bf16[128,512]{1,0:T(8,128)(2,1)S(1)} %get-tuple-element.42), channel_id=1, source_target_pairs={{5,0},{4,1},{7,2},{6,3},{1,4},{0,5},{3,6},{2,7},{13,8},{12,9},{15,... | collective-permute-start | bytes 393224 | tf_op jit(solution)/shard_map/ppermute | solution.py:395
  113.7 3.8 %collective-permute-start.18 = (bf16[128,512]{1,0:T(8,128)(2,1)S(1)}, bf16[128,512]{1,0:T(8,128)(2,1)S(1)}, u32[]{:S(2)}, u32[]{:S(2)}) collective-permute-start(bf16[128,512]{1,0:T(8,128)(2,1)S(1)} %get-tuple-element.44), channel_id=1, source_target_pairs={{7,0},{6,1},{5,2},{4,3},{3,4},{2,5},{1,6},{0,7},{15,8},{14,9},{13,... | collective-permute-start | bytes 393224 | tf_op jit(solution)/shard_map/ppermute | solution.py:395
  117.5 1.8 %collective-permute-done.14.refs_3_ = bf16[128,512]{1,0:T(8,128)(2,1)S(1)} collective-permute-done((bf16[128,512]{1,0:T(8,128)(2,1)S(1)}, bf16[128,512]{1,0:T(8,128)(2,1)S(1)}, u32[]{:S(2)}, u32[]{:S(2)}) %collective-permute-start.14) | collective-permute-done | bytes 131104 | tf_op jit(solution)/shard_map/ppermute | solution.py:395
  119.8 7.6 %collective-permute-done.16.refs_5_ = bf16[128,512]{1,0:T(8,128)(2,1)S(1)} collective-permute-done((bf16[128,512]{1,0:T(8,128)(2,1)S(1)}, bf16[128,512]{1,0:T(8,128)(2,1)S(1)}, u32[]{:S(2)}, u32[]{:S(2)}) %collective-permute-start.16) | collective-permute-done | bytes 131104 | tf_op jit(solution)/shard_map/ppermute | solution.py:395
  127.3 4.5 %collective-permute-done.17.refs_6_ = bf16[128,512]{1,0:T(8,128)(2,1)S(1)} collective-permute-done((bf16[128,512]{1,0:T(8,128)(2,1)S(1)}, bf16[128,512]{1,0:T(8,128)(2,1)S(1)}, u32[]{:S(2)}, u32[]{:S(2)}) %collective-permute-start.17) | collective-permute-done | bytes 131104 | tf_op jit(solution)/shard_map/ppermute | solution.py:395
  131.9 2.8 %collective-permute-done.18.refs_7_ = bf16[128,512]{1,0:T(8,128)(2,1)S(1)} collective-permute-done((bf16[128,512]{1,0:T(8,128)(2,1)S(1)}, bf16[128,512]{1,0:T(8,128)(2,1)S(1)}, u32[]{:S(2)}, u32[]{:S(2)}) %collective-permute-start.18) | collective-permute-done | bytes 131104 | tf_op jit(solution)/shard_map/ppermute | solution.py:395
  134.7 3.4 %last_product.1 = bf16[1024,512]{1,0:T(8,128)(2,1)} custom-call(s32[1]{0:T(128)} %bitcast.refs_0_.me_ref, s32[1,8]{1,0:T(1,128)S(1)} %copy-done.11, s32[1]{0:T(128)S(6)} %min.3.refs_11_.lead, bf16[128,512]{1,0:T(8,128)(2,1)S(1)} %get-tuple-element.37.refs_0_, bf16[128,512]{1,0:T(8,128)(2,1)S(1)} %collective-permute-done.12.refs_1_, ...), custom_call_target="tpu_custom_call" | custom-call | tf_op jit(solution)/shard_map/last_product/pallas_call | solution.py:320
  (93 shorter events, 26.6 us)
Async XLA Ops:
  26.2 61.2 %copy-start = (bf16[512,1536]{1,0:T(8,128)(2,1)S(1)}, bf16[512,1536]{1,0:T(8,128)(2,1)}, u32[]{:S(2)}) copy-start(bf16[512,1536]{1,0:T(8,128)(2,1)} %refs_12_.1) | copy-start | bytes 4718596
  26.2 61.2 %copy-start.1 = (bf16[512,1024]{1,0:T(8,128)(2,1)S(1)}, bf16[512,1024]{1,0:T(8,128)(2,1)}, u32[]{:S(2)}) copy-start(bf16[512,1024]{1,0:T(8,128)(2,1)} %refs_11_.1) | copy-start | bytes 3145732
  26.3 61.2 %copy-start.9 = (s32[1,8]{1,0:T(1,128)S(1)}, s32[1,8]{1,0:T(1,128)}, u32[]{:S(2)}) copy-start(s32[1,8]{1,0:T(1,128)} %refs_1_.5) | copy-start | bytes 100
  42.0 2.5 %collective-permute-start.7 = (bf16[4,512]{1,0:T(4,128)(2,1)S(1)}, bf16[4,512]{1,0:T(4,128)(2,1)S(1)}, u32[]{:S(2)}, u32[]{:S(2)}) collective-permute-start(bf16[4,512]{1,0:T(4,128)(2,1)S(1)} %pad_maximum_fusion.2), channel_id=1, source_target_pairs={{0,8},{8,0},{16,24},{24,16},{1,9},{9,1},{17,25},{25,17},{2,10},{10... | collective-permute-start | bytes 12296 | tf_op jit(solution)/shard_map/ppermute | solution.py:338
  44.5 4.6 %collective-permute-start.8 = (bf16[8,512]{1,0:T(8,128)(2,1)S(1)}, bf16[8,512]{1,0:T(8,128)(2,1)S(1)}, u32[]{:S(2)}, u32[]{:S(2)}) collective-permute-start(bf16[8,512]{1,0:T(8,128)(2,1)S(1)} %pad_maximum_fusion.1), channel_id=1, source_target_pairs={{0,16},{8,24},{16,0},{24,8},{1,17},{9,25},{17,1},{25,9},{2,18},{10... | collective-permute-start | bytes 24584 | tf_op jit(solution)/shard_map/ppermute | solution.py:338
  45.8 23.1 %collective-permute-start.6 = (bf16[128,512]{1,0:T(8,128)(2,1)}, bf16[128,512]{1,0:T(8,128)(2,1)S(1)}, u32[]{:S(2)}, u32[]{:S(2)}) collective-permute-start(bf16[128,512]{1,0:T(8,128)(2,1)} %get-tuple-element.34), channel_id=1, source_target_pairs={{0,7},{1,6},{2,5},{3,4},{4,3},{5,2},{6,1},{7,0},{8,15},{9,14},{10,... | collective-permute-start | bytes 393224 | tf_op jit(solution)/shard_map/ppermute | solution.py:395
  49.1 22.8 %collective-permute-start = (bf16[128,512]{1,0:T(8,128)(2,1)}, bf16[128,512]{1,0:T(8,128)(2,1)S(1)}, u32[]{:S(2)}, u32[]{:S(2)}) collective-permute-start(bf16[128,512]{1,0:T(8,128)(2,1)} %get-tuple-element.28), channel_id=1, source_target_pairs={{0,1},{1,0},{2,3},{3,2},{4,5},{5,4},{6,7},{7,6},{8,9},{9,8},{10,11... | collective-permute-start | bytes 393224 | tf_op jit(solution)/shard_map/ppermute | solution.py:395
  49.2 1.8 %collective-permute-start.9 = (bf16[16,512]{1,0:T(8,128)(2,1)S(1)}, bf16[16,512]{1,0:T(8,128)(2,1)S(1)}, u32[]{:S(2)}, u32[]{:S(2)}) collective-permute-start(bf16[16,512]{1,0:T(8,128)(2,1)S(1)} %pad_maximum_fusion), channel_id=1, source_target_pairs={{0,1},{1,0},{2,3},{3,2},{4,5},{5,4},{6,7},{7,6},{8,9},{9,8},{10,11... | collective-permute-start | bytes 49160 | tf_op jit(solution)/shard_map/ppermute | solution.py:338
  51.6 83.1 %copy-start.11 = (s32[1,8]{1,0:T(1,128)S(1)}, s32[1,8]{1,0:T(1,128)}, u32[]{:S(2)}) copy-start(s32[1,8]{1,0:T(1,128)} %pick_ref.1) | copy-start | bytes 100
  53.4 81.3 %copy-start.2 = (bf16[512,512]{1,0:T(8,128)(2,1)S(1)}, bf16[512,512]{1,0:T(8,128)(2,1)}, u32[]{:S(2)}) copy-start(bf16[512,512]{1,0:T(8,128)(2,1)} %refs_8_.5) | copy-start | bytes 1572868
  53.4 3.4 %collective-permute-start.10 = (bf16[32,512]{1,0:T(8,128)(2,1)}, bf16[32,512]{1,0:T(8,128)(2,1)}, u32[]{:S(2)}, u32[]{:S(2)}) collective-permute-start(bf16[32,512]{1,0:T(8,128)(2,1)} %concatenate.26), channel_id=1, source_target_pairs={{0,2},{1,3},{2,0},{3,1},{4,6},{5,7},{6,4},{7,5},{8,10},{9,11},{10,... | collective-permute-start | bytes 98312 | tf_op jit(solution)/shard_map/ppermute | solution.py:338
  62.1 5.4 %collective-permute-start.11 = (bf16[64,512]{1,0:T(8,128)(2,1)}, bf16[64,512]{1,0:T(8,128)(2,1)S(1)}, u32[]{:S(2)}, u32[]{:S(2)}) collective-permute-start(bf16[64,512]{1,0:T(8,128)(2,1)} %concatenate.27), channel_id=1, source_target_pairs={{0,4},{1,5},{2,6},{3,7},{4,0},{5,1},{6,2},{7,3},{8,12},{9,13},{10,... | collective-permute-start | bytes 196616 | tf_op jit(solution)/shard_map/ppermute | solution.py:338
  64.1 13.4 %collective-permute-start.1 = (bf16[128,512]{1,0:T(8,128)(2,1)}, bf16[128,512]{1,0:T(8,128)(2,1)}, u32[]{:S(2)}, u32[]{:S(2)}) collective-permute-start(bf16[128,512]{1,0:T(8,128)(2,1)} %copy-done.21), channel_id=1, source_target_pairs={{0,2},{1,3},{2,0},{3,1},{4,6},{5,7},{6,4},{7,5},{8,10},{9,11},{10,... | collective-permute-start | bytes 393224 | tf_op jit(solution)/shard_map/ppermute | solution.py:395
  64.2 13.3 %collective-permute-start.2 = (bf16[128,512]{1,0:T(8,128)(2,1)}, bf16[128,512]{1,0:T(8,128)(2,1)}, u32[]{:S(2)}, u32[]{:S(2)}) collective-permute-start(bf16[128,512]{1,0:T(8,128)(2,1)} %copy-done.20), channel_id=1, source_target_pairs={{0,3},{1,2},{2,1},{3,0},{4,7},{5,6},{6,5},{7,4},{8,11},{9,10},{10,... | collective-permute-start | bytes 393224 | tf_op jit(solution)/shard_map/ppermute | solution.py:395
  67.5 10.0 %collective-permute-start.3 = (bf16[128,512]{1,0:T(8,128)(2,1)}, bf16[128,512]{1,0:T(8,128)(2,1)}, u32[]{:S(2)}, u32[]{:S(2)}) collective-permute-start(bf16[128,512]{1,0:T(8,128)(2,1)} %copy-done.19), channel_id=1, source_target_pairs={{0,4},{1,5},{2,6},{3,7},{4,0},{5,1},{6,2},{7,3},{8,12},{9,13},{10,... | collective-permute-start | bytes 393224 | tf_op jit(solution)/shard_map/ppermute | solution.py:395
  69.0 13.9 %collective-permute-start.4 = (bf16[128,512]{1,0:T(8,128)(2,1)}, bf16[128,512]{1,0:T(8,128)(2,1)}, u32[]{:S(2)}, u32[]{:S(2)}) collective-permute-start(bf16[128,512]{1,0:T(8,128)(2,1)} %copy-done.18), channel_id=1, source_target_pairs={{0,5},{1,4},{2,7},{3,6},{4,1},{5,0},{6,3},{7,2},{8,13},{9,12},{10,... | collective-permute-start | bytes 393224 | tf_op jit(solution)/shard_map/ppermute | solution.py:395
  72.5 14.9 %collective-permute-start.5 = (bf16[128,512]{1,0:T(8,128)(2,1)}, bf16[128,512]{1,0:T(8,128)(2,1)}, u32[]{:S(2)}, u32[]{:S(2)}) collective-permute-start(bf16[128,512]{1,0:T(8,128)(2,1)} %copy-done.17), channel_id=1, source_target_pairs={{0,6},{1,7},{2,4},{3,5},{4,2},{5,3},{6,0},{7,1},{8,14},{9,15},{10,... | collective-permute-start | bytes 393224 | tf_op jit(solution)/shard_map/ppermute | solution.py:395
  106.9 6.0 %collective-permute-start.12 = (bf16[128,512]{1,0:T(8,128)(2,1)S(1)}, bf16[128,512]{1,0:T(8,128)(2,1)S(1)}, u32[]{:S(2)}, u32[]{:S(2)}) collective-permute-start(bf16[128,512]{1,0:T(8,128)(2,1)S(1)} %get-tuple-element.38), channel_id=1, source_target_pairs={{1,0},{0,1},{3,2},{2,3},{5,4},{4,5},{7,6},{6,7},{9,8},{8,9},{11,10... | collective-permute-start | bytes 393224 | tf_op jit(solution)/shard_map/ppermute | solution.py:395
  108.5 5.3 %collective-permute-start.13 = (bf16[128,512]{1,0:T(8,128)(2,1)S(1)}, bf16[128,512]{1,0:T(8,128)(2,1)S(1)}, u32[]{:S(2)}, u32[]{:S(2)}) collective-permute-start(bf16[128,512]{1,0:T(8,128)(2,1)S(1)} %get-tuple-element.39), channel_id=1, source_target_pairs={{2,0},{3,1},{0,2},{1,3},{6,4},{7,5},{4,6},{5,7},{10,8},{11,9},{8,1... | collective-permute-start | bytes 393224 | tf_op jit(solution)/shard_map/ppermute | solution.py:395
  108.5 10.9 %collective-permute-start.14 = (bf16[128,512]{1,0:T(8,128)(2,1)S(1)}, bf16[128,512]{1,0:T(8,128)(2,1)S(1)}, u32[]{:S(2)}, u32[]{:S(2)}) collective-permute-start(bf16[128,512]{1,0:T(8,128)(2,1)S(1)} %get-tuple-element.40), channel_id=1, source_target_pairs={{3,0},{2,1},{1,2},{0,3},{7,4},{6,5},{5,6},{4,7},{11,8},{10,9},{9,1... | collective-permute-start | bytes 393224 | tf_op jit(solution)/shard_map/ppermute | solution.py:395
  110.2 9.6 %collective-permute-start.15 = (bf16[128,512]{1,0:T(8,128)(2,1)S(1)}, bf16[128,512]{1,0:T(8,128)(2,1)S(1)}, u32[]{:S(2)}, u32[]{:S(2)}) collective-permute-start(bf16[128,512]{1,0:T(8,128)(2,1)S(1)} %get-tuple-element.41), channel_id=1, source_target_pairs={{4,0},{5,1},{6,2},{7,3},{0,4},{1,5},{2,6},{3,7},{12,8},{13,9},{14,... | collective-permute-start | bytes 393224 | tf_op jit(solution)/shard_map/ppermute | solution.py:395
  110.5 16.8 %collective-permute-start.16 = (bf16[128,512]{1,0:T(8,128)(2,1)S(1)}, bf16[128,512]{1,0:T(8,128)(2,1)S(1)}, u32[]{:S(2)}, u32[]{:S(2)}) collective-permute-start(bf16[128,512]{1,0:T(8,128)(2,1)S(1)} %get-tuple-element.42), channel_id=1, source_target_pairs={{5,0},{4,1},{7,2},{6,3},{1,4},{0,5},{3,6},{2,7},{13,8},{12,9},{15,... | collective-permute-start | bytes 393224 | tf_op jit(solution)/shard_map/ppermute | solution.py:395
  112.9 19.0 %collective-permute-start.17 = (bf16[128,512]{1,0:T(8,128)(2,1)S(1)}, bf16[128,512]{1,0:T(8,128)(2,1)S(1)}, u32[]{:S(2)}, u32[]{:S(2)}) collective-permute-start(bf16[128,512]{1,0:T(8,128)(2,1)S(1)} %get-tuple-element.43), channel_id=1, source_target_pairs={{6,0},{7,1},{4,2},{5,3},{2,4},{3,5},{0,6},{1,7},{14,8},{15,9},{12,... | collective-permute-start | bytes 393224 | tf_op jit(solution)/shard_map/ppermute | solution.py:395
  113.7 21.0 %collective-permute-start.18 = (bf16[128,512]{1,0:T(8,128)(2,1)S(1)}, bf16[128,512]{1,0:T(8,128)(2,1)S(1)}, u32[]{:S(2)}, u32[]{:S(2)}) collective-permute-start(bf16[128,512]{1,0:T(8,128)(2,1)S(1)} %get-tuple-element.44), channel_id=1, source_target_pairs={{7,0},{6,1},{5,2},{4,3},{3,4},{2,5},{1,6},{0,7},{15,8},{14,9},{13,... | collective-permute-start | bytes 393224 | tf_op jit(solution)/shard_map/ppermute | solution.py:395
  (29 other events, 193.6 us)

commit v2 on v1

v2 whole, which is shorter than its diff:
```python
from functools import partial
import math

import jax
import jax.numpy as jnp
from jax import lax
from jax.experimental import pallas as pl
from jax.experimental.pallas import tpu as pltpu
from jax.sharding import PartitionSpec as P

HEAD = 64
LEAF = 128
BALL = 512
CMP = 256
PAIR = 2 * HEAD
HIDE = 512
CHUNK = 256
MIB = 1 << 20
LATER = 40 * MIB
F32 = jnp.float32
BF16 = jnp.bfloat16
SCALE = HEAD ** (-0.5) * math.log2(math.e)

ANY = pl.BlockSpec(memory_space=pl.ANY)
VMEM = pl.BlockSpec(memory_space=pltpu.VMEM)
SMEM = pl.BlockSpec(memory_space=pltpu.SMEM)


def norm(values, gain):
    wide = values.astype(F32)
    return wide * lax.rsqrt(jnp.mean(wide * wide, axis=-1, keepdims=True) + 1e-06) * gain


def gelu(x):
    c = math.sqrt(2.0 / math.pi)
    t = jnp.tanh(x * (c + (c * 0.044715) * (x * x)))
    return x * (0.5 + 0.5 * t)


def dot(a, b):
    return jnp.dot(a, b, preferred_element_type=F32)


def dot_t(a, b):
    return lax.dot_general(a, b, (((1,), (1,)), ((), ())), preferred_element_type=F32)


def aligned(index, size):
    return pl.ds(pl.multiple_of(index * size, size), size)


def only_head(pair, half):
    lane = lax.broadcasted_iota(jnp.int32, pair.shape, 1)
    return jnp.where((lane >= HEAD) == bool(half), pair, jnp.zeros_like(pair))


def pair_scores(queries, keys):
    both = jnp.concatenate([only_head(queries, 0), only_head(queries, 1)], axis=0)
    return dot_t(both, keys)


def lay_values(out, values):
    keys = values.shape[0]
    ones = jnp.ones_like(values)
    for half in range(2):
        rows = slice(half * keys, (half + 1) * keys)
        out[rows, :PAIR] = only_head(values, half)
        out[rows, PAIR:] = only_head(ones, half)


def weigh(scores, laid):
    rows = scores.shape[0] // 2
    parts = []
    for half in range(2):
        own = scores[half * rows : (half + 1) * rows]
        parts.append(jnp.exp2(own - jnp.max(own, axis=1, keepdims=True)).astype(BF16))
    mixed = dot(jnp.concatenate(parts, axis=1), laid)
    return mixed[:, :PAIR] / mixed[:, PAIR:]


def pipelined(items, first, second):
    held = first(items[0])
    for n, item in enumerate(items):
        now = held
        if n + 1 < len(items):
            held = first(items[n + 1])
        second(item, now)


def send_to(me, s, peers):
    return me ^ s if peers & (peers - 1) == 0 else (me + s) % peers


def got_from(me, s, peers):
    return me ^ s if peers & (peers - 1) == 0 else (me + peers - s) % peers


def start_all(copies):
    for copy in copies:
        copy.start()


def wait_all(copies):
    for copy in copies:
        copy.wait()


def layer_one_kernel(peers, cap, slots, late, *refs):
    me_ref, pick_ref, lead, ids, gain1, gain2, gain3, points, w_in, w_out, w_up, w_down = refs[:12]
    refs = refs[12:]
    if late:
        (h_first, pool_first), refs = refs[:2], refs[2:]
    z_out, h_out, pool_out = refs[:3]
    sends, refs = refs[3 : 3 + len(slots)], refs[3 + len(slots) :]
    x_s, win_s, wout_s, wup_s, wdown_s, q_s, k_s, v_s, bias_s, mix_s, y_s, z_s, h_s, sem, send_sem = refs
    first = lead[0]
    ball = (1 - first) if late else first
    rows = aligned(ball, BALL)
    width = x_s.shape[1]
    hidden = wup_s.shape[1]
    pairs = width // PAIR
    copies = [
        pltpu.make_async_copy(points.at[rows, :], x_s, sem.at[0]),
        pltpu.make_async_copy(w_in, win_s, sem.at[1]),
        pltpu.make_async_copy(w_out, wout_s, sem.at[2]),
        pltpu.make_async_copy(w_up, wup_s, sem.at[3]),
        pltpu.make_async_copy(w_down, wdown_s, sem.at[4]),
    ]
    if late:
        copies.append(pltpu.make_async_copy(h_first, h_s.at[aligned(first, BALL), :], sem.at[5]))
    start_all(copies)

    own = ids[pl.ds(ball, 1), :]
    across = jnp.broadcast_to(own, (LEAF, BALL)).astype(F32)
    down = across.T
    for c in range(BALL // LEAF):
        cols = slice(c * LEAF, (c + 1) * LEAF)
        bias_s[:, cols] = jnp.where(down == across[:1, cols], 0.0, -1e30)

    copies[0].wait()
    h1 = norm(x_s[...], gain1[...]).astype(BF16)
    copies[1].wait()
    q_s[...] = (dot(h1, win_s[:, :width]) * SCALE).astype(BF16)
    k_s[...] = dot(h1, win_s[:, width : 2 * width]).astype(BF16)
    values = dot(h1, win_s[:, 2 * width :]).astype(BF16)
    for g in range(pairs):
        lay_values(v_s.at[g], values[:, g * PAIR : (g + 1) * PAIR])

    def scores(item):
        g, c = item
        cols = slice(g * PAIR, (g + 1) * PAIR)
        return pair_scores(q_s[c * CHUNK : (c + 1) * CHUNK, cols], k_s[:, cols])

    def mix(item, got):
        g, c = item
        at = slice(c * CHUNK, (c + 1) * CHUNK)
        bias = bias_s[at, :]
        out = weigh(got + jnp.concatenate([bias, bias], axis=0), v_s[g])
        mix_s[at, g * PAIR : (g + 1) * PAIR] = out.astype(BF16)

    pipelined([(g, c) for g in range(pairs) for c in range(BALL // CHUNK)], scores, mix)

    copies[2].wait()
    y = (x_s[...].astype(F32) + dot(mix_s[...], wout_s[...])).astype(BF16)
    y_s[...] = y
    inner = norm(y, gain2[...]).astype(BF16)
    copies[3].wait()
    copies[4].wait()
    total = y_s[...].astype(F32)
    for c in range(hidden // HIDE):
        cols = slice(c * HIDE, (c + 1) * HIDE)
        up = gelu(dot(inner, wup_s[:, cols])).astype(BF16)
        total = total + dot(up, wdown_s[cols, :])
    z = total.astype(BF16)
    z_s[...] = z
    h3 = norm(z, gain3[...]).astype(BF16)
    h_s[rows, :] = h3
    me = me_ref[0]
    per = BALL // LEAF
    if late:
        copies[5].wait()
    outgoing = []
    for n, (s, send) in enumerate(zip(slots, sends)):
        for c in range(cap):
            block = jnp.minimum(pick_ref[0, send_to(me, s, peers) * cap + c], 2 * per - 1)
            at = pl.ds(c * LEAF, LEAF)
            outgoing.append(
                pltpu.make_async_copy(h_s.at[aligned(block, LEAF), :], send.at[at, :], send_sem.at[n * cap + c])
            )
    outgoing.append(pltpu.make_async_copy(z_s, z_out, sem.at[6]))
    outgoing.append(pltpu.make_async_copy(h_s.at[rows, :], h_out, sem.at[7]))
    start_all(outgoing)
    wide = h3.astype(F32)
    pooled = []
    for c in range(BALL // CMP):
        pooled.append(jnp.sum(wide[c * CMP : (c + 1) * CMP], axis=0, keepdims=True) * CMP ** (-0.5))
    if late:
        pooled = [pool_first[c : c + 1, :] for c in range(BALL // CMP)] + pooled
        row = lax.broadcasted_iota(jnp.int32, pool_out.shape, 0) - me_ref[1] * len(pooled)
        placed = jnp.zeros(pool_out.shape, F32)
        for c, part in enumerate(pooled):
            placed = jnp.where(row == c, part, placed)
        pool_out[...] = placed.astype(BF16)
    else:
        for c, part in enumerate(pooled):
            pool_out[c : c + 1, :] = part
    wait_all(outgoing)


def layer_one(peers, cap, slots, late, rows, me, pick, lead, ids, gains, points, weights, *first):
    width = points.shape[1]
    hidden = weights[2].shape[1]
    half = jax.ShapeDtypeStruct((BALL, width), BF16)
    block = jax.ShapeDtypeStruct((cap * LEAF, width), BF16)
    pool = jax.ShapeDtypeStruct((rows, width), BF16 if late else F32)
    outs = [half, half, pool] + [block] * len(slots)
    out_specs = [ANY, ANY, VMEM] + [ANY] * len(slots)
    args = [me, pick, lead, ids, *gains, points, *weights]
    specs = [SMEM] * 3 + [VMEM] * 4 + [ANY] * 5
    if late:
        specs += [ANY, VMEM]
        args += first
    return pl.pallas_call(
        partial(layer_one_kernel, peers, cap, slots, late),
        out_shape=outs,
        in_specs=specs,
        out_specs=out_specs,
        scratch_shapes=[
            pltpu.VMEM((BALL, width), BF16),
            pltpu.VMEM((width, 3 * width), BF16),
            pltpu.VMEM((width, width), BF16),
            pltpu.VMEM((width, hidden), BF16),
            pltpu.VMEM((hidden, width), BF16),
            pltpu.VMEM((BALL, width), BF16),
            pltpu.VMEM((BALL, width), BF16),
            pltpu.VMEM((width // PAIR, 2 * BALL, 2 * PAIR), BF16),
            pltpu.VMEM((BALL, BALL), F32),
            pltpu.VMEM((BALL, width), BF16),
            pltpu.VMEM((BALL, width), BF16),
            pltpu.VMEM((BALL, width), BF16),
            pltpu.VMEM((points.shape[0], width), BF16),
            pltpu.SemaphoreType.DMA((8,)),
            pltpu.SemaphoreType.DMA((len(slots) * cap,)),
        ],
        compiler_params=pltpu.CompilerParams(vmem_limit_bytes=60 * MIB),
        cost_estimate=pl.CostEstimate(
            flops=2 * BALL * width * (4 * width + 2 * hidden) + 16 * BALL * BALL * width,
            bytes_accessed=8 * MIB,
            transcendentals=BALL * BALL * width // HEAD,
        ),
        name="layer_one_late" if late else "layer_one_lead",
    )(*args)


def place_of(recv_ref, slot, blocks):
    place, found = jnp.int32(0), jnp.int32(0)
    for j in range(blocks):
        hit = (recv_ref[0, j] == slot).astype(jnp.int32)
        place = place + j * hit
        found = found + hit
    return place, found > 0


def layer_two_kernel(peers, cap, blocks, start, columns, *refs):
    me_ref, recv_ref = refs[:2]
    arrived = refs[2 : 2 + peers]
    w_in = refs[2 + peers]
    outs = refs[3 + peers : 3 + 2 * peers]
    h_s, w_s, q_s, k_s, v_s, a_s, sem, block_sem = refs[3 + 2 * peers :]
    width = h_s.shape[1]
    pairs = columns // PAIR
    me = me_ref[0]
    balls = blocks * LEAF // BALL
    copies = []
    for i in range(3):
        cols = pl.ds(i * width + start, columns)
        copies.append(
            pltpu.make_async_copy(w_in.at[:, cols], w_s.at[:, pl.ds(i * columns, columns)], sem.at[i])
        )
    start_all(copies)
    places, moves = [], []
    for s in range(peers):
        for c in range(cap):
            place, found = place_of(recv_ref, got_from(me, s, peers) * cap + c, blocks)
            at = pl.ds(c * LEAF, LEAF)
            move = pltpu.make_async_copy(
                arrived[s].at[at, :], h_s.at[aligned(place, LEAF), :], block_sem.at[s * cap + c]
            )
            places.append(place)
            moves.append((found, move))
            pl.when(found)(move.start)
    wait_all(copies)
    for found, move in moves:
        pl.when(found)(move.wait)
    for b in range(balls):
        rows = slice(b * BALL, (b + 1) * BALL)
        h = h_s[rows, :]
        q_s[rows, :] = (dot(h, w_s[:, :columns]) * SCALE).astype(BF16)
        k_s[rows, :] = dot(h, w_s[:, columns : 2 * columns]).astype(BF16)
        values = dot(h, w_s[:, 2 * columns :]).astype(BF16)
        for g in range(pairs):
            lay_values(v_s.at[b * pairs + g], values[:, g * PAIR : (g + 1) * PAIR])

    def scores(item):
        b, g, c = item
        cols = slice(g * PAIR, (g + 1) * PAIR)
        at = b * BALL + c * CHUNK
        return pair_scores(q_s[at : at + CHUNK, cols], k_s[b * BALL : (b + 1) * BALL, cols])

    def mix(item, got):
        b, g, c = item
        at = b * BALL + c * CHUNK
        a_s[at : at + CHUNK, g * PAIR : (g + 1) * PAIR] = weigh(got, v_s[b * pairs + g]).astype(BF16)

    pipelined(
        [(b, g, c) for b in range(balls) for g in range(pairs) for c in range(BALL // CHUNK)], scores, mix
    )
    outgoing = []
    for s in range(peers):
        for c in range(cap):
            n = s * cap + c
            at = pl.ds(c * LEAF, LEAF)
            outgoing.append(
                pltpu.make_async_copy(a_s.at[aligned(places[n], LEAF), :], outs[s].at[at, :], block_sem.at[n])
            )
    start_all(outgoing)
    wait_all(outgoing)


def layer_two(peers, cap, start, columns, me, recv, arrived, w_in):
    blocks = recv.shape[1]
    width = w_in.shape[0]
    pairs = columns // PAIR
    rows = blocks * LEAF
    block = jax.ShapeDtypeStruct((cap * LEAF, columns), BF16)
    return pl.pallas_call(
        partial(layer_two_kernel, peers, cap, blocks, start, columns),
        out_shape=[block] * peers,
        in_specs=[SMEM, SMEM] + [ANY] * (peers + 1),
        out_specs=[ANY] * peers,
        scratch_shapes=[
            pltpu.VMEM((rows, width), BF16),
            pltpu.VMEM((width, 3 * columns), BF16),
            pltpu.VMEM((rows, columns), BF16),
            pltpu.VMEM((rows, columns), BF16),
            pltpu.VMEM((rows // BALL * pairs, 2 * BALL, 2 * PAIR), BF16),
            pltpu.VMEM((rows, columns), BF16),
            pltpu.SemaphoreType.DMA((3,)),
            pltpu.SemaphoreType.DMA((peers * cap,)),
        ],
        compiler_params=pltpu.CompilerParams(vmem_limit_bytes=LATER),
        cost_estimate=pl.CostEstimate(
            flops=rows * columns * (6 * width + 16 * BALL),
            bytes_accessed=4 * MIB,
            transcendentals=rows * BALL * columns // HEAD,
        ),
        name=f"layer_two_{start}",
    )(me, recv, *arrived, w_in)


def compressed_kernel(*refs):
    lead, h_first, h_late, z_first, z_late, pooled, w_comp, w_in, w_out, out = refs[:10]
    h_s, z_s, p_s, wc_s, wq_s, wo_s, q_s, ck_s, cv_s, a_s, o_s, sem, out_sem = refs[10:]
    rows, width = h_s.shape
    pairs = width // PAIR
    first = lead[0]
    copies = [
        pltpu.make_async_copy(pooled, p_s, sem.at[0]),
        pltpu.make_async_copy(w_comp, wc_s, sem.at[1]),
        pltpu.make_async_copy(w_in.at[:, pl.ds(0, width)], wq_s, sem.at[2]),
        pltpu.make_async_copy(h_first, h_s.at[aligned(first, BALL), :], sem.at[3]),
        pltpu.make_async_copy(h_late, h_s.at[aligned(1 - first, BALL), :], sem.at[4]),
        pltpu.make_async_copy(w_out, wo_s, sem.at[5]),
        pltpu.make_async_copy(z_first, z_s.at[aligned(first, BALL), :], sem.at[6]),
        pltpu.make_async_copy(z_late, z_s.at[aligned(1 - first, BALL), :], sem.at[7]),
    ]
    start_all(copies)
    wait_all(copies[:2])
    far = dot(p_s[...], wc_s[...]).astype(BF16)
    ck_s[...] = far[:, :width]
    for g in range(pairs):
        lay_values(cv_s.at[g], far[:, width + g * PAIR : width + (g + 1) * PAIR])
    wait_all(copies[2:5])
    q_s[...] = (dot(h_s[...], wq_s[...]) * SCALE).astype(BF16)

    def scores(item):
        g, c = item
        cols = slice(g * PAIR, (g + 1) * PAIR)
        return pair_scores(q_s[c * CHUNK : (c + 1) * CHUNK, cols], ck_s[:, cols])

    def mix(item, got):
        g, c = item
        a_s[c * CHUNK : (c + 1) * CHUNK, g * PAIR : (g + 1) * PAIR] = weigh(got, cv_s[g]).astype(BF16)

    pipelined([(g, c) for c in range(rows // CHUNK) for g in range(pairs)], scores, mix)
    wait_all(copies[5:])
    outgoing = []
    for c in range(rows // CHUNK):
        at = slice(c * CHUNK, (c + 1) * CHUNK)
        o_s[at, :] = z_s[at, :].astype(F32) + dot(a_s[at, :], wo_s[...])
        there = pl.ds(c * CHUNK, CHUNK)
        copy = pltpu.make_async_copy(o_s.at[there, :], out.at[there, :], out_sem.at[c])
        copy.start()
        outgoing.append(copy)
    wait_all(outgoing)


def compressed(lead, h_first, h_late, z_first, z_late, pooled, w_comp, w_in, w_out):
    rows, width = 2 * h_first.shape[0], h_first.shape[1]
    comp = pooled.shape[0]
    return pl.pallas_call(
        compressed_kernel,
        out_shape=jax.ShapeDtypeStruct((rows, width), F32),
        in_specs=[SMEM] + [ANY] * 8,
        out_specs=ANY,
        scratch_shapes=[
            pltpu.VMEM((rows, width), BF16),
            pltpu.VMEM((rows, width), BF16),
            pltpu.VMEM((comp, width), BF16),
            pltpu.VMEM((width, 2 * width), BF16),
            pltpu.VMEM((width, width), BF16),
            pltpu.VMEM((width, width), BF16),
            pltpu.VMEM((rows, width), BF16),
            pltpu.VMEM((comp, width), BF16),
            pltpu.VMEM((width // PAIR, 2 * comp, 2 * PAIR), BF16),
            pltpu.VMEM((rows, width), BF16),
            pltpu.VMEM((rows, width), F32),
            pltpu.SemaphoreType.DMA((8,)),
            pltpu.SemaphoreType.DMA((rows // CHUNK,)),
        ],
        compiler_params=pltpu.CompilerParams(vmem_limit_bytes=60 * MIB),
        cost_estimate=pl.CostEstimate(
            flops=rows * width * (4 * width + 16 * comp),
            bytes_accessed=8 * MIB,
            transcendentals=rows * comp * width // HEAD,
        ),
        name="compressed",
    )(lead, h_first, h_late, z_first, z_late, pooled, w_comp, w_in, w_out)


def final_kernel(peers, cap, bounds, me_ref, pick_ref, *refs):
    parts = len(bounds)
    back = [refs[p * peers : (p + 1) * peers] for p in range(parts)]
    w_out, base, out, w_s, b_s, m_s, o_s, sem, block_sem, out_sem = refs[parts * peers :]
    blocks = b_s.shape[0] // LEAF
    me = me_ref[0]
    copies = [
        pltpu.make_async_copy(w_out, w_s, sem.at[0]),
        pltpu.make_async_copy(base, b_s, sem.at[1]),
    ]
    start_all(copies)
    moves = []
    for p, (start, columns) in enumerate(bounds):
        for s in range(peers):
            for c in range(cap):
                block = pick_ref[0, send_to(me, s, peers) * cap + c]
                found = block < blocks
                at = pl.ds(c * LEAF, LEAF)
                place = aligned(jnp.minimum(block, blocks - 1), LEAF)
                move = pltpu.make_async_copy(
                    back[p][s].at[at, :],
                    m_s.at[place, pl.ds(start, columns)],
                    block_sem.at[(p * peers + s) * cap + c],
                )
                moves.append((found, move))
                pl.when(found)(move.start)
    wait_all(copies)
    for found, move in moves:
        pl.when(found)(move.wait)
    outgoing = []
    for b in range(b_s.shape[0] // CHUNK):
        rows = slice(b * CHUNK, (b + 1) * CHUNK)
        o_s[rows, :] = (b_s[rows, :] + dot(m_s[rows, :], w_s[...])).astype(BF16)
        at = pl.ds(b * CHUNK, CHUNK)
        copy = pltpu.make_async_copy(o_s.at[at, :], out.at[at, :], out_sem.at[b])
        copy.start()
        outgoing.append(copy)
    wait_all(outgoing)


def final(peers, cap, bounds, me, pick, back, w_out, base):
    rows, width = base.shape
    return pl.pallas_call(
        partial(final_kernel, peers, cap, bounds),
        out_shape=jax.ShapeDtypeStruct((rows, width), BF16),
        in_specs=[SMEM] * 2 + [ANY] * (peers * len(bounds) + 2),
        out_specs=ANY,
        scratch_shapes=[
            pltpu.VMEM((width, width), BF16),
            pltpu.VMEM((rows, width), F32),
            pltpu.VMEM((rows, width), BF16),
            pltpu.VMEM((rows, width), BF16),
            pltpu.SemaphoreType.DMA((2,)),
            pltpu.SemaphoreType.DMA((len(bounds) * peers * cap,)),
            pltpu.SemaphoreType.DMA((rows // CHUNK,)),
        ],
        compiler_params=pltpu.CompilerParams(vmem_limit_bytes=LATER),
        cost_estimate=pl.CostEstimate(
            flops=2 * rows * width * width, bytes_accessed=4 * MIB, transcendentals=0
        ),
        name="last_product",
    )(me, pick, *back, w_out, base)


def shards(
    axes,
    points,
    ball_ids,
    send_pick,
    recv_from,
    gain_one,
    attn_in_one,
    attn_out_one,
    gain_two,
    mlp_up,
    mlp_down,
    gain_three,
    compress_proj,
    attn_in_two,
    attn_out_two,
):
    peers = axes[1][1]
    cap = send_pick.shape[1] // peers
    per = BALL // LEAF
    width = points.shape[1]
    me = lax.axis_index("pts").astype(jnp.int32)
    far = peers - 1
    target = send_to(me, far, peers)
    lead_slot = lax.dynamic_slice(send_pick[0], (target * cap,), (1,))
    lead = jnp.minimum(lead_slot // per, ball_ids.shape[0] - 1).astype(jnp.int32)
    place = lax.axis_index("grp").astype(jnp.int32) * peers + me
    me1 = jnp.stack([me, place])
    gains = tuple(g.reshape(1, -1) for g in (gain_one, gain_two, gain_three))
    weights = (attn_in_one, attn_out_one, mlp_up, mlp_down)
    one = partial(layer_one, peers, cap)

    def travel(blocks, s, home):
        if s == 0:
            return blocks
        pattern = [(i, send_to(i, s, peers)) for i in range(peers)]
        if home:
            pattern = [(b, a) for a, b in pattern]
        return lax.ppermute(blocks, "pts", pattern)

    early = [far] if cap == 1 else []
    local = points.shape[0] // CMP
    z_first, h_first, pool_first, *lead_sends = one(
        early, False, local // 2, me1, send_pick, lead, ball_ids, gains, points, weights
    )
    arrived = {s: travel(b, s, False) for s, b in zip(early, lead_sends)}
    order = [s for s in range(peers) if s not in early]
    every = local * axes[0][1] * peers
    late_outs = one(
        order, True, every, me1, send_pick, lead, ball_ids, gains, points, weights, h_first, pool_first
    )
    late_outs, arrived = lax.optimization_barrier((late_outs, arrived))
    z_late, h_late, placed, *late_sends = late_outs
    arrived.update({s: travel(b, s, False) for s, b in zip(order, late_sends)})
    pooled = lax.psum(placed, ("grp", "pts"))
    bounds = [(0, width // 2), (width // 2, width // 2)]
    back = []
    for start, columns in bounds:
        mixed = layer_two(
            peers, cap, start, columns, me1, recv_from, [arrived[s] for s in range(peers)], attn_in_two
        )
        part = {s: travel(mixed[s], s, True) for s in range(peers)}
        back.extend(part[s] for s in range(peers))
    base = compressed(
        lead, h_first, h_late, z_first, z_late, pooled, compress_proj, attn_in_two, attn_out_two
    )
    return final(peers, cap, bounds, me1, send_pick, back, attn_out_two, base)


def solution(mesh):
    rows = P(("grp", "pts"), None)
    axes = (("grp", mesh.shape["grp"]), ("pts", mesh.shape["pts"]))
    return jax.shard_map(
        partial(shards, axes),
        mesh=mesh,
        in_specs=(rows,) * 4 + (P(),) * 10,
        out_specs=rows,
        check_vma=False,
    )
```

time: 139 us -> 226 us (1.63)
  the two profiles are of different devices: /device:TPU:11 before, /device:TPU:0 now
where the time goes in v2:
time: 226 us
  waiting for transfers between devices  131 us (58%)
  Pallas kernels  45.4 us (20%)
  starting transfers between devices  28.5 us (13%)
  between operations  16 us (7%)
  local copies, waits for them, and re-layouts  3.77 us (2%)
    psum x1, waiting for transfers between devices, shards(): pooled = lax.psum(placed, ('grp', 'pts'))  115 us
    ppermute x21, starting transfers between devices, travel(): return lax.ppermute(blocks, 'pts', pattern)  28.5 us
    pallas_call x2, Pallas kernels, layer_one(): pl.pallas_call(partial(layer_one_kernel, peers, cap, slots, late), out_sh...  23.4 us
    ppermute x21, waiting for transfers between devices, travel(): return lax.ppermute(blocks, 'pts', pattern)  16 us
    pallas_call x2, Pallas kernels, layer_two(): pl.pallas_call(partial(layer_two_kernel, peers, cap, blocks, start, colum...  13.7 us
    pallas_call x1, Pallas kernels, compressed(): pl.pallas_call(compressed_kernel, out_shape=jax.ShapeDtypeStruct((rows, w...  5.75 us
  transfers between devices with their start and end apart: 22, of which 6 were waited for; matrix products, arithmetic and copies ran while one was open for 0% of the time, Pallas kernels for 11%

profile of v2, /device:TPU:0, one launch (start us, length us, event | category | flops | bytes accessed | tf_op | source)
XLA Modules:
  0.0 225.7 jit_solution(17952311668273866308)
XLA Ops:
  6.5 1.3 constant_dynamic-slice_fusion
  10.8 11.4 %layer_one_lead.1 = (bf16[512,512]{1,0:T(8,128)(2,1)}, bf16[512,512]{1,0:T(8,128)(2,1)}, f32[2,512]{1,0:T(2,128)}, bf16[128,512]{1,0:T(8,128)(2,1)}) custom-call(s32[2]{0:T(128)} %pad_add_fusion.refs_0_.me_ref, s32[1,8]{1,0:T(1,128)} %pick_ref.1, s32[1]{0:T(128)S(6)} %min.3.refs_2_.refs_0_, s32[2,512]{1,0:T(2,128)} %refs_3_.3, f32[1,512]{1,0:T(1,128)} %bitcast.6, ...), custom_call_target="tpu_custom_call" | custom-call | flops 5368709120 | bytes 8388608 | tf_op jit(solution)/shard_map/layer_one_lead/pallas_call | solution.py:223
  22.2 4.5 %collective-permute-start = (bf16[128,512]{1,0:T(8,128)(2,1)}, bf16[128,512]{1,0:T(8,128)(2,1)S(1)}, u32[]{:S(2)}, u32[]{:S(2)}) collective-permute-start(bf16[128,512]{1,0:T(8,128)(2,1)} %get-tuple-element.58), channel_id=1, source_target_pairs={{0,7},{1,6},{2,5},{3,4},{4,3},{5,2},{6,1},{7,0},{8,15},{9,14},{10,... | collective-permute-start | bytes 393224 | tf_op jit(solution)/shard_map/ppermute | solution.py:543
  26.7 12.1 %layer_one_late.1 = (bf16[512,512]{1,0:T(8,128)(2,1)}, bf16[512,512]{1,0:T(8,128)(2,1)}, bf16[128,512]{1,0:T(8,128)(2,1)}, bf16[128,512]{1,0:T(8,128)(2,1)}, bf1...) custom-call(s32[2]{0:T(128)} %pad_add_fusion.refs_0_.me_ref, ...), custom_call_target="tpu_custom_call" | custom-call | flops 5368709120 | bytes 8388608 | tf_op jit(solution)/shard_map/layer_one_late/pallas_call | solution.py:223
  39.6 1.4 collective-permute-start.3
  41.0 3.0 %collective-permute-start.5 = (bf16[128,512]{1,0:T(8,128)(2,1)}, bf16[128,512]{1,0:T(8,128)(2,1)S(1)}, u32[]{:S(2)}, u32[]{:S(2)}) collective-permute-start(bf16[128,512]{1,0:T(8,128)(2,1)} %get-tuple-element.64), channel_id=1, source_target_pairs={{0,5},{1,4},{2,7},{3,6},{4,1},{5,0},{6,3},{7,2},{8,13},{9,12},{10,... | collective-permute-start | bytes 393224 | tf_op jit(solution)/shard_map/ppermute | solution.py:543
  44.0 3.5 %collective-permute-done.2.refs_4_ = bf16[128,512]{1,0:T(8,128)(2,1)S(1)} collective-permute-done((bf16[128,512]{1,0:T(8,128)(2,1)}, bf16[128,512]{1,0:T(8,128)(2,1)S(1)}, u32[]{:S(2)}, u32[]{:S(2)}) %collective-permute-start.2) | collective-permute-done | bytes 131104 | tf_op jit(solution)/shard_map/ppermute | solution.py:543
  47.5 1.3 collective-permute-done.3.refs_5_
  48.8 8.1 %collective-permute-done.4.refs_6_ = bf16[128,512]{1,0:T(8,128)(2,1)S(1)} collective-permute-done((bf16[128,512]{1,0:T(8,128)(2,1)}, bf16[128,512]{1,0:T(8,128)(2,1)S(1)}, u32[]{:S(2)}, u32[]{:S(2)}) %collective-permute-start.4) | collective-permute-done | bytes 131104 | tf_op jit(solution)/shard_map/ppermute | solution.py:543
  56.9 2.3 %collective-permute-done.5.refs_7_ = bf16[128,512]{1,0:T(8,128)(2,1)S(1)} collective-permute-done((bf16[128,512]{1,0:T(8,128)(2,1)}, bf16[128,512]{1,0:T(8,128)(2,1)S(1)}, u32[]{:S(2)}, u32[]{:S(2)}) %collective-permute-start.5) | collective-permute-done | bytes 131104 | tf_op jit(solution)/shard_map/ppermute | solution.py:543
  60.1 6.7 %layer_two_256.1 = (bf16[128,256]{1,0:T(8,128)(2,1)S(1)}, bf16[128,256]{1,0:T(8,128)(2,1)S(1)}, bf16[128,256]{1,0:T(8,128)(2,1)S(1)}, bf16[128,256]{1,0:T(8,128)...) custom-call(s32[2]{0:T(128)S(1)} %copy-done.3, ...), custom_call_target="tpu_custom_call" | custom-call | flops 2952790016 | bytes 4194304 | tf_op jit(solution)/shard_map/layer_two_256/pallas_call | solution.py:336
  67.3 3.4 %collective-permute-start.15 = (bf16[128,256]{1,0:T(8,128)(2,1)S(1)}, bf16[128,256]{1,0:T(8,128)(2,1)S(1)}, u32[]{:S(2)}, u32[]{:S(2)}) collective-permute-start(bf16[128,256]{1,0:T(8,128)(2,1)S(1)} %get-tuple-element.77), channel_id=1, source_target_pairs={{2,0},{3,1},{0,2},{1,3},{6,4},{7,5},{4,6},{5,7},{10,8},{11,9},{8,1... | collective-permute-start | bytes 196616 | tf_op jit(solution)/shard_map/ppermute | solution.py:543
  71.5 1.6 collective-permute-start.18
  73.1 6.9 %layer_two_0.1 = (bf16[128,256]{1,0:T(8,128)(2,1)S(1)}, bf16[128,256]{1,0:T(8,128)(2,1)S(1)}, bf16[128,256]{1,0:T(8,128)(2,1)S(1)}, bf16[128,256]{1,0:T(8,128)(2...) custom-call(s32[2]{0:T(128)S(1)} %copy-done.3, ...), custom_call_target="tpu_custom_call" | custom-call | flops 2952790016 | bytes 4194304 | tf_op jit(solution)/shard_map/layer_two_0/pallas_call | solution.py:336
  80.0 1.8 collective-permute-start.19
  81.8 2.1 collective-permute-start.20
  84.2 1.6 collective-permute-start.9
  86.7 2.1 collective-permute-start.10
  88.7 1.4 collective-permute-start.11
  90.2 2.7 %collective-permute-start.12 = (bf16[128,256]{1,0:T(8,128)(2,1)S(1)}, bf16[128,256]{1,0:T(8,128)(2,1)S(1)}, u32[]{:S(2)}, u32[]{:S(2)}) collective-permute-start(bf16[128,256]{1,0:T(8,128)(2,1)S(1)} %get-tuple-element.73), channel_id=1, source_target_pairs={{6,0},{7,1},{4,2},{5,3},{2,4},{3,5},{0,6},{1,7},{14,8},{15,9},{12,... | collective-permute-start | bytes 196616 | tf_op jit(solution)/shard_map/ppermute | solution.py:543
  93.5 115.4 %all-reduce.2.cloned.1.call-done.refs_5_ = bf16[128,512]{1,0:T(8,128)(2,1)} async-done(((bf16[128,512]{1,0:T(8,128)(2,1)}), bf16[128,512]{1,0:T(8,128)(2,1)}) %all-reduce.2.cloned.1.call-update) | async-done | bytes 131088 | tf_op jit(solution)/shard_map/psum | solution.py:559
  208.8 5.7 %compressed.1.refs_17_ = f32[1024,512]{1,0:T(8,128)} custom-call(s32[1]{0:T(128)S(6)} %min.3.refs_2_.refs_0_, bf16[512,512]{1,0:T(8,128)(2,1)} %get-tuple-element.46.refs_12_.refs_1_, bf16[512,512]{1,0:T(8,128)(2,1)} %get-tuple-element.83.refs_2_, bf16[512,512]{1,0:T(8,128)(2,1)} %get-tuple-element.84.refs_3_, bf16[512,512]{1,0:T(8,128)(2,1)} %get-tuple-element.85.refs_4_, ...), custom_call_target="tpu_custom_call" | custom-call | flops 2147483648 | bytes 8388608 | tf_op jit(solution)/shard_map/compressed/pallas_call | solution.py:411
  214.7 1.6 copy-done
  216.3 2.6 %last_product.1 = bf16[1024,512]{1,0:T(8,128)(2,1)} custom-call(s32[2]{0:T(128)S(1)} %copy-done.3, s32[1,8]{1,0:T(1,128)S(1)} %copy-done.2, bf16[128,256]{1,0:T(8,128)(2,1)S(1)} %get-tuple-element.67.refs_0_, bf16[128,256]{1,0:T(8,128)(2,1)S(1)} %collective-permute-done.7.refs_1_, bf16[128,256]{1,0:T(8,128)(2,1)S(1)} %collective-permute-done.8.refs_2_, ...), custom_call_target="tpu_custom_call" | custom-call | flops 536870912 | bytes 4194304 | tf_op jit(solution)/shard_map/last_product/pallas_call | solution.py:483
  (45 shorter events, 5.3 us)
Async XLA Ops:
  6.5 202.3 %all-reduce.2.cloned.1.call-start = ((), (), s32[]{:S(2)}) async-start(), calls=%async_computation | async-start | bytes 262144 | tf_op jit(solution)/shard_map/psum | solution.py:559
  22.2 16.6 %collective-permute-start = (bf16[128,512]{1,0:T(8,128)(2,1)}, bf16[128,512]{1,0:T(8,128)(2,1)S(1)}, u32[]{:S(2)}, u32[]{:S(2)}) collective-permute-start(bf16[128,512]{1,0:T(8,128)(2,1)} %get-tuple-element.58), channel_id=1, source_target_pairs={{0,7},{1,6},{2,5},{3,4},{4,3},{5,2},{6,1},{7,0},{8,15},{9,14},{10,... | collective-permute-start | bytes 393224 | tf_op jit(solution)/shard_map/ppermute | solution.py:543
  26.7 32.5 %copy-start.4 = (bf16[512,1536]{1,0:T(8,128)(2,1)S(1)}, bf16[512,1536]{1,0:T(8,128)(2,1)}, u32[]{:S(2)}) copy-start(bf16[512,1536]{1,0:T(8,128)(2,1)} %refs_7_.5) | copy-start | bytes 4718596
  26.7 32.5 %copy-start.5 = (s32[1,8]{1,0:T(1,128)S(1)}, s32[1,8]{1,0:T(1,128)}, u32[]{:S(2)}) copy-start(s32[1,8]{1,0:T(1,128)} %refs_1_.7) | copy-start | bytes 100
  38.8 5.2 %collective-permute-start.1 = (bf16[128,512]{1,0:T(8,128)(2,1)}, bf16[128,512]{1,0:T(8,128)(2,1)S(1)}, u32[]{:S(2)}, u32[]{:S(2)}) collective-permute-start(bf16[128,512]{1,0:T(8,128)(2,1)} %get-tuple-element.60), channel_id=1, source_target_pairs={{0,1},{1,0},{2,3},{3,2},{4,5},{5,4},{6,7},{7,6},{8,9},{9,8},{10,11... | collective-permute-start | bytes 393224 | tf_op jit(solution)/shard_map/ppermute | solution.py:543
  39.6 7.9 %collective-permute-start.2 = (bf16[128,512]{1,0:T(8,128)(2,1)}, bf16[128,512]{1,0:T(8,128)(2,1)S(1)}, u32[]{:S(2)}, u32[]{:S(2)}) collective-permute-start(bf16[128,512]{1,0:T(8,128)(2,1)} %get-tuple-element.61), channel_id=1, source_target_pairs={{0,2},{1,3},{2,0},{3,1},{4,6},{5,7},{6,4},{7,5},{8,10},{9,11},{10,... | collective-permute-start | bytes 393224 | tf_op jit(solution)/shard_map/ppermute | solution.py:543
  39.6 9.3 %collective-permute-start.3 = (bf16[128,512]{1,0:T(8,128)(2,1)}, bf16[128,512]{1,0:T(8,128)(2,1)S(1)}, u32[]{:S(2)}, u32[]{:S(2)}) collective-permute-start(bf16[128,512]{1,0:T(8,128)(2,1)} %get-tuple-element.62), channel_id=1, source_target_pairs={{0,3},{1,2},{2,1},{3,0},{4,7},{5,6},{6,5},{7,4},{8,11},{9,10},{10,... | collective-permute-start | bytes 393224 | tf_op jit(solution)/shard_map/ppermute | solution.py:543
  41.0 15.9 %collective-permute-start.4 = (bf16[128,512]{1,0:T(8,128)(2,1)}, bf16[128,512]{1,0:T(8,128)(2,1)S(1)}, u32[]{:S(2)}, u32[]{:S(2)}) collective-permute-start(bf16[128,512]{1,0:T(8,128)(2,1)} %get-tuple-element.63), channel_id=1, source_target_pairs={{0,4},{1,5},{2,6},{3,7},{4,0},{5,1},{6,2},{7,3},{8,12},{9,13},{10,... | collective-permute-start | bytes 393224 | tf_op jit(solution)/shard_map/ppermute | solution.py:543
  41.0 18.2 %collective-permute-start.5 = (bf16[128,512]{1,0:T(8,128)(2,1)}, bf16[128,512]{1,0:T(8,128)(2,1)S(1)}, u32[]{:S(2)}, u32[]{:S(2)}) collective-permute-start(bf16[128,512]{1,0:T(8,128)(2,1)} %get-tuple-element.64), channel_id=1, source_target_pairs={{0,5},{1,4},{2,7},{3,6},{4,1},{5,0},{6,3},{7,2},{8,13},{9,12},{10,... | collective-permute-start | bytes 393224 | tf_op jit(solution)/shard_map/ppermute | solution.py:543
  44.0 15.2 %collective-permute-start.6 = (bf16[128,512]{1,0:T(8,128)(2,1)}, bf16[128,512]{1,0:T(8,128)(2,1)S(1)}, u32[]{:S(2)}, u32[]{:S(2)}) collective-permute-start(bf16[128,512]{1,0:T(8,128)(2,1)} %get-tuple-element.65), channel_id=1, source_target_pairs={{0,6},{1,7},{2,4},{3,5},{4,2},{5,3},{6,0},{7,1},{8,14},{9,15},{10,... | collective-permute-start | bytes 393224 | tf_op jit(solution)/shard_map/ppermute | solution.py:543
  66.9 13.2 %collective-permute-start.14 = (bf16[128,256]{1,0:T(8,128)(2,1)S(1)}, bf16[128,256]{1,0:T(8,128)(2,1)S(1)}, u32[]{:S(2)}, u32[]{:S(2)}) collective-permute-start(bf16[128,256]{1,0:T(8,128)(2,1)S(1)} %get-tuple-element.76), channel_id=1, source_target_pairs={{1,0},{0,1},{3,2},{2,3},{5,4},{4,5},{7,6},{6,7},{9,8},{8,9},{11,10... | collective-permute-start | bytes 196616 | tf_op jit(solution)/shard_map/ppermute | solution.py:543
  67.3 14.6 %collective-permute-start.15 = (bf16[128,256]{1,0:T(8,128)(2,1)S(1)}, bf16[128,256]{1,0:T(8,128)(2,1)S(1)}, u32[]{:S(2)}, u32[]{:S(2)}) collective-permute-start(bf16[128,256]{1,0:T(8,128)(2,1)S(1)} %get-tuple-element.77), channel_id=1, source_target_pairs={{2,0},{3,1},{0,2},{1,3},{6,4},{7,5},{4,6},{5,7},{10,8},{11,9},{8,1... | collective-permute-start | bytes 196616 | tf_op jit(solution)/shard_map/ppermute | solution.py:543
  70.6 13.3 %collective-permute-start.16 = (bf16[128,256]{1,0:T(8,128)(2,1)S(1)}, bf16[128,256]{1,0:T(8,128)(2,1)S(1)}, u32[]{:S(2)}, u32[]{:S(2)}) collective-permute-start(bf16[128,256]{1,0:T(8,128)(2,1)S(1)} %get-tuple-element.78), channel_id=1, source_target_pairs={{3,0},{2,1},{1,2},{0,3},{7,4},{6,5},{5,6},{4,7},{11,8},{10,9},{9,1... | collective-permute-start | bytes 196616 | tf_op jit(solution)/shard_map/ppermute | solution.py:543
  70.7 13.4 %collective-permute-start.17 = (bf16[128,256]{1,0:T(8,128)(2,1)S(1)}, bf16[128,256]{1,0:T(8,128)(2,1)S(1)}, u32[]{:S(2)}, u32[]{:S(2)}) collective-permute-start(bf16[128,256]{1,0:T(8,128)(2,1)S(1)} %get-tuple-element.79), channel_id=1, source_target_pairs={{4,0},{5,1},{6,2},{7,3},{0,4},{1,5},{2,6},{3,7},{12,8},{13,9},{14,... | collective-permute-start | bytes 196616 | tf_op jit(solution)/shard_map/ppermute | solution.py:543
  71.5 12.7 %collective-permute-start.18 = (bf16[128,256]{1,0:T(8,128)(2,1)S(1)}, bf16[128,256]{1,0:T(8,128)(2,1)S(1)}, u32[]{:S(2)}, u32[]{:S(2)}) collective-permute-start(bf16[128,256]{1,0:T(8,128)(2,1)S(1)} %get-tuple-element.80), channel_id=1, source_target_pairs={{5,0},{4,1},{7,2},{6,3},{1,4},{0,5},{3,6},{2,7},{13,8},{12,9},{15,... | collective-permute-start | bytes 196616 | tf_op jit(solution)/shard_map/ppermute | solution.py:543
  80.0 6.6 %collective-permute-start.19 = (bf16[128,256]{1,0:T(8,128)(2,1)S(1)}, bf16[128,256]{1,0:T(8,128)(2,1)S(1)}, u32[]{:S(2)}, u32[]{:S(2)}) collective-permute-start(bf16[128,256]{1,0:T(8,128)(2,1)S(1)} %get-tuple-element.81), channel_id=1, source_target_pairs={{6,0},{7,1},{4,2},{5,3},{2,4},{3,5},{0,6},{1,7},{14,8},{15,9},{12,... | collective-permute-start | bytes 196616 | tf_op jit(solution)/shard_map/ppermute | solution.py:543
  81.8 6.9 %collective-permute-start.20 = (bf16[128,256]{1,0:T(8,128)(2,1)S(1)}, bf16[128,256]{1,0:T(8,128)(2,1)S(1)}, u32[]{:S(2)}, u32[]{:S(2)}) collective-permute-start(bf16[128,256]{1,0:T(8,128)(2,1)S(1)} %get-tuple-element.82), channel_id=1, source_target_pairs={{7,0},{6,1},{5,2},{4,3},{3,4},{2,5},{1,6},{0,7},{15,8},{14,9},{13,... | collective-permute-start | bytes 196616 | tf_op jit(solution)/shard_map/ppermute | solution.py:543
  83.9 6.2 %collective-permute-start.7 = (bf16[128,256]{1,0:T(8,128)(2,1)S(1)}, bf16[128,256]{1,0:T(8,128)(2,1)S(1)}, u32[]{:S(2)}, u32[]{:S(2)}) collective-permute-start(bf16[128,256]{1,0:T(8,128)(2,1)S(1)} %get-tuple-element.68), channel_id=1, source_target_pairs={{1,0},{0,1},{3,2},{2,3},{5,4},{4,5},{7,6},{6,7},{9,8},{8,9},{11,10... | collective-permute-start | bytes 196616 | tf_op jit(solution)/shard_map/ppermute | solution.py:543
  84.1 8.7 %collective-permute-start.8 = (bf16[128,256]{1,0:T(8,128)(2,1)S(1)}, bf16[128,256]{1,0:T(8,128)(2,1)S(1)}, u32[]{:S(2)}, u32[]{:S(2)}) collective-permute-start(bf16[128,256]{1,0:T(8,128)(2,1)S(1)} %get-tuple-element.69), channel_id=1, source_target_pairs={{2,0},{3,1},{0,2},{1,3},{6,4},{7,5},{4,6},{5,7},{10,8},{11,9},{8,1... | collective-permute-start | bytes 196616 | tf_op jit(solution)/shard_map/ppermute | solution.py:543
  84.2 130.4 %collective-permute-start.9 = (bf16[128,256]{1,0:T(8,128)(2,1)S(1)}, bf16[128,256]{1,0:T(8,128)(2,1)S(1)}, u32[]{:S(2)}, u32[]{:S(2)}) collective-permute-start(bf16[128,256]{1,0:T(8,128)(2,1)S(1)} %get-tuple-element.70), channel_id=1, source_target_pairs={{3,0},{2,1},{1,2},{0,3},{7,4},{6,5},{5,6},{4,7},{11,8},{10,9},{9,1... | collective-permute-start | bytes 196616 | tf_op jit(solution)/shard_map/ppermute | solution.py:543
  86.7 128.0 %collective-permute-start.10 = (bf16[128,256]{1,0:T(8,128)(2,1)S(1)}, bf16[128,256]{1,0:T(8,128)(2,1)S(1)}, u32[]{:S(2)}, u32[]{:S(2)}) collective-permute-start(bf16[128,256]{1,0:T(8,128)(2,1)S(1)} %get-tuple-element.71), channel_id=1, source_target_pairs={{4,0},{5,1},{6,2},{7,3},{0,4},{1,5},{2,6},{3,7},{12,8},{13,9},{14,... | collective-permute-start | bytes 196616 | tf_op jit(solution)/shard_map/ppermute | solution.py:543
  88.7 125.9 %collective-permute-start.11 = (bf16[128,256]{1,0:T(8,128)(2,1)S(1)}, bf16[128,256]{1,0:T(8,128)(2,1)S(1)}, u32[]{:S(2)}, u32[]{:S(2)}) collective-permute-start(bf16[128,256]{1,0:T(8,128)(2,1)S(1)} %get-tuple-element.72), channel_id=1, source_target_pairs={{5,0},{4,1},{7,2},{6,3},{1,4},{0,5},{3,6},{2,7},{13,8},{12,9},{15,... | collective-permute-start | bytes 196616 | tf_op jit(solution)/shard_map/ppermute | solution.py:543
  90.2 124.5 %collective-permute-start.12 = (bf16[128,256]{1,0:T(8,128)(2,1)S(1)}, bf16[128,256]{1,0:T(8,128)(2,1)S(1)}, u32[]{:S(2)}, u32[]{:S(2)}) collective-permute-start(bf16[128,256]{1,0:T(8,128)(2,1)S(1)} %get-tuple-element.73), channel_id=1, source_target_pairs={{6,0},{7,1},{4,2},{5,3},{2,4},{3,5},{0,6},{1,7},{14,8},{15,9},{12,... | collective-permute-start | bytes 196616 | tf_op jit(solution)/shard_map/ppermute | solution.py:543
  92.8 121.8 %collective-permute-start.13 = (bf16[128,256]{1,0:T(8,128)(2,1)S(1)}, bf16[128,256]{1,0:T(8,128)(2,1)S(1)}, u32[]{:S(2)}, u32[]{:S(2)}) collective-permute-start(bf16[128,256]{1,0:T(8,128)(2,1)S(1)} %get-tuple-element.74), channel_id=1, source_target_pairs={{7,0},{6,1},{5,2},{4,3},{3,4},{2,5},{1,6},{0,7},{15,8},{14,9},{13,... | collective-permute-start | bytes 196616 | tf_op jit(solution)/shard_map/ppermute | solution.py:543
  (6 other events, 59.6 us)
Sparse Core Ops, SparseCore 0:
  84.3 124.4 all-reduce.1

commit v3 on v2

v3 whole, which is shorter than its diff:
```python
from functools import partial
import math

import jax
import jax.numpy as jnp
from jax import lax
from jax.experimental import pallas as pl
from jax.experimental.pallas import tpu as pltpu
from jax.sharding import PartitionSpec as P

HEAD = 64
LEAF = 128
BALL = 512
CMP = 256
PAIR = 2 * HEAD
HIDE = 512
CHUNK = 256
MIB = 1 << 20
LATER = 40 * MIB
F32 = jnp.float32
BF16 = jnp.bfloat16
SCALE = HEAD ** (-0.5) * math.log2(math.e)

ANY = pl.BlockSpec(memory_space=pl.ANY)
VMEM = pl.BlockSpec(memory_space=pltpu.VMEM)
SMEM = pl.BlockSpec(memory_space=pltpu.SMEM)


def norm(values, gain):
    wide = values.astype(F32)
    return wide * lax.rsqrt(jnp.mean(wide * wide, axis=-1, keepdims=True) + 1e-06) * gain


def gelu(x):
    c = math.sqrt(2.0 / math.pi)
    t = jnp.tanh(x * (c + (c * 0.044715) * (x * x)))
    return x * (0.5 + 0.5 * t)


def dot(a, b):
    return jnp.dot(a, b, preferred_element_type=F32)


def dot_t(a, b):
    return lax.dot_general(a, b, (((1,), (1,)), ((), ())), preferred_element_type=F32)


def aligned(index, size):
    return pl.ds(pl.multiple_of(index * size, size), size)


def only_head(pair, half):
    lane = lax.broadcasted_iota(jnp.int32, pair.shape, 1)
    return jnp.where((lane >= HEAD) == bool(half), pair, jnp.zeros_like(pair))


def pair_scores(queries, keys):
    both = jnp.concatenate([only_head(queries, 0), only_head(queries, 1)], axis=0)
    return dot_t(both, keys)


def lay_values(out, values):
    keys = values.shape[0]
    ones = jnp.ones_like(values)
    for half in range(2):
        rows = slice(half * keys, (half + 1) * keys)
        out[rows, :PAIR] = only_head(values, half)
        out[rows, PAIR:] = only_head(ones, half)


def weigh(scores, laid):
    rows = scores.shape[0] // 2
    parts = []
    for half in range(2):
        own = scores[half * rows : (half + 1) * rows]
        parts.append(jnp.exp2(own - jnp.max(own, axis=1, keepdims=True)).astype(BF16))
    mixed = dot(jnp.concatenate(parts, axis=1), laid)
    return mixed[:, :PAIR] / mixed[:, PAIR:]


def pipelined(items, first, second):
    held = first(items[0])
    for n, item in enumerate(items):
        now = held
        if n + 1 < len(items):
            held = first(items[n + 1])
        second(item, now)


def send_to(me, s, peers):
    return me ^ s if peers & (peers - 1) == 0 else (me + s) % peers


def got_from(me, s, peers):
    return me ^ s if peers & (peers - 1) == 0 else (me + peers - s) % peers


def start_all(copies):
    for copy in copies:
        copy.start()


def wait_all(copies):
    for copy in copies:
        copy.wait()


def feed_forward(y, gain2, gain3, up_s, down_s):
    inner = norm(y, gain2[...]).astype(BF16)
    total = y.astype(F32)
    for c in range(up_s.shape[1] // HIDE):
        cols = slice(c * HIDE, (c + 1) * HIDE)
        up = gelu(dot(inner, up_s[:, cols])).astype(BF16)
        total = total + dot(up, down_s[cols, :])
    z = total.astype(BF16)
    return z, norm(z, gain3[...]).astype(BF16)


def layer_one_kernel(peers, cap, *refs):
    pick_ref, ids, gain1, gain2, gain3, points, w_in, w_out, w_up, w_down = refs[:10]
    z_out, h_out, pool_out = refs[10:13]
    sends, refs = refs[13 : 13 + peers], refs[13 + peers :]
    x_s, in_s, wo_s, up_s, down_s, q_s, k_s, v_s, bias_s, mix_s, y_s, z_s, h_s, sem, send_sem = refs
    me = lax.axis_index("pts").astype(jnp.int32)
    count, width = x_s.shape
    balls = count // BALL
    pairs = width // PAIR
    blocks = count // LEAF
    copies = [
        pltpu.make_async_copy(points, x_s, sem.at[0]),
        pltpu.make_async_copy(w_in, in_s, sem.at[1]),
        pltpu.make_async_copy(w_out, wo_s, sem.at[2]),
        pltpu.make_async_copy(w_up, up_s, sem.at[3]),
        pltpu.make_async_copy(w_down, down_s, sem.at[4]),
    ]
    start_all(copies)
    for b in range(balls):
        across = jnp.broadcast_to(ids[b : b + 1, :], (LEAF, BALL)).astype(F32)
        down = across.T
        for c in range(BALL // LEAF):
            cols = slice(c * LEAF, (c + 1) * LEAF)
            bias_s[b, :, cols] = jnp.where(down == across[:1, cols], 0.0, -1e30)
    copies[0].wait()
    for b in range(balls):
        rows = slice(b * BALL, (b + 1) * BALL)
        h1 = norm(x_s[rows, :], gain1[...]).astype(BF16)
        if b == 0:
            copies[1].wait()
        q_s[rows, :] = (dot(h1, in_s[:, :width]) * SCALE).astype(BF16)
        k_s[rows, :] = dot(h1, in_s[:, width : 2 * width]).astype(BF16)
        values = dot(h1, in_s[:, 2 * width :]).astype(BF16)
        for g in range(pairs):
            lay_values(v_s.at[b * pairs + g], values[:, g * PAIR : (g + 1) * PAIR])

    def scores(item):
        b, g, c = item
        cols = slice(g * PAIR, (g + 1) * PAIR)
        at = b * BALL + c * CHUNK
        return pair_scores(q_s[at : at + CHUNK, cols], k_s[b * BALL : (b + 1) * BALL, cols])

    def mix(item, got):
        b, g, c = item
        at = b * BALL + c * CHUNK
        bias = bias_s[b, c * CHUNK : (c + 1) * CHUNK, :]
        out = weigh(got + jnp.concatenate([bias, bias], axis=0), v_s[b * pairs + g])
        mix_s[at : at + CHUNK, g * PAIR : (g + 1) * PAIR] = out.astype(BF16)

    pipelined(
        [(b, g, c) for b in range(balls) for g in range(pairs) for c in range(BALL // CHUNK)], scores, mix
    )
    copies[2].wait()
    for b in range(balls):
        rows = slice(b * BALL, (b + 1) * BALL)
        y_s[rows, :] = (x_s[rows, :].astype(F32) + dot(mix_s[rows, :], wo_s[...])).astype(BF16)
    copies[3].wait()
    copies[4].wait()
    outgoing = []
    for b in range(balls):
        rows = slice(b * BALL, (b + 1) * BALL)
        z, h3 = feed_forward(y_s[rows, :], gain2, gain3, up_s, down_s)
        z_s[rows, :] = z
        h_s[rows, :] = h3
        wide = h3.astype(F32)
        for c in range(BALL // CMP):
            part = jnp.sum(wide[c * CMP : (c + 1) * CMP], axis=0, keepdims=True) * CMP ** (-0.5)
            at = b * (BALL // CMP) + c
            pool_out[at : at + 1, :] = part.astype(BF16)
        at = pl.ds(b * BALL, BALL)
        for n, (source, there) in enumerate(((z_s, z_out), (h_s, h_out))):
            copy = pltpu.make_async_copy(source.at[at, :], there.at[at, :], sem.at[5 + 2 * b + n])
            copy.start()
            outgoing.append(copy)
    for s in range(peers - 1, -1, -1):
        for c in range(cap):
            slot = send_to(me, s, peers) * cap + c
            block = jnp.minimum(pick_ref[0, slot], blocks - 1)
            there = sends[s].at[pl.ds(c * LEAF, LEAF), :]
            copy = pltpu.make_async_copy(h_s.at[aligned(block, LEAF), :], there, send_sem.at[s * cap + c])
            copy.start()
            outgoing.append(copy)
    wait_all(outgoing)


def layer_one(peers, cap, pick, ids, gains, points, weights):
    count, width = points.shape
    hidden = weights[2].shape[1]
    whole = jax.ShapeDtypeStruct((count, width), BF16)
    block = jax.ShapeDtypeStruct((cap * LEAF, width), BF16)
    pool = jax.ShapeDtypeStruct((count // CMP, width), BF16)
    balls = count // BALL
    return pl.pallas_call(
        partial(layer_one_kernel, peers, cap),
        out_shape=[whole, whole, pool] + [block] * peers,
        in_specs=[SMEM] + [VMEM] * 4 + [ANY] * 5,
        out_specs=[ANY, ANY, VMEM] + [ANY] * peers,
        scratch_shapes=[
            pltpu.VMEM((count, width), BF16),
            pltpu.VMEM((width, 3 * width), BF16),
            pltpu.VMEM((width, width), BF16),
            pltpu.VMEM((width, hidden), BF16),
            pltpu.VMEM((hidden, width), BF16),
            pltpu.VMEM((count, width), BF16),
            pltpu.VMEM((count, width), BF16),
            pltpu.VMEM((balls * width // PAIR, 2 * BALL, 2 * PAIR), BF16),
            pltpu.VMEM((balls, BALL, BALL), F32),
            pltpu.VMEM((count, width), BF16),
            pltpu.VMEM((count, width), BF16),
            pltpu.VMEM((count, width), BF16),
            pltpu.VMEM((count, width), BF16),
            pltpu.SemaphoreType.DMA((5 + 2 * balls,)),
            pltpu.SemaphoreType.DMA((peers * cap,)),
        ],
        compiler_params=pltpu.CompilerParams(vmem_limit_bytes=60 * MIB),
        cost_estimate=pl.CostEstimate(
            flops=count * width * (8 * width + 4 * hidden + 16 * BALL),
            bytes_accessed=10 * MIB,
            transcendentals=count * BALL * width // HEAD,
        ),
        name="layer_one",
    )(pick, ids, *gains, points, *weights)


def place_of(recv_ref, slot, blocks):
    place, found = jnp.int32(0), jnp.int32(0)
    for j in range(blocks):
        hit = (recv_ref[0, j] == slot).astype(jnp.int32)
        place = place + j * hit
        found = found + hit
    return place, found > 0


def layer_two_kernel(peers, cap, blocks, start, columns, *refs):
    recv_ref = refs[0]
    arrived = refs[1 : 1 + peers][::-1]
    w_in = refs[1 + peers]
    outs = refs[2 + peers : 2 + 2 * peers]
    h_s, w_s, q_s, k_s, v_s, a_s, sem, block_sem = refs[2 + 2 * peers :]
    width = h_s.shape[1]
    pairs = columns // PAIR
    me = lax.axis_index("pts").astype(jnp.int32)
    balls = blocks * LEAF // BALL
    copies = []
    for i in range(3):
        cols = pl.ds(i * width + start, columns)
        copies.append(
            pltpu.make_async_copy(w_in.at[:, cols], w_s.at[:, pl.ds(i * columns, columns)], sem.at[i])
        )
    start_all(copies)
    places, moves = [], []
    for s in range(peers):
        for c in range(cap):
            place, found = place_of(recv_ref, got_from(me, s, peers) * cap + c, blocks)
            at = pl.ds(c * LEAF, LEAF)
            move = pltpu.make_async_copy(
                arrived[s].at[at, :], h_s.at[aligned(place, LEAF), :], block_sem.at[s * cap + c]
            )
            places.append(place)
            moves.append((found, move))
            pl.when(found)(move.start)
    wait_all(copies)
    for found, move in moves:
        pl.when(found)(move.wait)
    for b in range(balls):
        rows = slice(b * BALL, (b + 1) * BALL)
        h = h_s[rows, :]
        q_s[rows, :] = (dot(h, w_s[:, :columns]) * SCALE).astype(BF16)
        k_s[rows, :] = dot(h, w_s[:, columns : 2 * columns]).astype(BF16)
        values = dot(h, w_s[:, 2 * columns :]).astype(BF16)
        for g in range(pairs):
            lay_values(v_s.at[b * pairs + g], values[:, g * PAIR : (g + 1) * PAIR])

    def scores(item):
        b, g, c = item
        cols = slice(g * PAIR, (g + 1) * PAIR)
        at = b * BALL + c * CHUNK
        return pair_scores(q_s[at : at + CHUNK, cols], k_s[b * BALL : (b + 1) * BALL, cols])

    def mix(item, got):
        b, g, c = item
        at = b * BALL + c * CHUNK
        a_s[at : at + CHUNK, g * PAIR : (g + 1) * PAIR] = weigh(got, v_s[b * pairs + g]).astype(BF16)

    pipelined(
        [(b, g, c) for b in range(balls) for g in range(pairs) for c in range(BALL // CHUNK)], scores, mix
    )
    outgoing = []
    for s in range(peers):
        for c in range(cap):
            n = s * cap + c
            at = pl.ds(c * LEAF, LEAF)
            outgoing.append(
                pltpu.make_async_copy(a_s.at[aligned(places[n], LEAF), :], outs[s].at[at, :], block_sem.at[n])
            )
    start_all(outgoing)
    wait_all(outgoing)


def layer_two(peers, cap, start, columns, recv, arrived, w_in):
    blocks = recv.shape[1]
    width = w_in.shape[0]
    pairs = columns // PAIR
    rows = blocks * LEAF
    block = jax.ShapeDtypeStruct((cap * LEAF, columns), BF16)
    return pl.pallas_call(
        partial(layer_two_kernel, peers, cap, blocks, start, columns),
        out_shape=[block] * peers,
        in_specs=[SMEM] + [ANY] * (peers + 1),
        out_specs=[ANY] * peers,
        scratch_shapes=[
            pltpu.VMEM((rows, width), BF16),
            pltpu.VMEM((width, 3 * columns), BF16),
            pltpu.VMEM((rows, columns), BF16),
            pltpu.VMEM((rows, columns), BF16),
            pltpu.VMEM((rows // BALL * pairs, 2 * BALL, 2 * PAIR), BF16),
            pltpu.VMEM((rows, columns), BF16),
            pltpu.SemaphoreType.DMA((3,)),
            pltpu.SemaphoreType.DMA((peers * cap,)),
        ],
        compiler_params=pltpu.CompilerParams(vmem_limit_bytes=LATER),
        cost_estimate=pl.CostEstimate(
            flops=rows * columns * (6 * width + 16 * BALL),
            bytes_accessed=4 * MIB,
            transcendentals=rows * BALL * columns // HEAD,
        ),
        name=f"layer_two_{start}",
    )(recv, *arrived[::-1], w_in)


def compressed_kernel(h, z, pool_a, pool_b, w_comp, w_in, w_out, out, *scratch):
    h_s, z_s, p_s, wc_s, wq_s, wo_s, q_s, ck_s, cv_s, a_s, o_s, sem, out_sem = scratch
    rows, width = h_s.shape
    pairs = width // PAIR
    near = pool_a.shape[0]
    copies = [
        pltpu.make_async_copy(pool_a, p_s.at[pl.ds(0, near), :], sem.at[0]),
        pltpu.make_async_copy(pool_b, p_s.at[pl.ds(near, pool_b.shape[0]), :], sem.at[1]),
        pltpu.make_async_copy(w_comp, wc_s, sem.at[2]),
        pltpu.make_async_copy(w_in.at[:, pl.ds(0, width)], wq_s, sem.at[3]),
        pltpu.make_async_copy(h, h_s, sem.at[4]),
        pltpu.make_async_copy(w_out, wo_s, sem.at[5]),
        pltpu.make_async_copy(z, z_s, sem.at[6]),
    ]
    start_all(copies)
    wait_all(copies[:3])
    far = dot(p_s[...], wc_s[...]).astype(BF16)
    ck_s[...] = far[:, :width]
    for g in range(pairs):
        lay_values(cv_s.at[g], far[:, width + g * PAIR : width + (g + 1) * PAIR])
    wait_all(copies[3:5])
    q_s[...] = (dot(h_s[...], wq_s[...]) * SCALE).astype(BF16)

    def scores(item):
        g, c = item
        cols = slice(g * PAIR, (g + 1) * PAIR)
        return pair_scores(q_s[c * CHUNK : (c + 1) * CHUNK, cols], ck_s[:, cols])

    def mix(item, got):
        g, c = item
        a_s[c * CHUNK : (c + 1) * CHUNK, g * PAIR : (g + 1) * PAIR] = weigh(got, cv_s[g]).astype(BF16)

    pipelined([(g, c) for c in range(rows // CHUNK) for g in range(pairs)], scores, mix)
    wait_all(copies[5:])
    outgoing = []
    for c in range(rows // CHUNK):
        at = slice(c * CHUNK, (c + 1) * CHUNK)
        o_s[at, :] = z_s[at, :].astype(F32) + dot(a_s[at, :], wo_s[...])
        there = pl.ds(c * CHUNK, CHUNK)
        copy = pltpu.make_async_copy(o_s.at[there, :], out.at[there, :], out_sem.at[c])
        copy.start()
        outgoing.append(copy)
    wait_all(outgoing)


def compressed(h, z, pooled, w_comp, w_in, w_out):
    rows, width = h.shape
    comp = sum(p.shape[0] for p in pooled)
    return pl.pallas_call(
        compressed_kernel,
        out_shape=jax.ShapeDtypeStruct((rows, width), F32),
        in_specs=[ANY] * 7,
        out_specs=ANY,
        scratch_shapes=[
            pltpu.VMEM((rows, width), BF16),
            pltpu.VMEM((rows, width), BF16),
            pltpu.VMEM((comp, width), BF16),
            pltpu.VMEM((width, 2 * width), BF16),
            pltpu.VMEM((width, width), BF16),
            pltpu.VMEM((width, width), BF16),
            pltpu.VMEM((rows, width), BF16),
            pltpu.VMEM((comp, width), BF16),
            pltpu.VMEM((width // PAIR, 2 * comp, 2 * PAIR), BF16),
            pltpu.VMEM((rows, width), BF16),
            pltpu.VMEM((rows, width), F32),
            pltpu.SemaphoreType.DMA((7,)),
            pltpu.SemaphoreType.DMA((rows // CHUNK,)),
        ],
        compiler_params=pltpu.CompilerParams(vmem_limit_bytes=60 * MIB),
        cost_estimate=pl.CostEstimate(
            flops=rows * width * (4 * width + 16 * comp),
            bytes_accessed=8 * MIB,
            transcendentals=rows * comp * width // HEAD,
        ),
        name="compressed",
    )(h, z, *pooled, w_comp, w_in, w_out)


def final_kernel(peers, cap, bounds, pick_ref, *refs):
    parts = len(bounds)
    back = [refs[p * peers : (p + 1) * peers][::-1] for p in range(parts)]
    w_out, base, out, w_s, b_s, m_s, o_s, sem, block_sem, out_sem = refs[parts * peers :]
    blocks = b_s.shape[0] // LEAF
    me = lax.axis_index("pts").astype(jnp.int32)
    copies = [
        pltpu.make_async_copy(w_out, w_s, sem.at[0]),
        pltpu.make_async_copy(base, b_s, sem.at[1]),
    ]
    start_all(copies)
    moves = []
    for p, (start, columns) in enumerate(bounds):
        for s in range(peers):
            for c in range(cap):
                block = pick_ref[0, send_to(me, s, peers) * cap + c]
                found = block < blocks
                at = pl.ds(c * LEAF, LEAF)
                place = aligned(jnp.minimum(block, blocks - 1), LEAF)
                move = pltpu.make_async_copy(
                    back[p][s].at[at, :],
                    m_s.at[place, pl.ds(start, columns)],
                    block_sem.at[(p * peers + s) * cap + c],
                )
                moves.append((found, move))
                pl.when(found)(move.start)
    wait_all(copies)
    for found, move in moves:
        pl.when(found)(move.wait)
    outgoing = []
    for b in range(b_s.shape[0] // CHUNK):
        rows = slice(b * CHUNK, (b + 1) * CHUNK)
        o_s[rows, :] = (b_s[rows, :] + dot(m_s[rows, :], w_s[...])).astype(BF16)
        at = pl.ds(b * CHUNK, CHUNK)
        copy = pltpu.make_async_copy(o_s.at[at, :], out.at[at, :], out_sem.at[b])
        copy.start()
        outgoing.append(copy)
    wait_all(outgoing)


def final(peers, cap, bounds, pick, back, w_out, base):
    rows, width = base.shape
    return pl.pallas_call(
        partial(final_kernel, peers, cap, bounds),
        out_shape=jax.ShapeDtypeStruct((rows, width), BF16),
        in_specs=[SMEM] + [ANY] * (peers * len(bounds) + 2),
        out_specs=ANY,
        scratch_shapes=[
            pltpu.VMEM((width, width), BF16),
            pltpu.VMEM((rows, width), F32),
            pltpu.VMEM((rows, width), BF16),
            pltpu.VMEM((rows, width), BF16),
            pltpu.SemaphoreType.DMA((2,)),
            pltpu.SemaphoreType.DMA((len(bounds) * peers * cap,)),
            pltpu.SemaphoreType.DMA((rows // CHUNK,)),
        ],
        compiler_params=pltpu.CompilerParams(vmem_limit_bytes=LATER),
        cost_estimate=pl.CostEstimate(
            flops=2 * rows * width * width, bytes_accessed=4 * MIB, transcendentals=0
        ),
        name="last_product",
    )(pick, *back, w_out, base)


def xor_pairs(size, s):
    return [(i, i ^ s) for i in range(size)]


def gather_all(rows, axes):
    (grp, groups), (pts, peers) = axes
    if groups & (groups - 1) or peers & (peers - 1) or peers == 1:
        rows = lax.all_gather(rows, (grp, pts), axis=0, tiled=True)
        return rows[: rows.shape[0] // 2], rows[rows.shape[0] // 2 :]
    for axis, shifts in ((grp, range(1, groups)), (pts, range(2, peers, 2))):
        pieces = [rows] + [lax.ppermute(rows, axis, xor_pairs(axes[axis == pts][1], s)) for s in shifts]
        rows = lax.optimization_barrier(jnp.concatenate(pieces))
    return rows, lax.ppermute(rows, pts, xor_pairs(peers, 1))


def shards(
    axes,
    points,
    ball_ids,
    send_pick,
    recv_from,
    gain_one,
    attn_in_one,
    attn_out_one,
    gain_two,
    mlp_up,
    mlp_down,
    gain_three,
    compress_proj,
    attn_in_two,
    attn_out_two,
):
    peers = axes[1][1]
    cap = send_pick.shape[1] // peers
    width = points.shape[1]
    gains = tuple(g.reshape(1, -1) for g in (gain_one, gain_two, gain_three))
    weights = (attn_in_one, attn_out_one, mlp_up, mlp_down)

    def travel(blocks, s, home):
        if s == 0:
            return blocks
        pattern = [(i, send_to(i, s, peers)) for i in range(peers)]
        if home:
            pattern = [(b, a) for a, b in pattern]
        return lax.ppermute(blocks, "pts", pattern)

    z, h, pool, *sends = layer_one(peers, cap, send_pick, ball_ids, gains, points, weights)
    arrived = [travel(sends[s], s, False) for s in range(peers)]
    pool, far = lax.optimization_barrier((pool, arrived[: -3 : -1]))
    arrived[-2:] = far[::-1]
    pooled = gather_all(pool, axes)
    arrived, pooled = lax.optimization_barrier((arrived[::-1], pooled))
    bounds = [(0, width)]
    back = []
    for start, columns in bounds:
        mixed = layer_two(peers, cap, start, columns, recv_from, arrived[::-1], attn_in_two)
        back.extend(travel(mixed[s], s, True) for s in range(peers - 1, -1, -1))
    base = compressed(h, z, pooled, compress_proj, attn_in_two, attn_out_two)
    return final(peers, cap, bounds, send_pick, back, attn_out_two, base)


def solution(mesh):
    rows = P(("grp", "pts"), None)
    axes = (("grp", mesh.shape["grp"]), ("pts", mesh.shape["pts"]))
    return jax.shard_map(
        partial(shards, axes),
        mesh=mesh,
        in_specs=(rows,) * 4 + (P(),) * 10,
        out_specs=rows,
        check_vma=False,
    )
```

time: 226 us -> 102 us (0.45)
  waiting for transfers between devices: 131 us -> 18.8 us
  between operations: 16 us -> 0.31 us
  starting transfers between devices: 28.5 us -> 40.4 us
  Pallas kernels: 45.4 us -> 38.9 us
    psum x1 -> x0, waiting for transfers between devices: 115 us -> none  [shards(): pooled = lax.psum(placed, ('grp', 'pts'))]
    ppermute x0 -> x7, starting transfers between devices: none -> 9.08 us  [the longest x6 8.53 us: gather_all(): lax.ppermute(rows, axis, xor_pairs(axes[axis == pts][1], s))]
    pallas_call x2 -> x1, Pallas kernels: 23.4 us -> 18.7 us  [layer_one(): pl.pallas_call(partial(layer_one_kernel, peers, cap), out_shape=[whole, w...]
    pallas_call x2 -> x1, Pallas kernels: 13.7 us -> 10.8 us  [layer_two(): pl.pallas_call(partial(layer_two_kernel, peers, cap, blocks, start, colum...]
    ppermute x21 -> x14, waiting for transfers between devices: 16 us -> 18.8 us  [travel(): return lax.ppermute(blocks, 'pts', pattern)]
    ppermute x21 -> x14, starting transfers between devices: 28.5 us -> 31.3 us  [travel(): return lax.ppermute(blocks, 'pts', pattern)]
  transfers between devices with their start and end apart: 22 -> 21, of which waited for: 6 -> 8; matrix products, arithmetic and copies ran while one was open for 0% -> 1% of each run, Pallas kernels for 11% -> 6%
where the time goes in v3:
time: 102 us
  starting transfers between devices  40.4 us (40%)
  Pallas kernels  38.9 us (38%)
  waiting for transfers between devices  18.8 us (18%)
  local copies, waits for them, and re-layouts  2.53 us (2%)
    ppermute x14, starting transfers between devices, travel(): return lax.ppermute(blocks, 'pts', pattern)  31.3 us
    ppermute x14, waiting for transfers between devices, travel(): return lax.ppermute(blocks, 'pts', pattern)  18.8 us
    pallas_call x1, Pallas kernels, layer_one(): pl.pallas_call(partial(layer_one_kernel, peers, cap), out_shape=[whole, w...  18.7 us
    pallas_call x1, Pallas kernels, layer_two(): pl.pallas_call(partial(layer_two_kernel, peers, cap, blocks, start, colum...  10.8 us
    ppermute x6, starting transfers between devices, gather_all(): lax.ppermute(rows, axis, xor_pairs(axes[axis == pts][1], s))  8.53 us
    pallas_call x1, Pallas kernels, compressed(): pl.pallas_call(compressed_kernel, out_shape=jax.ShapeDtypeStruct((rows, w...  5.77 us
    pallas_call x1, Pallas kernels, final(): pl.pallas_call(partial(final_kernel, peers, cap, bounds), out_shape=jax.S...  3.69 us
    unnamed x16, local copies, waits for them, and re-layouts  2.53 us
  transfers between devices with their start and end apart: 21, of which 8 were waited for; matrix products, arithmetic and copies ran while one was open for 1% of the time, Pallas kernels for 6%

profile of v3, /device:TPU:0, one launch (start us, length us, event | category | flops | bytes accessed | tf_op | source)
XLA Modules:
  0.0 101.7 jit_solution(17515128814069163686)
XLA Ops:
  0.0 18.7 %layer_one.1 = (bf16[1024,512]{1,0:T(8,128)(2,1)}, bf16[1024,512]{1,0:T(8,128)(2,1)}, bf16[4,512]{1,0:T(4,128)(2,1)}, bf16[128,512]{1,0:T(8,128)(2,1)}, bf16[128...) custom-call(s32[1,8]{1,0:T(1,128)} %pick_ref.1, ...), custom_call_target="tpu_custom_call" | custom-call | flops 10737418240 | bytes 10485760 | tf_op jit(solution)/shard_map/layer_one/pallas_call | solution.py:211
  18.7 4.6 %collective-permute-start = (bf16[128,512]{1,0:T(8,128)(2,1)}, bf16[128,512]{1,0:T(8,128)(2,1)S(1)}, u32[]{:S(2)}, u32[]{:S(2)}) collective-permute-start(bf16[128,512]{1,0:T(8,128)(2,1)} %get-tuple-element.38), channel_id=1, source_target_pairs={{0,7},{1,6},{2,5},{3,4},{4,3},{5,2},{6,1},{7,0},{8,15},{9,14},{10,... | collective-permute-start | bytes 393224 | tf_op jit(solution)/shard_map/ppermute | solution.py:535
  23.9 3.6 %collective-permute-done.refs_1_ = bf16[128,512]{1,0:T(8,128)(2,1)S(1)} collective-permute-done((bf16[128,512]{1,0:T(8,128)(2,1)}, bf16[128,512]{1,0:T(8,128)(2,1)S(1)}, u32[]{:S(2)}, u32[]{:S(2)}) %collective-permute-start) | collective-permute-done | bytes 131104 | tf_op jit(solution)/shard_map/ppermute | solution.py:535
  27.5 3.9 %collective-permute-done.1.refs_2_ = bf16[128,512]{1,0:T(8,128)(2,1)S(1)} collective-permute-done((bf16[128,512]{1,0:T(8,128)(2,1)}, bf16[128,512]{1,0:T(8,128)(2,1)S(1)}, u32[]{:S(2)}, u32[]{:S(2)}) %collective-permute-start.1) | collective-permute-done | bytes 131104 | tf_op jit(solution)/shard_map/ppermute | solution.py:535
  31.4 2.4 %collective-permute-start.9 = (bf16[4,512]{1,0:T(4,128)(2,1)}, bf16[4,512]{1,0:T(4,128)(2,1)S(1)}, u32[]{:S(2)}, u32[]{:S(2)}) collective-permute-start(bf16[4,512]{1,0:T(4,128)(2,1)} %get-tuple-element.48), channel_id=1, source_target_pairs={{0,24},{8,16},{16,8},{24,0},{1,25},{9,17},{17,9},{25,1},{2,26},{10... | collective-permute-start | bytes 12296 | tf_op jit(solution)/shard_map/ppermute | solution.py:501
  34.9 4.7 %collective-permute-start.2 = (bf16[128,512]{1,0:T(8,128)(2,1)}, bf16[128,512]{1,0:T(8,128)(2,1)S(1)}, u32[]{:S(2)}, u32[]{:S(2)}) collective-permute-start(bf16[128,512]{1,0:T(8,128)(2,1)} %get-tuple-element.42), channel_id=1, source_target_pairs={{0,5},{1,4},{2,7},{3,6},{4,1},{5,0},{6,3},{7,2},{8,13},{9,12},{10,... | collective-permute-start | bytes 393224 | tf_op jit(solution)/shard_map/ppermute | solution.py:535
  40.3 1.8 %collective-permute-start.12 = (bf16[16,512]{1,0:T(8,128)(2,1)S(1)}, bf16[16,512]{1,0:T(8,128)(2,1)S(1)}, u32[]{:S(2)}, u32[]{:S(2)}) collective-permute-start(bf16[16,512]{1,0:T(8,128)(2,1)S(1)} %pad_maximum_fusion.1), channel_id=1, source_target_pairs={{0,6},{1,7},{2,4},{3,5},{4,2},{5,3},{6,0},{7,1},{8,14},{9,15},{10,... | collective-permute-start | bytes 49160 | tf_op jit(solution)/shard_map/ppermute | solution.py:501
  42.0 3.1 %collective-permute-start.11 = (bf16[16,512]{1,0:T(8,128)(2,1)S(1)}, bf16[16,512]{1,0:T(8,128)(2,1)S(1)}, u32[]{:S(2)}, u32[]{:S(2)}) collective-permute-start(bf16[16,512]{1,0:T(8,128)(2,1)S(1)} %pad_maximum_fusion.1), channel_id=1, source_target_pairs={{0,4},{1,5},{2,6},{3,7},{4,0},{5,1},{6,2},{7,3},{8,12},{9,13},{10,... | collective-permute-start | bytes 49160 | tf_op jit(solution)/shard_map/ppermute | solution.py:501
  45.3 2.9 %collective-permute-start.3 = (bf16[128,512]{1,0:T(8,128)(2,1)}, bf16[128,512]{1,0:T(8,128)(2,1)S(1)}, u32[]{:S(2)}, u32[]{:S(2)}) collective-permute-start(bf16[128,512]{1,0:T(8,128)(2,1)} %get-tuple-element.43), channel_id=1, source_target_pairs={{0,4},{1,5},{2,6},{3,7},{4,0},{5,1},{6,2},{7,3},{8,12},{9,13},{10,... | collective-permute-start | bytes 393224 | tf_op jit(solution)/shard_map/ppermute | solution.py:535
  48.3 1.9 %collective-permute-start.5 = (bf16[128,512]{1,0:T(8,128)(2,1)}, bf16[128,512]{1,0:T(8,128)(2,1)S(1)}, u32[]{:S(2)}, u32[]{:S(2)}) collective-permute-start(bf16[128,512]{1,0:T(8,128)(2,1)} %get-tuple-element.45), channel_id=1, source_target_pairs={{0,2},{1,3},{2,0},{3,1},{4,6},{5,7},{6,4},{7,5},{8,10},{9,11},{10,... | collective-permute-start | bytes 393224 | tf_op jit(solution)/shard_map/ppermute | solution.py:535
  50.7 3.7 %collective-permute-done.3.refs_4_ = bf16[128,512]{1,0:T(8,128)(2,1)S(1)} collective-permute-done((bf16[128,512]{1,0:T(8,128)(2,1)}, bf16[128,512]{1,0:T(8,128)(2,1)S(1)}, u32[]{:S(2)}, u32[]{:S(2)}) %collective-permute-start.3) | collective-permute-done | bytes 131104 | tf_op jit(solution)/shard_map/ppermute | solution.py:535
  54.4 1.5 %collective-permute-done.4.refs_5_ = bf16[128,512]{1,0:T(8,128)(2,1)S(1)} collective-permute-done((bf16[128,512]{1,0:T(8,128)(2,1)}, bf16[128,512]{1,0:T(8,128)(2,1)S(1)}, u32[]{:S(2)}, u32[]{:S(2)}) %collective-permute-start.4) | collective-permute-done | bytes 131104 | tf_op jit(solution)/shard_map/ppermute | solution.py:535
  55.9 1.9 %collective-permute-done.5.refs_6_ = bf16[128,512]{1,0:T(8,128)(2,1)S(1)} collective-permute-done((bf16[128,512]{1,0:T(8,128)(2,1)}, bf16[128,512]{1,0:T(8,128)(2,1)S(1)}, u32[]{:S(2)}, u32[]{:S(2)}) %collective-permute-start.5) | collective-permute-done | bytes 131104 | tf_op jit(solution)/shard_map/ppermute | solution.py:535
  58.8 10.8 %layer_two_0.1 = (bf16[128,512]{1,0:T(8,128)(2,1)S(1)}, bf16[128,512]{1,0:T(8,128)(2,1)S(1)}, bf16[128,512]{1,0:T(8,128)(2,1)S(1)}, bf16[128,512]{1,0:T(8,128)(2...) custom-call(s32[1,8]{1,0:T(1,128)S(1)} %copy-done.4, ...), custom_call_target="tpu_custom_call" | custom-call | flops 5905580032 | bytes 4194304 | tf_op jit(solution)/shard_map/layer_two_0/pallas_call | solution.py:324
  69.6 1.4 %collective-permute-start.14 = (bf16[128,512]{1,0:T(8,128)(2,1)S(1)}, bf16[128,512]{1,0:T(8,128)(2,1)S(1)}, u32[]{:S(2)}, u32[]{:S(2)}) collective-permute-start(bf16[128,512]{1,0:T(8,128)(2,1)S(1)} %get-tuple-element.57), channel_id=1, source_target_pairs={{7,0},{6,1},{5,2},{4,3},{3,4},{2,5},{1,6},{0,7},{15,8},{14,9},{13,... | collective-permute-start | bytes 393224 | tf_op jit(solution)/shard_map/ppermute | solution.py:535
  71.0 2.4 %collective-permute-start.15 = (bf16[128,512]{1,0:T(8,128)(2,1)S(1)}, bf16[128,512]{1,0:T(8,128)(2,1)S(1)}, u32[]{:S(2)}, u32[]{:S(2)}) collective-permute-start(bf16[128,512]{1,0:T(8,128)(2,1)S(1)} %get-tuple-element.58), channel_id=1, source_target_pairs={{6,0},{7,1},{4,2},{5,3},{2,4},{3,5},{0,6},{1,7},{14,8},{15,9},{12,... | collective-permute-start | bytes 393224 | tf_op jit(solution)/shard_map/ppermute | solution.py:535
  73.4 2.5 %collective-permute-start.17 = (bf16[128,512]{1,0:T(8,128)(2,1)S(1)}, bf16[128,512]{1,0:T(8,128)(2,1)S(1)}, u32[]{:S(2)}, u32[]{:S(2)}) collective-permute-start(bf16[128,512]{1,0:T(8,128)(2,1)S(1)} %get-tuple-element.60), channel_id=1, source_target_pairs={{4,0},{5,1},{6,2},{7,3},{0,4},{1,5},{2,6},{3,7},{12,8},{13,9},{14,... | collective-permute-start | bytes 393224 | tf_op jit(solution)/shard_map/ppermute | solution.py:535
  75.9 1.1 %collective-permute-done.14.refs_0_ = bf16[128,512]{1,0:T(8,128)(2,1)S(1)} collective-permute-done((bf16[128,512]{1,0:T(8,128)(2,1)S(1)}, bf16[128,512]{1,0:T(8,128)(2,1)S(1)}, u32[]{:S(2)}, u32[]{:S(2)}) %collective-permute-start.14) | collective-permute-done | bytes 131104 | tf_op jit(solution)/shard_map/ppermute | solution.py:535
  77.0 10.4 %collective-permute-start.19 = (bf16[128,512]{1,0:T(8,128)(2,1)S(1)}, bf16[128,512]{1,0:T(8,128)(2,1)S(1)}, u32[]{:S(2)}, u32[]{:S(2)}) collective-permute-start(bf16[128,512]{1,0:T(8,128)(2,1)S(1)} %get-tuple-element.62), channel_id=1, source_target_pairs={{2,0},{3,1},{0,2},{1,3},{6,4},{7,5},{4,6},{5,7},{10,8},{11,9},{8,1... | collective-permute-start | bytes 393224 | tf_op jit(solution)/shard_map/ppermute | solution.py:535
  87.4 5.8 %compressed.1.refs_9_ = f32[1024,512]{1,0:T(8,128)} custom-call(bf16[1024,512]{1,0:T(8,128)(2,1)} %get-tuple-element.65.h, bf16[1024,512]{1,0:T(8,128)(2,1)} %get-tuple-element.66.z, bf16[64,512]{1,0:T(8,128)(2,1)} %copy-done.6, bf16[64,512]{1,0:T(8,128)(2,1)} %copy-done.7, bf16[512,1024]{1,0:T(8,128)(2,1)} %w_comp.1, bf16[512,1536]{1,0:T(8,128)(2,1)} %w_in.1, ...), custom_call_target="tpu_custom_call" | custom-call | flops 2147483648 | bytes 8388608 | tf_op jit(solution)/shard_map/compressed/pallas_call | solution.py:397
  93.2 1.6 %collective-permute-done.17.refs_3_ = bf16[128,512]{1,0:T(8,128)(2,1)S(1)} collective-permute-done((bf16[128,512]{1,0:T(8,128)(2,1)S(1)}, bf16[128,512]{1,0:T(8,128)(2,1)S(1)}, u32[]{:S(2)}, u32[]{:S(2)}) %collective-permute-start.17) | collective-permute-done | bytes 131104 | tf_op jit(solution)/shard_map/ppermute | solution.py:535
  94.8 1.4 %collective-permute-done.19.refs_5_ = bf16[128,512]{1,0:T(8,128)(2,1)S(1)} collective-permute-done((bf16[128,512]{1,0:T(8,128)(2,1)S(1)}, bf16[128,512]{1,0:T(8,128)(2,1)S(1)}, u32[]{:S(2)}, u32[]{:S(2)}) %collective-permute-start.19) | collective-permute-done | bytes 131104 | tf_op jit(solution)/shard_map/ppermute | solution.py:535
  96.2 1.6 %copy-done = f32[1024,512]{1,0:T(8,128)S(1)} copy-done((f32[1024,512]{1,0:T(8,128)S(1)}, f32[1024,512]{1,0:T(8,128)}, u32[]{:S(2)}) %copy-start) | copy-done | bytes 2097176
  97.8 3.7 %last_product.1 = bf16[1024,512]{1,0:T(8,128)(2,1)} custom-call(s32[1,8]{1,0:T(1,128)S(1)} %copy-done.2, bf16[128,512]{1,0:T(8,128)(2,1)S(1)} %collective-permute-done.14.refs_0_, bf16[128,512]{1,0:T(8,128)(2,1)S(1)} %collective-permute-done.15.refs_1_, bf16[128,512]{1,0:T(8,128)(2,1)S(1)} %collective-permute-done.16.refs_2_, ...), custom_call_target="tpu_custom_call" | custom-call | flops 536870912 | bytes 4194304 | tf_op jit(solution)/shard_map/last_product/pallas_call | solution.py:469
  (40 shorter events, 4.1 us)
Async XLA Ops:
  0.0 57.9 %copy-start.3 = (bf16[512,1536]{1,0:T(8,128)(2,1)S(1)}, bf16[512,1536]{1,0:T(8,128)(2,1)}, u32[]{:S(2)}) copy-start(bf16[512,1536]{1,0:T(8,128)(2,1)} %w_in.1) | copy-start | bytes 4718596
  0.0 57.9 %copy-start.4 = (s32[1,8]{1,0:T(1,128)S(1)}, s32[1,8]{1,0:T(1,128)}, u32[]{:S(2)}) copy-start(s32[1,8]{1,0:T(1,128)} %refs_0_.3) | copy-start | bytes 100
  18.7 8.8 %collective-permute-start = (bf16[128,512]{1,0:T(8,128)(2,1)}, bf16[128,512]{1,0:T(8,128)(2,1)S(1)}, u32[]{:S(2)}, u32[]{:S(2)}) collective-permute-start(bf16[128,512]{1,0:T(8,128)(2,1)} %get-tuple-element.38), channel_id=1, source_target_pairs={{0,7},{1,6},{2,5},{3,4},{4,3},{5,2},{6,1},{7,0},{8,15},{9,14},{10,... | collective-permute-start | bytes 393224 | tf_op jit(solution)/shard_map/ppermute | solution.py:535
  23.2 8.2 %collective-permute-start.1 = (bf16[128,512]{1,0:T(8,128)(2,1)}, bf16[128,512]{1,0:T(8,128)(2,1)S(1)}, u32[]{:S(2)}, u32[]{:S(2)}) collective-permute-start(bf16[128,512]{1,0:T(8,128)(2,1)} %get-tuple-element.39), channel_id=1, source_target_pairs={{0,6},{1,7},{2,4},{3,5},{4,2},{5,3},{6,0},{7,1},{8,14},{9,15},{10,... | collective-permute-start | bytes 393224 | tf_op jit(solution)/shard_map/ppermute | solution.py:535
  31.4 8.1 %collective-permute-start.9 = (bf16[4,512]{1,0:T(4,128)(2,1)}, bf16[4,512]{1,0:T(4,128)(2,1)S(1)}, u32[]{:S(2)}, u32[]{:S(2)}) collective-permute-start(bf16[4,512]{1,0:T(4,128)(2,1)} %get-tuple-element.48), channel_id=1, source_target_pairs={{0,24},{8,16},{16,8},{24,0},{1,25},{9,17},{17,9},{25,1},{2,26},{10... | collective-permute-start | bytes 12296 | tf_op jit(solution)/shard_map/ppermute | solution.py:501
  33.8 5.7 %collective-permute-start.8 = (bf16[4,512]{1,0:T(4,128)(2,1)}, bf16[4,512]{1,0:T(4,128)(2,1)S(1)}, u32[]{:S(2)}, u32[]{:S(2)}) collective-permute-start(bf16[4,512]{1,0:T(4,128)(2,1)} %get-tuple-element.48), channel_id=1, source_target_pairs={{0,16},{8,24},{16,0},{24,8},{1,17},{9,25},{17,1},{25,9},{2,18},{10... | collective-permute-start | bytes 12296 | tf_op jit(solution)/shard_map/ppermute | solution.py:501
  34.3 5.3 %collective-permute-start.7 = (bf16[4,512]{1,0:T(4,128)(2,1)}, bf16[4,512]{1,0:T(4,128)(2,1)S(1)}, u32[]{:S(2)}, u32[]{:S(2)}) collective-permute-start(bf16[4,512]{1,0:T(4,128)(2,1)} %get-tuple-element.48), channel_id=1, source_target_pairs={{0,8},{8,0},{16,24},{24,16},{1,9},{9,1},{17,25},{25,17},{2,10},{10... | collective-permute-start | bytes 12296 | tf_op jit(solution)/shard_map/ppermute | solution.py:501
  34.9 15.3 %collective-permute-start.2 = (bf16[128,512]{1,0:T(8,128)(2,1)}, bf16[128,512]{1,0:T(8,128)(2,1)S(1)}, u32[]{:S(2)}, u32[]{:S(2)}) collective-permute-start(bf16[128,512]{1,0:T(8,128)(2,1)} %get-tuple-element.42), channel_id=1, source_target_pairs={{0,5},{1,4},{2,7},{3,6},{4,1},{5,0},{6,3},{7,2},{8,13},{9,12},{10,... | collective-permute-start | bytes 393224 | tf_op jit(solution)/shard_map/ppermute | solution.py:535
  40.3 8.0 %collective-permute-start.12 = (bf16[16,512]{1,0:T(8,128)(2,1)S(1)}, bf16[16,512]{1,0:T(8,128)(2,1)S(1)}, u32[]{:S(2)}, u32[]{:S(2)}) collective-permute-start(bf16[16,512]{1,0:T(8,128)(2,1)S(1)} %pad_maximum_fusion.1), channel_id=1, source_target_pairs={{0,6},{1,7},{2,4},{3,5},{4,2},{5,3},{6,0},{7,1},{8,14},{9,15},{10,... | collective-permute-start | bytes 49160 | tf_op jit(solution)/shard_map/ppermute | solution.py:501
  42.0 6.2 %collective-permute-start.11 = (bf16[16,512]{1,0:T(8,128)(2,1)S(1)}, bf16[16,512]{1,0:T(8,128)(2,1)S(1)}, u32[]{:S(2)}, u32[]{:S(2)}) collective-permute-start(bf16[16,512]{1,0:T(8,128)(2,1)S(1)} %pad_maximum_fusion.1), channel_id=1, source_target_pairs={{0,4},{1,5},{2,6},{3,7},{4,0},{5,1},{6,2},{7,3},{8,12},{9,13},{10,... | collective-permute-start | bytes 49160 | tf_op jit(solution)/shard_map/ppermute | solution.py:501
  45.2 5.0 %collective-permute-start.10 = (bf16[16,512]{1,0:T(8,128)(2,1)S(1)}, bf16[16,512]{1,0:T(8,128)(2,1)S(1)}, u32[]{:S(2)}, u32[]{:S(2)}) collective-permute-start(bf16[16,512]{1,0:T(8,128)(2,1)S(1)} %pad_maximum_fusion.1), channel_id=1, source_target_pairs={{0,2},{1,3},{2,0},{3,1},{4,6},{5,7},{6,4},{7,5},{8,10},{9,11},{10,... | collective-permute-start | bytes 49160 | tf_op jit(solution)/shard_map/ppermute | solution.py:501
  45.3 9.1 %collective-permute-start.3 = (bf16[128,512]{1,0:T(8,128)(2,1)}, bf16[128,512]{1,0:T(8,128)(2,1)S(1)}, u32[]{:S(2)}, u32[]{:S(2)}) collective-permute-start(bf16[128,512]{1,0:T(8,128)(2,1)} %get-tuple-element.43), channel_id=1, source_target_pairs={{0,4},{1,5},{2,6},{3,7},{4,0},{5,1},{6,2},{7,3},{8,12},{9,13},{10,... | collective-permute-start | bytes 393224 | tf_op jit(solution)/shard_map/ppermute | solution.py:535
  48.2 7.7 %collective-permute-start.4 = (bf16[128,512]{1,0:T(8,128)(2,1)}, bf16[128,512]{1,0:T(8,128)(2,1)S(1)}, u32[]{:S(2)}, u32[]{:S(2)}) collective-permute-start(bf16[128,512]{1,0:T(8,128)(2,1)} %get-tuple-element.44), channel_id=1, source_target_pairs={{0,3},{1,2},{2,1},{3,0},{4,7},{5,6},{6,5},{7,4},{8,11},{9,10},{10,... | collective-permute-start | bytes 393224 | tf_op jit(solution)/shard_map/ppermute | solution.py:535
  48.3 9.6 %collective-permute-start.5 = (bf16[128,512]{1,0:T(8,128)(2,1)}, bf16[128,512]{1,0:T(8,128)(2,1)S(1)}, u32[]{:S(2)}, u32[]{:S(2)}) collective-permute-start(bf16[128,512]{1,0:T(8,128)(2,1)} %get-tuple-element.45), channel_id=1, source_target_pairs={{0,2},{1,3},{2,0},{3,1},{4,6},{5,7},{6,4},{7,5},{8,10},{9,11},{10,... | collective-permute-start | bytes 393224 | tf_op jit(solution)/shard_map/ppermute | solution.py:535
  50.1 7.7 %collective-permute-start.6 = (bf16[128,512]{1,0:T(8,128)(2,1)}, bf16[128,512]{1,0:T(8,128)(2,1)S(1)}, u32[]{:S(2)}, u32[]{:S(2)}) collective-permute-start(bf16[128,512]{1,0:T(8,128)(2,1)} %get-tuple-element.46), channel_id=1, source_target_pairs={{0,1},{1,0},{2,3},{3,2},{4,5},{5,4},{6,7},{7,6},{8,9},{9,8},{10,11... | collective-permute-start | bytes 393224 | tf_op jit(solution)/shard_map/ppermute | solution.py:535
  50.2 19.4 %copy-start.6 = (bf16[64,512]{1,0:T(8,128)(2,1)}, bf16[64,512]{1,0:T(8,128)(2,1)S(1)}, u32[]{:S(2)}) copy-start(bf16[64,512]{1,0:T(8,128)(2,1)S(1)} %pad_maximum_fusion.pool_a) | copy-start | bytes 196612
  50.2 7.7 %collective-permute-start.13 = (bf16[64,512]{1,0:T(8,128)(2,1)S(1)}, bf16[64,512]{1,0:T(8,128)(2,1)S(1)}, u32[]{:S(2)}, u32[]{:S(2)}) collective-permute-start(bf16[64,512]{1,0:T(8,128)(2,1)S(1)} %pad_maximum_fusion.pool_a), channel_id=1, source_target_pairs={{0,1},{1,0},{2,3},{3,2},{4,5},{5,4},{6,7},{7,6},{8,9},{9,8},{10,11... | collective-permute-start | bytes 196616 | tf_op jit(solution)/shard_map/ppermute | solution.py:503
  69.6 7.4 %collective-permute-start.14 = (bf16[128,512]{1,0:T(8,128)(2,1)S(1)}, bf16[128,512]{1,0:T(8,128)(2,1)S(1)}, u32[]{:S(2)}, u32[]{:S(2)}) collective-permute-start(bf16[128,512]{1,0:T(8,128)(2,1)S(1)} %get-tuple-element.57), channel_id=1, source_target_pairs={{7,0},{6,1},{5,2},{4,3},{3,4},{2,5},{1,6},{0,7},{15,8},{14,9},{13,... | collective-permute-start | bytes 393224 | tf_op jit(solution)/shard_map/ppermute | solution.py:535
  71.0 16.4 %collective-permute-start.15 = (bf16[128,512]{1,0:T(8,128)(2,1)S(1)}, bf16[128,512]{1,0:T(8,128)(2,1)S(1)}, u32[]{:S(2)}, u32[]{:S(2)}) collective-permute-start(bf16[128,512]{1,0:T(8,128)(2,1)S(1)} %get-tuple-element.58), channel_id=1, source_target_pairs={{6,0},{7,1},{4,2},{5,3},{2,4},{3,5},{0,6},{1,7},{14,8},{15,9},{12,... | collective-permute-start | bytes 393224 | tf_op jit(solution)/shard_map/ppermute | solution.py:535
  73.4 19.8 %collective-permute-start.16 = (bf16[128,512]{1,0:T(8,128)(2,1)S(1)}, bf16[128,512]{1,0:T(8,128)(2,1)S(1)}, u32[]{:S(2)}, u32[]{:S(2)}) collective-permute-start(bf16[128,512]{1,0:T(8,128)(2,1)S(1)} %get-tuple-element.59), channel_id=1, source_target_pairs={{5,0},{4,1},{7,2},{6,3},{1,4},{0,5},{3,6},{2,7},{13,8},{12,9},{15,... | collective-permute-start | bytes 393224 | tf_op jit(solution)/shard_map/ppermute | solution.py:535
  73.4 21.4 %collective-permute-start.17 = (bf16[128,512]{1,0:T(8,128)(2,1)S(1)}, bf16[128,512]{1,0:T(8,128)(2,1)S(1)}, u32[]{:S(2)}, u32[]{:S(2)}) collective-permute-start(bf16[128,512]{1,0:T(8,128)(2,1)S(1)} %get-tuple-element.60), channel_id=1, source_target_pairs={{4,0},{5,1},{6,2},{7,3},{0,4},{1,5},{2,6},{3,7},{12,8},{13,9},{14,... | collective-permute-start | bytes 393224 | tf_op jit(solution)/shard_map/ppermute | solution.py:535
  75.9 18.9 %collective-permute-start.18 = (bf16[128,512]{1,0:T(8,128)(2,1)S(1)}, bf16[128,512]{1,0:T(8,128)(2,1)S(1)}, u32[]{:S(2)}, u32[]{:S(2)}) collective-permute-start(bf16[128,512]{1,0:T(8,128)(2,1)S(1)} %get-tuple-element.61), channel_id=1, source_target_pairs={{3,0},{2,1},{1,2},{0,3},{7,4},{6,5},{5,6},{4,7},{11,8},{10,9},{9,1... | collective-permute-start | bytes 393224 | tf_op jit(solution)/shard_map/ppermute | solution.py:535
  77.0 19.2 %collective-permute-start.19 = (bf16[128,512]{1,0:T(8,128)(2,1)S(1)}, bf16[128,512]{1,0:T(8,128)(2,1)S(1)}, u32[]{:S(2)}, u32[]{:S(2)}) collective-permute-start(bf16[128,512]{1,0:T(8,128)(2,1)S(1)} %get-tuple-element.62), channel_id=1, source_target_pairs={{2,0},{3,1},{0,2},{1,3},{6,4},{7,5},{4,6},{5,7},{10,8},{11,9},{8,1... | collective-permute-start | bytes 393224 | tf_op jit(solution)/shard_map/ppermute | solution.py:535
  87.4 8.8 %collective-permute-start.20 = (bf16[128,512]{1,0:T(8,128)(2,1)S(1)}, bf16[128,512]{1,0:T(8,128)(2,1)S(1)}, u32[]{:S(2)}, u32[]{:S(2)}) collective-permute-start(bf16[128,512]{1,0:T(8,128)(2,1)S(1)} %get-tuple-element.63), channel_id=1, source_target_pairs={{1,0},{0,1},{3,2},{2,3},{5,4},{4,5},{7,6},{6,7},{9,8},{8,9},{11,10... | collective-permute-start | bytes 393224 | tf_op jit(solution)/shard_map/ppermute | solution.py:535
  (5 other events, 32.0 us)

commit v4 on v3

--- a/solution.py
+++ b/solution.py
@@ -15,6 +15,7 @@
 PAIR = 2 * HEAD
 HIDE = 512
 CHUNK = 256
+TILE = 16
 MIB = 1 << 20
 LATER = 40 * MIB
 F32 = jnp.float32
@@ -118,9 +119,9 @@
 
 def layer_one_kernel(peers, cap, *refs):
     pick_ref, ids, gain1, gain2, gain3, points, w_in, w_out, w_up, w_down = refs[:10]
-    z_out, h_out, pool_out = refs[10:13]
-    sends, refs = refs[13 : 13 + peers], refs[13 + peers :]
-    x_s, in_s, wo_s, up_s, down_s, q_s, k_s, v_s, bias_s, mix_s, y_s, z_s, h_s, sem, send_sem = refs
+    z_out, h_out = refs[10:12]
+    sends, refs = refs[12 : 12 + peers], refs[12 + peers :]
+    x_s, in_s, wo_s, up_s, down_s, q_s, k_s, v_s, bias_s, mix_s, y_s, z_s, h_s, p_s, sem, send_sem = refs
     me = lax.axis_index("pts").astype(jnp.int32)
     count, width = x_s.shape
     balls = count // BALL
@@ -174,7 +175,7 @@
         y_s[rows, :] = (x_s[rows, :].astype(F32) + dot(mix_s[rows, :], wo_s[...])).astype(BF16)
     copies[3].wait()
     copies[4].wait()
-    outgoing = []
+    outgoing, pooled = [], []
     for b in range(balls):
         rows = slice(b * BALL, (b + 1) * BALL)
         z, h3 = feed_forward(y_s[rows, :], gain2, gain3, up_s, down_s)
@@ -182,15 +183,22 @@
         h_s[rows, :] = h3
         wide = h3.astype(F32)
         for c in range(BALL // CMP):
-            part = jnp.sum(wide[c * CMP : (c + 1) * CMP], axis=0, keepdims=True) * CMP ** (-0.5)
-            at = b * (BALL // CMP) + c
-            pool_out[at : at + 1, :] = part.astype(BF16)
+            pooled.append(jnp.sum(wide[c * CMP : (c + 1) * CMP], axis=0, keepdims=True) * CMP ** (-0.5))
         at = pl.ds(b * BALL, BALL)
         for n, (source, there) in enumerate(((z_s, z_out), (h_s, h_out))):
             copy = pltpu.make_async_copy(source.at[at, :], there.at[at, :], sem.at[5 + 2 * b + n])
             copy.start()
             outgoing.append(copy)
+    row = lax.broadcasted_iota(jnp.int32, p_s.shape, 0)
+    small = jnp.zeros(p_s.shape, F32)
+    for i, part in enumerate(pooled):
+        small = jnp.where(row == i, part, small)
+    p_s[...] = small.astype(BF16)
     for s in range(peers - 1, -1, -1):
+        there = sends[s].at[pl.ds(cap * LEAF, p_s.shape[0]), :]
+        copy = pltpu.make_async_copy(p_s, there, send_sem.at[peers * cap + s])
+        copy.start()
+        outgoing.append(copy)
         for c in range(cap):
             slot = send_to(me, s, peers) * cap + c
             block = jnp.minimum(pick_ref[0, slot], blocks - 1)
@@ -205,14 +213,14 @@
     count, width = points.shape
     hidden = weights[2].shape[1]
     whole = jax.ShapeDtypeStruct((count, width), BF16)
-    block = jax.ShapeDtypeStruct((cap * LEAF, width), BF16)
-    pool = jax.ShapeDtypeStruct((count // CMP, width), BF16)
+    tail = -(-(count // CMP) // TILE) * TILE
+    block = jax.ShapeDtypeStruct((cap * LEAF + tail, width), BF16)
     balls = count // BALL
     return pl.pallas_call(
         partial(layer_one_kernel, peers, cap),
-        out_shape=[whole, whole, pool] + [block] * peers,
+        out_shape=[whole, whole] + [block] * peers,
         in_specs=[SMEM] + [VMEM] * 4 + [ANY] * 5,
-        out_specs=[ANY, ANY, VMEM] + [ANY] * peers,
+        out_specs=[ANY, ANY] + [ANY] * peers,
         scratch_shapes=[
             pltpu.VMEM((count, width), BF16),
             pltpu.VMEM((width, 3 * width), BF16),
@@ -227,8 +235,9 @@
             pltpu.VMEM((count, width), BF16),
             pltpu.VMEM((count, width), BF16),
             pltpu.VMEM((count, width), BF16),
+            pltpu.VMEM((tail, width), BF16),
             pltpu.SemaphoreType.DMA((5 + 2 * balls,)),
-            pltpu.SemaphoreType.DMA((peers * cap,)),
+            pltpu.SemaphoreType.DMA((peers * (cap + 1),)),
         ],
         compiler_params=pltpu.CompilerParams(vmem_limit_bytes=60 * MIB),
         cost_estimate=pl.CostEstimate(
@@ -346,27 +355,37 @@
     )(recv, *arrived[::-1], w_in)
 
 
-def compressed_kernel(h, z, pool_a, pool_b, w_comp, w_in, w_out, out, *scratch):
-    h_s, z_s, p_s, wc_s, wq_s, wo_s, q_s, ck_s, cv_s, a_s, o_s, sem, out_sem = scratch
+def compressed_kernel(slabs, tail, local, *refs):
+    pools = refs[:slabs]
+    h, z, w_comp, w_in, w_out, out = refs[slabs : slabs + 6]
+    h_s, z_s, p_s, wc_s, wq_s, wo_s, q_s, ck_s, cv_s, a_s, o_s, sem, pool_sem, out_sem = refs[slabs + 6 :]
     rows, width = h_s.shape
     pairs = width // PAIR
-    near = pool_a.shape[0]
+    comp = ck_s.shape[0]
     copies = [
-        pltpu.make_async_copy(pool_a, p_s.at[pl.ds(0, near), :], sem.at[0]),
-        pltpu.make_async_copy(pool_b, p_s.at[pl.ds(near, pool_b.shape[0]), :], sem.at[1]),
-        pltpu.make_async_copy(w_comp, wc_s, sem.at[2]),
-        pltpu.make_async_copy(w_in.at[:, pl.ds(0, width)], wq_s, sem.at[3]),
-        pltpu.make_async_copy(h, h_s, sem.at[4]),
-        pltpu.make_async_copy(w_out, wo_s, sem.at[5]),
-        pltpu.make_async_copy(z, z_s, sem.at[6]),
+        pltpu.make_async_copy(w_comp, wc_s, sem.at[0]),
+        pltpu.make_async_copy(w_in.at[:, pl.ds(0, width)], wq_s, sem.at[1]),
+        pltpu.make_async_copy(h, h_s, sem.at[2]),
+        pltpu.make_async_copy(w_out, wo_s, sem.at[3]),
+        pltpu.make_async_copy(z, z_s, sem.at[4]),
     ]
+    small = []
+    for n, pool in enumerate(pools):
+        there = p_s.at[pl.ds(n * pool.shape[0], pool.shape[0]), :]
+        small.append(pltpu.make_async_copy(pool, there, pool_sem.at[n]))
+    start_all(small)
     start_all(copies)
-    wait_all(copies[:3])
-    far = dot(p_s[...], wc_s[...]).astype(BF16)
+    key = lax.broadcasted_iota(jnp.int32, (comp, p_s.shape[0]), 0)
+    at = lax.broadcasted_iota(jnp.int32, (comp, p_s.shape[0]), 1)
+    taken = jnp.where(at == key // local * tail + key % local, 1.0, 0.0).astype(BF16)
+    wait_all(small)
+    pooled = dot(taken, p_s[...]).astype(BF16)
+    copies[0].wait()
+    far = dot(pooled, wc_s[...]).astype(BF16)
     ck_s[...] = far[:, :width]
     for g in range(pairs):
         lay_values(cv_s.at[g], far[:, width + g * PAIR : width + (g + 1) * PAIR])
-    wait_all(copies[3:5])
+    wait_all(copies[1:3])
     q_s[...] = (dot(h_s[...], wq_s[...]) * SCALE).astype(BF16)
 
     def scores(item):
@@ -379,7 +398,7 @@
         a_s[c * CHUNK : (c + 1) * CHUNK, g * PAIR : (g + 1) * PAIR] = weigh(got, cv_s[g]).astype(BF16)
 
     pipelined([(g, c) for c in range(rows // CHUNK) for g in range(pairs)], scores, mix)
-    wait_all(copies[5:])
+    wait_all(copies[3:])
     outgoing = []
     for c in range(rows // CHUNK):
         at = slice(c * CHUNK, (c + 1) * CHUNK)
@@ -391,18 +410,19 @@
     wait_all(outgoing)
 
 
-def compressed(h, z, pooled, w_comp, w_in, w_out):
+def compressed(tail, local, pools, h, z, w_comp, w_in, w_out):
     rows, width = h.shape
-    comp = sum(p.shape[0] for p in pooled)
+    held = sum(p.shape[0] for p in pools)
+    comp = held // tail * local
     return pl.pallas_call(
-        compressed_kernel,
+        partial(compressed_kernel, len(pools), tail, local),
         out_shape=jax.ShapeDtypeStruct((rows, width), F32),
-        in_specs=[ANY] * 7,
+        in_specs=[ANY] * (5 + len(pools)),
         out_specs=ANY,
         scratch_shapes=[
             pltpu.VMEM((rows, width), BF16),
             pltpu.VMEM((rows, width), BF16),
-            pltpu.VMEM((comp, width), BF16),
+            pltpu.VMEM((held, width), BF16),
             pltpu.VMEM((width, 2 * width), BF16),
             pltpu.VMEM((width, width), BF16),
             pltpu.VMEM((width, width), BF16),
@@ -411,17 +431,18 @@
             pltpu.VMEM((width // PAIR, 2 * comp, 2 * PAIR), BF16),
             pltpu.VMEM((rows, width), BF16),
             pltpu.VMEM((rows, width), F32),
-            pltpu.SemaphoreType.DMA((7,)),
+            pltpu.SemaphoreType.DMA((5,)),
+            pltpu.SemaphoreType.DMA((len(pools),)),
             pltpu.SemaphoreType.DMA((rows // CHUNK,)),
         ],
-        compiler_params=pltpu.CompilerParams(vmem_limit_bytes=60 * MIB),
+        compiler_params=pltpu.CompilerParams(vmem_limit_bytes=LATER),
         cost_estimate=pl.CostEstimate(
             flops=rows * width * (4 * width + 16 * comp),
             bytes_accessed=8 * MIB,
             transcendentals=rows * comp * width // HEAD,
         ),
         name="compressed",
-    )(h, z, *pooled, w_comp, w_in, w_out)
+    )(*pools, h, z, w_comp, w_in, w_out)
 
 
 def final_kernel(peers, cap, bounds, pick_ref, *refs):
@@ -488,21 +509,6 @@
     )(pick, *back, w_out, base)
 
 
-def xor_pairs(size, s):
-    return [(i, i ^ s) for i in range(size)]
-
-
-def gather_all(rows, axes):
-    (grp, groups), (pts, peers) = axes
-    if groups & (groups - 1) or peers & (peers - 1) or peers == 1:
-        rows = lax.all_gather(rows, (grp, pts), axis=0, tiled=True)
-        return rows[: rows.shape[0] // 2], rows[rows.shape[0] // 2 :]
-    for axis, shifts in ((grp, range(1, groups)), (pts, range(2, peers, 2))):
-        pieces = [rows] + [lax.ppermute(rows, axis, xor_pairs(axes[axis == pts][1], s)) for s in shifts]
-        rows = lax.optimization_barrier(jnp.concatenate(pieces))
-    return rows, lax.ppermute(rows, pts, xor_pairs(peers, 1))
-
-
 def shards(
     axes,
     points,
@@ -534,18 +540,19 @@
             pattern = [(b, a) for a, b in pattern]
         return lax.ppermute(blocks, "pts", pattern)
 
-    z, h, pool, *sends = layer_one(peers, cap, send_pick, ball_ids, gains, points, weights)
+    z, h, *sends = layer_one(peers, cap, send_pick, ball_ids, gains, points, weights)
     arrived = [travel(sends[s], s, False) for s in range(peers)]
-    pool, far = lax.optimization_barrier((pool, arrived[: -3 : -1]))
-    arrived[-2:] = far[::-1]
-    pooled = gather_all(pool, axes)
-    arrived, pooled = lax.optimization_barrier((arrived[::-1], pooled))
+    tail = sends[0].shape[0] - cap * LEAF
+    slab = jnp.concatenate([block[cap * LEAF :] for block in arrived])
+    groups = axes[0][1]
+    turns = [[(i, (i + s) % groups) for i in range(groups)] for s in range(1, groups)]
+    pools = [slab] + [lax.ppermute(slab, "grp", turn) for turn in turns]
+    mixed = layer_two(peers, cap, 0, width, recv_from, arrived, attn_in_two)
+    mixed, pools = lax.optimization_barrier((mixed, pools))
     bounds = [(0, width)]
-    back = []
-    for start, columns in bounds:
-        mixed = layer_two(peers, cap, start, columns, recv_from, arrived[::-1], attn_in_two)
-        back.extend(travel(mixed[s], s, True) for s in range(peers - 1, -1, -1))
-    base = compressed(h, z, pooled, compress_proj, attn_in_two, attn_out_two)
+    back = [travel(mixed[s], s, True) for s in range(peers - 1, -1, -1)]
+    local = points.shape[0] // CMP
+    base = compressed(tail, local, pools, h, z, compress_proj, attn_in_two, attn_out_two)
     return final(peers, cap, bounds, send_pick, back, attn_out_two, base)
 
 

time: 102 us -> 97.8 us (0.959)
  starting transfers between devices: 40.4 us -> 31 us
  waiting for transfers between devices: 18.8 us -> 26.7 us
  Pallas kernels: 38.9 us -> 37.8 us
    ppermute x14, waiting for transfers between devices: 18.8 us -> 26.6 us  [travel(): return lax.ppermute(blocks, 'pts', pattern)]
    ppermute x14, starting transfers between devices: 31.3 us -> 26.6 us  [travel(): return lax.ppermute(blocks, 'pts', pattern)]
    ppermute x7 -> x3, starting transfers between devices: 9.08 us -> 4.48 us  [shards(): pools = [slab] + [lax.ppermute(slab, 'grp', turn) for turn in turns]]
    unnamed x16 -> x23, local copies, waits for them, and re-layouts: 2.53 us -> 1.68 us
  transfers between devices with their start and end apart: 21 -> 17, of which waited for: 8 -> 6; matrix products, arithmetic and copies ran while one was open for 1% -> 1% of each run, Pallas kernels for 6% -> 16%
where the time goes in v4:
time: 97.8 us; the launch traced here: 97.5 us
  Pallas kernels  37.8 us (39%)
  starting transfers between devices  31 us (32%)
  waiting for transfers between devices  26.7 us (27%)
  local copies, waits for them, and re-layouts  1.68 us (2%)
    ppermute x14, waiting for transfers between devices, travel(): return lax.ppermute(blocks, 'pts', pattern)  26.6 us
    ppermute x14, starting transfers between devices, travel(): return lax.ppermute(blocks, 'pts', pattern)  26.6 us
    pallas_call x1, Pallas kernels, layer_one(): pl.pallas_call(partial(layer_one_kernel, peers, cap), out_shape=[whole, w...  18.1 us
    pallas_call x1, Pallas kernels, layer_two(): pl.pallas_call(partial(layer_two_kernel, peers, cap, blocks, start, colum...  10.8 us
    pallas_call x1, Pallas kernels, compressed(): pl.pallas_call(partial(compressed_kernel, len(pools), tail, local), out_s...  5.23 us
    ppermute x3, starting transfers between devices, shards(): pools = [slab] + [lax.ppermute(slab, 'grp', turn) for turn in turns]  4.48 us
    pallas_call x1, Pallas kernels, final(): pl.pallas_call(partial(final_kernel, peers, cap, bounds), out_shape=jax.S...  3.69 us
  transfers between devices with their start and end apart: 17, of which 6 were waited for; matrix products, arithmetic and copies ran while one was open for 1% of the time, Pallas kernels for 16%

profile of v4, /device:TPU:0, one launch (start us, length us, event | category | flops | bytes accessed | tf_op | source)
XLA Modules:
  0.0 97.5 jit_solution(6046632043388495676)
XLA Ops:
  0.0 18.1 %layer_one.1 = (bf16[1024,512]{1,0:T(8,128)(2,1)}, bf16[1024,512]{1,0:T(8,128)(2,1)}, bf16[144,512]{1,0:T(8,128)(2,1)}, bf16[144,512]{1,0:T(8,128)(2,1)}, bf16[1...) custom-call(s32[1,8]{1,0:T(1,128)} %pick_ref.1, ...), custom_call_target="tpu_custom_call" | custom-call | flops 10737418240 | bytes 10485760 | tf_op jit(solution)/shard_map/layer_one/pallas_call | solution.py:219
  18.1 4.5 %collective-permute-start = (bf16[144,512]{1,0:T(8,128)(2,1)}, bf16[144,512]{1,0:T(8,128)(2,1)S(1)}, u32[]{:S(2)}, u32[]{:S(2)}) collective-permute-start(bf16[144,512]{1,0:T(8,128)(2,1)} %get-tuple-element.35), channel_id=1, source_target_pairs={{0,7},{1,6},{2,5},{3,4},{4,3},{5,2},{6,1},{7,0},{8,15},{9,14},{10,... | collective-permute-start | bytes 442376 | tf_op jit(solution)/shard_map/ppermute | solution.py:541
  22.7 0.6 collective-permute-start.1
  23.3 0.4 collective-permute-start.2
  23.7 2.2 %collective-permute-start.3 = (bf16[144,512]{1,0:T(8,128)(2,1)}, bf16[144,512]{1,0:T(8,128)(2,1)S(1)}, u32[]{:S(2)}, u32[]{:S(2)}) collective-permute-start(bf16[144,512]{1,0:T(8,128)(2,1)} %get-tuple-element.38), channel_id=1, source_target_pairs={{0,4},{1,5},{2,6},{3,7},{4,0},{5,1},{6,2},{7,3},{8,12},{9,13},{10,... | collective-permute-start | bytes 442376 | tf_op jit(solution)/shard_map/ppermute | solution.py:541
  26.1 0.7 constant_dynamic-update-slice_fusion.7
  26.8 0.7 collective-permute-done.6.refs_7_
  27.5 1.2 %collective-permute-start.5 = (bf16[144,512]{1,0:T(8,128)(2,1)}, bf16[144,512]{1,0:T(8,128)(2,1)S(1)}, u32[]{:S(2)}, u32[]{:S(2)}) collective-permute-start(bf16[144,512]{1,0:T(8,128)(2,1)} %get-tuple-element.40), channel_id=1, source_target_pairs={{0,2},{1,3},{2,0},{3,1},{4,6},{5,7},{6,4},{7,5},{8,10},{9,11},{10,... | collective-permute-start | bytes 442376 | tf_op jit(solution)/shard_map/ppermute | solution.py:541
  28.7 11.2 %collective-permute-done.5.refs_6_ = bf16[144,512]{1,0:T(8,128)(2,1)S(1)} collective-permute-done((bf16[144,512]{1,0:T(8,128)(2,1)}, bf16[144,512]{1,0:T(8,128)(2,1)S(1)}, u32[]{:S(2)}, u32[]{:S(2)}) %collective-permute-start.5) | collective-permute-done | bytes 147488 | tf_op jit(solution)/shard_map/ppermute | solution.py:541
  39.9 2.1 %collective-permute-start.4 = (bf16[144,512]{1,0:T(8,128)(2,1)}, bf16[144,512]{1,0:T(8,128)(2,1)S(1)}, u32[]{:S(2)}, u32[]{:S(2)}) collective-permute-start(bf16[144,512]{1,0:T(8,128)(2,1)} %get-tuple-element.39), channel_id=1, source_target_pairs={{0,3},{1,2},{2,1},{3,0},{4,7},{5,6},{6,5},{7,4},{8,11},{9,10},{10,... | collective-permute-start | bytes 442376 | tf_op jit(solution)/shard_map/ppermute | solution.py:541
  42.0 10.2 %collective-permute-done.4.refs_5_ = bf16[144,512]{1,0:T(8,128)(2,1)S(1)} collective-permute-done((bf16[144,512]{1,0:T(8,128)(2,1)}, bf16[144,512]{1,0:T(8,128)(2,1)S(1)}, u32[]{:S(2)}, u32[]{:S(2)}) %collective-permute-start.4) | collective-permute-done | bytes 147488 | tf_op jit(solution)/shard_map/ppermute | solution.py:541
  52.3 1.5 %collective-permute-start.7 = (bf16[128,512]{1,0:T(8,128)(2,1)S(1)}, bf16[128,512]{1,0:T(8,128)(2,1)S(1)}, u32[]{:S(2)}, u32[]{:S(2)}) collective-permute-start(bf16[128,512]{1,0:T(8,128)(2,1)S(1)} %constant_dynamic-update-slice_fusion.refs_0_), channel_id=1, source_target_pairs={{0,8},{8,16},{16,24},{24,0},{1,9},{9,17},{17,25},{25,1},{2,10},{10... | collective-permute-start | bytes 393224 | tf_op jit(solution)/shard_map/ppermute | solution.py:549
  53.9 1.5 %collective-permute-start.8 = (bf16[128,512]{1,0:T(8,128)(2,1)S(1)}, bf16[128,512]{1,0:T(8,128)(2,1)S(1)}, u32[]{:S(2)}, u32[]{:S(2)}) collective-permute-start(bf16[128,512]{1,0:T(8,128)(2,1)S(1)} %constant_dynamic-update-slice_fusion.refs_0_), channel_id=1, source_target_pairs={{0,16},{8,24},{16,0},{24,8},{1,17},{9,25},{17,1},{25,9},{2,18},{10... | collective-permute-start | bytes 393224 | tf_op jit(solution)/shard_map/ppermute | solution.py:549
  55.4 1.4 %collective-permute-start.9 = (bf16[128,512]{1,0:T(8,128)(2,1)S(1)}, bf16[128,512]{1,0:T(8,128)(2,1)S(1)}, u32[]{:S(2)}, u32[]{:S(2)}) collective-permute-start(bf16[128,512]{1,0:T(8,128)(2,1)S(1)} %constant_dynamic-update-slice_fusion.refs_0_), channel_id=1, source_target_pairs={{0,24},{8,0},{16,8},{24,16},{1,25},{9,1},{17,9},{25,17},{2,26},{10... | collective-permute-start | bytes 393224 | tf_op jit(solution)/shard_map/ppermute | solution.py:549
  56.8 0.9 copy-done.1
  57.7 10.8 %layer_two_0.1 = (bf16[128,512]{1,0:T(8,128)(2,1)S(1)}, bf16[128,512]{1,0:T(8,128)(2,1)S(1)}, bf16[128,512]{1,0:T(8,128)(2,1)S(1)}, bf16[128,512]{1,0:T(8,128)(2...) custom-call(s32[1,8]{1,0:T(1,128)S(1)} %copy-done.5, ...), custom_call_target="tpu_custom_call" | custom-call | flops 5905580032 | bytes 4194304 | tf_op jit(solution)/shard_map/layer_two_0/pallas_call | solution.py:333
  68.6 2.7 %collective-permute-start.11 = (bf16[128,512]{1,0:T(8,128)(2,1)S(1)}, bf16[128,512]{1,0:T(8,128)(2,1)S(1)}, u32[]{:S(2)}, u32[]{:S(2)}) collective-permute-start(bf16[128,512]{1,0:T(8,128)(2,1)S(1)} %get-tuple-element.52), channel_id=1, source_target_pairs={{6,0},{7,1},{4,2},{5,3},{2,4},{3,5},{0,6},{1,7},{14,8},{15,9},{12,... | collective-permute-start | bytes 393224 | tf_op jit(solution)/shard_map/ppermute | solution.py:541
  71.3 3.5 %collective-permute-start.13 = (bf16[128,512]{1,0:T(8,128)(2,1)S(1)}, bf16[128,512]{1,0:T(8,128)(2,1)S(1)}, u32[]{:S(2)}, u32[]{:S(2)}) collective-permute-start(bf16[128,512]{1,0:T(8,128)(2,1)S(1)} %get-tuple-element.54), channel_id=1, source_target_pairs={{4,0},{5,1},{6,2},{7,3},{0,4},{1,5},{2,6},{3,7},{12,8},{13,9},{14,... | collective-permute-start | bytes 393224 | tf_op jit(solution)/shard_map/ppermute | solution.py:541
  74.8 1.4 %collective-permute-done.10.refs_0_ = bf16[128,512]{1,0:T(8,128)(2,1)S(1)} collective-permute-done((bf16[128,512]{1,0:T(8,128)(2,1)S(1)}, bf16[128,512]{1,0:T(8,128)(2,1)S(1)}, u32[]{:S(2)}, u32[]{:S(2)}) %collective-permute-start.10) | collective-permute-done | bytes 131104 | tf_op jit(solution)/shard_map/ppermute | solution.py:541
  76.3 9.0 %collective-permute-start.15 = (bf16[128,512]{1,0:T(8,128)(2,1)S(1)}, bf16[128,512]{1,0:T(8,128)(2,1)S(1)}, u32[]{:S(2)}, u32[]{:S(2)}) collective-permute-start(bf16[128,512]{1,0:T(8,128)(2,1)S(1)} %get-tuple-element.56), channel_id=1, source_target_pairs={{2,0},{3,1},{0,2},{1,3},{6,4},{7,5},{4,6},{5,7},{10,8},{11,9},{8,1... | collective-permute-start | bytes 393224 | tf_op jit(solution)/shard_map/ppermute | solution.py:541
  85.4 5.2 %compressed.1.refs_9_ = f32[1024,512]{1,0:T(8,128)S(1)} custom-call(bf16[128,512]{1,0:T(8,128)(2,1)S(1)} %constant_dynamic-update-slice_fusion.refs_0_, bf16[128,512]{1,0:T(8,128)(2,1)S(1)} %collective-permute-done.7.refs_1_, bf16[128,512]{1,0:T(8,128)(2,1)S(1)} %collective-permute-done.8.refs_2_, bf16[128,512]{1,0:T(8,128)(2,1)S(1)} %collective-permute-done.9.refs_3_, ...), custom_call_target="tpu_custom_call" | custom-call | flops 2147483648 | bytes 8388608 | tf_op jit(solution)/shard_map/compressed/pallas_call | solution.py:417
  90.6 1.6 %collective-permute-done.13.refs_3_ = bf16[128,512]{1,0:T(8,128)(2,1)S(1)} collective-permute-done((bf16[128,512]{1,0:T(8,128)(2,1)S(1)}, bf16[128,512]{1,0:T(8,128)(2,1)S(1)}, u32[]{:S(2)}, u32[]{:S(2)}) %collective-permute-start.13) | collective-permute-done | bytes 131104 | tf_op jit(solution)/shard_map/ppermute | solution.py:541
  92.2 1.5 %collective-permute-done.15.refs_5_ = bf16[128,512]{1,0:T(8,128)(2,1)S(1)} collective-permute-done((bf16[128,512]{1,0:T(8,128)(2,1)S(1)}, bf16[128,512]{1,0:T(8,128)(2,1)S(1)}, u32[]{:S(2)}, u32[]{:S(2)}) %collective-permute-start.15) | collective-permute-done | bytes 131104 | tf_op jit(solution)/shard_map/ppermute | solution.py:541
  93.7 3.7 %last_product.1 = bf16[1024,512]{1,0:T(8,128)(2,1)} custom-call(s32[1,8]{1,0:T(1,128)S(1)} %copy-done.2, bf16[128,512]{1,0:T(8,128)(2,1)S(1)} %collective-permute-done.10.refs_0_, bf16[128,512]{1,0:T(8,128)(2,1)S(1)} %collective-permute-done.11.refs_1_, bf16[128,512]{1,0:T(8,128)(2,1)S(1)} %collective-permute-done.12.refs_2_, ...), custom_call_target="tpu_custom_call" | custom-call | flops 536870912 | bytes 4194304 | tf_op jit(solution)/shard_map/last_product/pallas_call | solution.py:490
  (38 shorter events, 0.4 us)
Async XLA Ops:
  0.0 56.8 %copy-start.3 = (bf16[512,1536]{1,0:T(8,128)(2,1)S(1)}, bf16[512,1536]{1,0:T(8,128)(2,1)}, u32[]{:S(2)}) copy-start(bf16[512,1536]{1,0:T(8,128)(2,1)} %refs_7_.3) | copy-start | bytes 4718596
  0.0 56.8 %copy-start.5 = (s32[1,8]{1,0:T(1,128)S(1)}, s32[1,8]{1,0:T(1,128)}, u32[]{:S(2)}) copy-start(s32[1,8]{1,0:T(1,128)} %refs_0_.3) | copy-start | bytes 100
  18.1 34.2 %collective-permute-start = (bf16[144,512]{1,0:T(8,128)(2,1)}, bf16[144,512]{1,0:T(8,128)(2,1)S(1)}, u32[]{:S(2)}, u32[]{:S(2)}) collective-permute-start(bf16[144,512]{1,0:T(8,128)(2,1)} %get-tuple-element.35), channel_id=1, source_target_pairs={{0,7},{1,6},{2,5},{3,4},{4,3},{5,2},{6,1},{7,0},{8,15},{9,14},{10,... | collective-permute-start | bytes 442376 | tf_op jit(solution)/shard_map/ppermute | solution.py:541
  22.7 29.6 %collective-permute-start.1 = (bf16[144,512]{1,0:T(8,128)(2,1)}, bf16[144,512]{1,0:T(8,128)(2,1)S(1)}, u32[]{:S(2)}, u32[]{:S(2)}) collective-permute-start(bf16[144,512]{1,0:T(8,128)(2,1)} %get-tuple-element.36), channel_id=1, source_target_pairs={{0,6},{1,7},{2,4},{3,5},{4,2},{5,3},{6,0},{7,1},{8,14},{9,15},{10,... | collective-permute-start | bytes 442376 | tf_op jit(solution)/shard_map/ppermute | solution.py:541
  23.3 28.9 %collective-permute-start.2 = (bf16[144,512]{1,0:T(8,128)(2,1)}, bf16[144,512]{1,0:T(8,128)(2,1)S(1)}, u32[]{:S(2)}, u32[]{:S(2)}) collective-permute-start(bf16[144,512]{1,0:T(8,128)(2,1)} %get-tuple-element.37), channel_id=1, source_target_pairs={{0,5},{1,4},{2,7},{3,6},{4,1},{5,0},{6,3},{7,2},{8,13},{9,12},{10,... | collective-permute-start | bytes 442376 | tf_op jit(solution)/shard_map/ppermute | solution.py:541
  23.7 28.5 %collective-permute-start.3 = (bf16[144,512]{1,0:T(8,128)(2,1)}, bf16[144,512]{1,0:T(8,128)(2,1)S(1)}, u32[]{:S(2)}, u32[]{:S(2)}) collective-permute-start(bf16[144,512]{1,0:T(8,128)(2,1)} %get-tuple-element.38), channel_id=1, source_target_pairs={{0,4},{1,5},{2,6},{3,7},{4,0},{5,1},{6,2},{7,3},{8,12},{9,13},{10,... | collective-permute-start | bytes 442376 | tf_op jit(solution)/shard_map/ppermute | solution.py:541
  25.9 1.6 %collective-permute-start.6 = (bf16[144,512]{1,0:T(8,128)(2,1)}, bf16[144,512]{1,0:T(8,128)(2,1)S(1)}, u32[]{:S(2)}, u32[]{:S(2)}) collective-permute-start(bf16[144,512]{1,0:T(8,128)(2,1)} %get-tuple-element.41), channel_id=1, source_target_pairs={{0,1},{1,0},{2,3},{3,2},{4,5},{5,4},{6,7},{7,6},{8,9},{9,8},{10,11... | collective-permute-start | bytes 442376 | tf_op jit(solution)/shard_map/ppermute | solution.py:541
  27.5 12.4 %collective-permute-start.5 = (bf16[144,512]{1,0:T(8,128)(2,1)}, bf16[144,512]{1,0:T(8,128)(2,1)S(1)}, u32[]{:S(2)}, u32[]{:S(2)}) collective-permute-start(bf16[144,512]{1,0:T(8,128)(2,1)} %get-tuple-element.40), channel_id=1, source_target_pairs={{0,2},{1,3},{2,0},{3,1},{4,6},{5,7},{6,4},{7,5},{8,10},{9,11},{10,... | collective-permute-start | bytes 442376 | tf_op jit(solution)/shard_map/ppermute | solution.py:541
  39.9 12.3 %collective-permute-start.4 = (bf16[144,512]{1,0:T(8,128)(2,1)}, bf16[144,512]{1,0:T(8,128)(2,1)S(1)}, u32[]{:S(2)}, u32[]{:S(2)}) collective-permute-start(bf16[144,512]{1,0:T(8,128)(2,1)} %get-tuple-element.39), channel_id=1, source_target_pairs={{0,3},{1,2},{2,1},{3,0},{4,7},{5,6},{6,5},{7,4},{8,11},{9,10},{10,... | collective-permute-start | bytes 442376 | tf_op jit(solution)/shard_map/ppermute | solution.py:541
  52.3 33.0 %copy-start = (bf16[512,512]{1,0:T(8,128)(2,1)S(1)}, bf16[512,512]{1,0:T(8,128)(2,1)}, u32[]{:S(2)}) copy-start(bf16[512,512]{1,0:T(8,128)(2,1)} %refs_8_.5) | copy-start | bytes 1572868
  52.3 16.2 %collective-permute-start.7 = (bf16[128,512]{1,0:T(8,128)(2,1)S(1)}, bf16[128,512]{1,0:T(8,128)(2,1)S(1)}, u32[]{:S(2)}, u32[]{:S(2)}) collective-permute-start(bf16[128,512]{1,0:T(8,128)(2,1)S(1)} %constant_dynamic-update-slice_fusion.refs_0_), channel_id=1, source_target_pairs={{0,8},{8,16},{16,24},{24,0},{1,9},{9,17},{17,25},{25,1},{2,10},{10... | collective-permute-start | bytes 393224 | tf_op jit(solution)/shard_map/ppermute | solution.py:549
  53.9 14.7 %collective-permute-start.8 = (bf16[128,512]{1,0:T(8,128)(2,1)S(1)}, bf16[128,512]{1,0:T(8,128)(2,1)S(1)}, u32[]{:S(2)}, u32[]{:S(2)}) collective-permute-start(bf16[128,512]{1,0:T(8,128)(2,1)S(1)} %constant_dynamic-update-slice_fusion.refs_0_), channel_id=1, source_target_pairs={{0,16},{8,24},{16,0},{24,8},{1,17},{9,25},{17,1},{25,9},{2,18},{10... | collective-permute-start | bytes 393224 | tf_op jit(solution)/shard_map/ppermute | solution.py:549
  55.4 13.2 %collective-permute-start.9 = (bf16[128,512]{1,0:T(8,128)(2,1)S(1)}, bf16[128,512]{1,0:T(8,128)(2,1)S(1)}, u32[]{:S(2)}, u32[]{:S(2)}) collective-permute-start(bf16[128,512]{1,0:T(8,128)(2,1)S(1)} %constant_dynamic-update-slice_fusion.refs_0_), channel_id=1, source_target_pairs={{0,24},{8,0},{16,8},{24,16},{1,25},{9,1},{17,9},{25,17},{2,26},{10... | collective-permute-start | bytes 393224 | tf_op jit(solution)/shard_map/ppermute | solution.py:549
  57.7 27.6 %copy-start.4 = (bf16[512,1024]{1,0:T(8,128)(2,1)S(1)}, bf16[512,1024]{1,0:T(8,128)(2,1)}, u32[]{:S(2)}) copy-start(bf16[512,1024]{1,0:T(8,128)(2,1)} %refs_6_.3) | copy-start | bytes 3145732
  57.7 27.6 %copy-start.6 = (bf16[1024,512]{1,0:T(8,128)(2,1)S(1)}, bf16[1024,512]{1,0:T(8,128)(2,1)}, u32[]{:S(2)}) copy-start(bf16[1024,512]{1,0:T(8,128)(2,1)} %get-tuple-element.64.refs_5_) | copy-start | bytes 3145732
  57.7 27.6 %copy-start.7 = (bf16[1024,512]{1,0:T(8,128)(2,1)S(1)}, bf16[1024,512]{1,0:T(8,128)(2,1)}, u32[]{:S(2)}) copy-start(bf16[1024,512]{1,0:T(8,128)(2,1)} %get-tuple-element.63.refs_4_) | copy-start | bytes 3145732
  68.6 7.7 %collective-permute-start.10 = (bf16[128,512]{1,0:T(8,128)(2,1)S(1)}, bf16[128,512]{1,0:T(8,128)(2,1)S(1)}, u32[]{:S(2)}, u32[]{:S(2)}) collective-permute-start(bf16[128,512]{1,0:T(8,128)(2,1)S(1)} %get-tuple-element.51), channel_id=1, source_target_pairs={{7,0},{6,1},{5,2},{4,3},{3,4},{2,5},{1,6},{0,7},{15,8},{14,9},{13,... | collective-permute-start | bytes 393224 | tf_op jit(solution)/shard_map/ppermute | solution.py:541
  68.6 16.7 %collective-permute-start.11 = (bf16[128,512]{1,0:T(8,128)(2,1)S(1)}, bf16[128,512]{1,0:T(8,128)(2,1)S(1)}, u32[]{:S(2)}, u32[]{:S(2)}) collective-permute-start(bf16[128,512]{1,0:T(8,128)(2,1)S(1)} %get-tuple-element.52), channel_id=1, source_target_pairs={{6,0},{7,1},{4,2},{5,3},{2,4},{3,5},{0,6},{1,7},{14,8},{15,9},{12,... | collective-permute-start | bytes 393224 | tf_op jit(solution)/shard_map/ppermute | solution.py:541
  71.3 19.3 %collective-permute-start.12 = (bf16[128,512]{1,0:T(8,128)(2,1)S(1)}, bf16[128,512]{1,0:T(8,128)(2,1)S(1)}, u32[]{:S(2)}, u32[]{:S(2)}) collective-permute-start(bf16[128,512]{1,0:T(8,128)(2,1)S(1)} %get-tuple-element.53), channel_id=1, source_target_pairs={{5,0},{4,1},{7,2},{6,3},{1,4},{0,5},{3,6},{2,7},{13,8},{12,9},{15,... | collective-permute-start | bytes 393224 | tf_op jit(solution)/shard_map/ppermute | solution.py:541
  71.3 20.8 %collective-permute-start.13 = (bf16[128,512]{1,0:T(8,128)(2,1)S(1)}, bf16[128,512]{1,0:T(8,128)(2,1)S(1)}, u32[]{:S(2)}, u32[]{:S(2)}) collective-permute-start(bf16[128,512]{1,0:T(8,128)(2,1)S(1)} %get-tuple-element.54), channel_id=1, source_target_pairs={{4,0},{5,1},{6,2},{7,3},{0,4},{1,5},{2,6},{3,7},{12,8},{13,9},{14,... | collective-permute-start | bytes 393224 | tf_op jit(solution)/shard_map/ppermute | solution.py:541
  74.8 17.4 %collective-permute-start.14 = (bf16[128,512]{1,0:T(8,128)(2,1)S(1)}, bf16[128,512]{1,0:T(8,128)(2,1)S(1)}, u32[]{:S(2)}, u32[]{:S(2)}) collective-permute-start(bf16[128,512]{1,0:T(8,128)(2,1)S(1)} %get-tuple-element.55), channel_id=1, source_target_pairs={{3,0},{2,1},{1,2},{0,3},{7,4},{6,5},{5,6},{4,7},{11,8},{10,9},{9,1... | collective-permute-start | bytes 393224 | tf_op jit(solution)/shard_map/ppermute | solution.py:541
  76.3 17.4 %collective-permute-start.15 = (bf16[128,512]{1,0:T(8,128)(2,1)S(1)}, bf16[128,512]{1,0:T(8,128)(2,1)S(1)}, u32[]{:S(2)}, u32[]{:S(2)}) collective-permute-start(bf16[128,512]{1,0:T(8,128)(2,1)S(1)} %get-tuple-element.56), channel_id=1, source_target_pairs={{2,0},{3,1},{0,2},{1,3},{6,4},{7,5},{4,6},{5,7},{10,8},{11,9},{8,1... | collective-permute-start | bytes 393224 | tf_op jit(solution)/shard_map/ppermute | solution.py:541
  85.3 8.4 %collective-permute-start.16 = (bf16[128,512]{1,0:T(8,128)(2,1)S(1)}, bf16[128,512]{1,0:T(8,128)(2,1)S(1)}, u32[]{:S(2)}, u32[]{:S(2)}) collective-permute-start(bf16[128,512]{1,0:T(8,128)(2,1)S(1)} %get-tuple-element.57), channel_id=1, source_target_pairs={{1,0},{0,1},{3,2},{2,3},{5,4},{4,5},{7,6},{6,7},{9,8},{8,9},{11,10... | collective-permute-start | bytes 393224 | tf_op jit(solution)/shard_map/ppermute | solution.py:541
  85.3 8.3 %copy-start.2 = (s32[1,8]{1,0:T(1,128)S(1)}, s32[1,8]{1,0:T(1,128)}, u32[]{:S(2)}) copy-start(s32[1,8]{1,0:T(1,128)} %pick_ref.1) | copy-start | bytes 100
  (1 other events, 0.9 us)

commit v5 on v4

--- a/solution.py
+++ b/solution.py
@@ -108,12 +108,16 @@
 
 def feed_forward(y, gain2, gain3, up_s, down_s):
     inner = norm(y, gain2[...]).astype(BF16)
-    total = y.astype(F32)
-    for c in range(up_s.shape[1] // HIDE):
-        cols = slice(c * HIDE, (c + 1) * HIDE)
-        up = gelu(dot(inner, up_s[:, cols])).astype(BF16)
-        total = total + dot(up, down_s[cols, :])
-    z = total.astype(BF16)
+    total = [y.astype(F32)]
+
+    def rise(c):
+        return dot(inner, up_s[:, c * HIDE : (c + 1) * HIDE])
+
+    def fall(c, got):
+        total[0] = total[0] + dot(gelu(got).astype(BF16), down_s[c * HIDE : (c + 1) * HIDE, :])
+
+    pipelined(list(range(up_s.shape[1] // HIDE)), rise, fall)
+    z = total[0].astype(BF16)
     return z, norm(z, gain3[...]).astype(BF16)
 
 
@@ -134,7 +138,7 @@
         pltpu.make_async_copy(w_up, up_s, sem.at[3]),
         pltpu.make_async_copy(w_down, down_s, sem.at[4]),
     ]
-    start_all(copies)
+    start_all(copies[:2])
     for b in range(balls):
         across = jnp.broadcast_to(ids[b : b + 1, :], (LEAF, BALL)).astype(F32)
         down = across.T
@@ -147,6 +151,7 @@
         h1 = norm(x_s[rows, :], gain1[...]).astype(BF16)
         if b == 0:
             copies[1].wait()
+            start_all(copies[2:])
         q_s[rows, :] = (dot(h1, in_s[:, :width]) * SCALE).astype(BF16)
         k_s[rows, :] = dot(h1, in_s[:, width : 2 * width]).astype(BF16)
         values = dot(h1, in_s[:, 2 * width :]).astype(BF16)
@@ -258,43 +263,35 @@
     return place, found > 0
 
 
-def layer_two_kernel(peers, cap, blocks, start, columns, *refs):
+def layer_two_kernel(peers, cap, flow, blocks, start, columns, *refs):
     recv_ref = refs[0]
-    arrived = refs[1 : 1 + peers][::-1]
+    arrived = dict(zip(flow, refs[1 : 1 + peers]))
     w_in = refs[1 + peers]
     outs = refs[2 + peers : 2 + 2 * peers]
-    h_s, w_s, q_s, k_s, v_s, a_s, sem, block_sem = refs[2 + 2 * peers :]
+    h_s, q_s, k_s, v_s, a_s = refs[2 + 2 * peers :]
     width = h_s.shape[1]
     pairs = columns // PAIR
     me = lax.axis_index("pts").astype(jnp.int32)
     balls = blocks * LEAF // BALL
-    copies = []
-    for i in range(3):
-        cols = pl.ds(i * width + start, columns)
-        copies.append(
-            pltpu.make_async_copy(w_in.at[:, cols], w_s.at[:, pl.ds(i * columns, columns)], sem.at[i])
-        )
-    start_all(copies)
-    places, moves = [], []
+    places = []
     for s in range(peers):
         for c in range(cap):
             place, found = place_of(recv_ref, got_from(me, s, peers) * cap + c, blocks)
-            at = pl.ds(c * LEAF, LEAF)
-            move = pltpu.make_async_copy(
-                arrived[s].at[at, :], h_s.at[aligned(place, LEAF), :], block_sem.at[s * cap + c]
-            )
             places.append(place)
-            moves.append((found, move))
-            pl.when(found)(move.start)
-    wait_all(copies)
-    for found, move in moves:
-        pl.when(found)(move.wait)
+
+            @pl.when(found)
+            def _():
+                h_s[aligned(place, LEAF), :] = arrived[s][c * LEAF : (c + 1) * LEAF, :]
+
+    def product(h, i):
+        return dot(h, w_in[:, i * width + start : i * width + start + columns])
+
     for b in range(balls):
         rows = slice(b * BALL, (b + 1) * BALL)
         h = h_s[rows, :]
-        q_s[rows, :] = (dot(h, w_s[:, :columns]) * SCALE).astype(BF16)
-        k_s[rows, :] = dot(h, w_s[:, columns : 2 * columns]).astype(BF16)
-        values = dot(h, w_s[:, 2 * columns :]).astype(BF16)
+        q_s[rows, :] = (product(h, 0) * SCALE).astype(BF16)
+        k_s[rows, :] = product(h, 1).astype(BF16)
+        values = product(h, 2).astype(BF16)
         for g in range(pairs):
             lay_values(v_s.at[b * pairs + g], values[:, g * PAIR : (g + 1) * PAIR])
 
@@ -312,38 +309,28 @@
     pipelined(
         [(b, g, c) for b in range(balls) for g in range(pairs) for c in range(BALL // CHUNK)], scores, mix
     )
-    outgoing = []
     for s in range(peers):
         for c in range(cap):
-            n = s * cap + c
-            at = pl.ds(c * LEAF, LEAF)
-            outgoing.append(
-                pltpu.make_async_copy(a_s.at[aligned(places[n], LEAF), :], outs[s].at[at, :], block_sem.at[n])
-            )
-    start_all(outgoing)
-    wait_all(outgoing)
-
-
-def layer_two(peers, cap, start, columns, recv, arrived, w_in):
+            outs[s][c * LEAF : (c + 1) * LEAF, :] = a_s[aligned(places[s * cap + c], LEAF), :]
+
+
+def layer_two(peers, cap, flow, start, columns, recv, arrived, w_in):
     blocks = recv.shape[1]
     width = w_in.shape[0]
     pairs = columns // PAIR
     rows = blocks * LEAF
     block = jax.ShapeDtypeStruct((cap * LEAF, columns), BF16)
     return pl.pallas_call(
-        partial(layer_two_kernel, peers, cap, blocks, start, columns),
+        partial(layer_two_kernel, peers, cap, flow, blocks, start, columns),
         out_shape=[block] * peers,
-        in_specs=[SMEM] + [ANY] * (peers + 1),
-        out_specs=[ANY] * peers,
+        in_specs=[SMEM] + [VMEM] * (peers + 1),
+        out_specs=[VMEM] * peers,
         scratch_shapes=[
             pltpu.VMEM((rows, width), BF16),
-            pltpu.VMEM((width, 3 * columns), BF16),
             pltpu.VMEM((rows, columns), BF16),
             pltpu.VMEM((rows, columns), BF16),
             pltpu.VMEM((rows // BALL * pairs, 2 * BALL, 2 * PAIR), BF16),
             pltpu.VMEM((rows, columns), BF16),
-            pltpu.SemaphoreType.DMA((3,)),
-            pltpu.SemaphoreType.DMA((peers * cap,)),
         ],
         compiler_params=pltpu.CompilerParams(vmem_limit_bytes=LATER),
         cost_estimate=pl.CostEstimate(
@@ -352,7 +339,7 @@
             transcendentals=rows * BALL * columns // HEAD,
         ),
         name=f"layer_two_{start}",
-    )(recv, *arrived[::-1], w_in)
+    )(recv, *[arrived[s] for s in flow], w_in)
 
 
 def compressed_kernel(slabs, tail, local, *refs):
@@ -448,36 +435,23 @@
 def final_kernel(peers, cap, bounds, pick_ref, *refs):
     parts = len(bounds)
     back = [refs[p * peers : (p + 1) * peers][::-1] for p in range(parts)]
-    w_out, base, out, w_s, b_s, m_s, o_s, sem, block_sem, out_sem = refs[parts * peers :]
-    blocks = b_s.shape[0] // LEAF
+    w_out, base, out, m_s, o_s, out_sem = refs[parts * peers :]
+    blocks = base.shape[0] // LEAF
     me = lax.axis_index("pts").astype(jnp.int32)
-    copies = [
-        pltpu.make_async_copy(w_out, w_s, sem.at[0]),
-        pltpu.make_async_copy(base, b_s, sem.at[1]),
-    ]
-    start_all(copies)
-    moves = []
     for p, (start, columns) in enumerate(bounds):
         for s in range(peers):
             for c in range(cap):
                 block = pick_ref[0, send_to(me, s, peers) * cap + c]
-                found = block < blocks
-                at = pl.ds(c * LEAF, LEAF)
-                place = aligned(jnp.minimum(block, blocks - 1), LEAF)
-                move = pltpu.make_async_copy(
-                    back[p][s].at[at, :],
-                    m_s.at[place, pl.ds(start, columns)],
-                    block_sem.at[(p * peers + s) * cap + c],
-                )
-                moves.append((found, move))
-                pl.when(found)(move.start)
-    wait_all(copies)
-    for found, move in moves:
-        pl.when(found)(move.wait)
+
+                @pl.when(block < blocks)
+                def _():
+                    got = back[p][s][c * LEAF : (c + 1) * LEAF, :]
+                    m_s[aligned(block, LEAF), start : start + columns] = got
+
     outgoing = []
-    for b in range(b_s.shape[0] // CHUNK):
+    for b in range(base.shape[0] // CHUNK):
         rows = slice(b * CHUNK, (b + 1) * CHUNK)
-        o_s[rows, :] = (b_s[rows, :] + dot(m_s[rows, :], w_s[...])).astype(BF16)
+        o_s[rows, :] = (base[rows, :] + dot(m_s[rows, :], w_out[...])).astype(BF16)
         at = pl.ds(b * CHUNK, CHUNK)
         copy = pltpu.make_async_copy(o_s.at[at, :], out.at[at, :], out_sem.at[b])
         copy.start()
@@ -490,15 +464,11 @@
     return pl.pallas_call(
         partial(final_kernel, peers, cap, bounds),
         out_shape=jax.ShapeDtypeStruct((rows, width), BF16),
-        in_specs=[SMEM] + [ANY] * (peers * len(bounds) + 2),
+        in_specs=[SMEM] + [VMEM] * (peers * len(bounds) + 2),
         out_specs=ANY,
         scratch_shapes=[
-            pltpu.VMEM((width, width), BF16),
-            pltpu.VMEM((rows, width), F32),
-            pltpu.VMEM((rows, width), BF16),
-            pltpu.VMEM((rows, width), BF16),
-            pltpu.SemaphoreType.DMA((2,)),
-            pltpu.SemaphoreType.DMA((len(bounds) * peers * cap,)),
+            pltpu.VMEM((rows, width), BF16),
+            pltpu.VMEM((rows, width), BF16),
             pltpu.SemaphoreType.DMA((rows // CHUNK,)),
         ],
         compiler_params=pltpu.CompilerParams(vmem_limit_bytes=LATER),
@@ -542,12 +512,15 @@
 
     z, h, *sends = layer_one(peers, cap, send_pick, ball_ids, gains, points, weights)
     arrived = [travel(sends[s], s, False) for s in range(peers)]
+    flow = [s for s in (2, 1, *range(peers - 1, 2, -1), 0) if s < peers]
     tail = sends[0].shape[0] - cap * LEAF
-    slab = jnp.concatenate([block[cap * LEAF :] for block in arrived])
+    first = [s for s in (1, 2, 3, 0) if s < peers]
+    last = list(range(peers - 1, 3, -1))
+    slab = jnp.concatenate([arrived[s][cap * LEAF :] for s in first + last])
     groups = axes[0][1]
     turns = [[(i, (i + s) % groups) for i in range(groups)] for s in range(1, groups)]
     pools = [slab] + [lax.ppermute(slab, "grp", turn) for turn in turns]
-    mixed = layer_two(peers, cap, 0, width, recv_from, arrived, attn_in_two)
+    mixed = layer_two(peers, cap, flow, 0, width, recv_from, arrived, attn_in_two)
     mixed, pools = lax.optimization_barrier((mixed, pools))
     bounds = [(0, width)]
     back = [travel(mixed[s], s, True) for s in range(peers - 1, -1, -1)]

time: 97.8 us -> 90.7 us (0.927)
  Pallas kernels: 37.8 us -> 32.4 us
    pallas_call x1, Pallas kernels: 10.8 us -> 7.64 us  [layer_two(): pl.pallas_call(partial(layer_two_kernel, peers, cap, flow, blocks, start,...]
    pallas_call x1, Pallas kernels: 3.69 us -> 2.12 us  [final(): pl.pallas_call(partial(final_kernel, peers, cap, bounds), out_shape=jax.S...]
  transfers between devices with their start and end apart: 17 -> 17, of which waited for: 6 -> 6; matrix products, arithmetic and copies ran while one was open for 1% -> 1% of each run, Pallas kernels for 16% -> 14%
where the time goes in v5:
time: 90.7 us; the launch traced here: 90.4 us
  Pallas kernels  32.4 us (36%)
  starting transfers between devices  30.1 us (33%)
  waiting for transfers between devices  25.9 us (29%)
  local copies, waits for them, and re-layouts  1.67 us (2%)
    ppermute x14, waiting for transfers between devices, travel(): return lax.ppermute(blocks, 'pts', pattern)  25.9 us
    ppermute x14, starting transfers between devices, travel(): return lax.ppermute(blocks, 'pts', pattern)  25.7 us
    pallas_call x1, Pallas kernels, layer_one(): pl.pallas_call(partial(layer_one_kernel, peers, cap), out_shape=[whole, w...  17.4 us
    pallas_call x1, Pallas kernels, layer_two(): pl.pallas_call(partial(layer_two_kernel, peers, cap, flow, blocks, start,...  7.64 us
    pallas_call x1, Pallas kernels, compressed(): pl.pallas_call(partial(compressed_kernel, len(pools), tail, local), out_s...  5.22 us
    ppermute x3, starting transfers between devices, shards(): pools = [slab] + [lax.ppermute(slab, 'grp', turn) for turn in turns]  4.44 us
    pallas_call x1, Pallas kernels, final(): pl.pallas_call(partial(final_kernel, peers, cap, bounds), out_shape=jax.S...  2.12 us
  transfers between devices with their start and end apart: 17, of which 6 were waited for; matrix products, arithmetic and copies ran while one was open for 1% of the time, Pallas kernels for 14%

profile of v5, /device:TPU:0, one launch (start us, length us, event | category | flops | bytes accessed | tf_op | source)
XLA Modules:
  0.0 90.4 jit_solution(13764773805475209461)
XLA Ops:
  0.0 17.4 %layer_one.1 = (bf16[1024,512]{1,0:T(8,128)(2,1)}, bf16[1024,512]{1,0:T(8,128)(2,1)}, bf16[144,512]{1,0:T(8,128)(2,1)}, bf16[144,512]{1,0:T(8,128)(2,1)}, bf16[1...) custom-call(s32[1,8]{1,0:T(1,128)} %pick_ref.1, ...), custom_call_target="tpu_custom_call" | custom-call | flops 10737418240 | bytes 10485760 | tf_op jit(solution)/shard_map/layer_one/pallas_call | solution.py:224
  17.4 0.5 collective-permute-start.1
  17.9 2.7 %collective-permute-start = (bf16[144,512]{1,0:T(8,128)(2,1)}, bf16[144,512]{1,0:T(8,128)(2,1)S(1)}, u32[]{:S(2)}, u32[]{:S(2)}) collective-permute-start(bf16[144,512]{1,0:T(8,128)(2,1)} %get-tuple-element.35), channel_id=1, source_target_pairs={{0,2},{1,3},{2,0},{3,1},{4,6},{5,7},{6,4},{7,5},{8,10},{9,11},{10,... | collective-permute-start | bytes 442376 | tf_op jit(solution)/shard_map/ppermute | solution.py:511
  20.6 2.2 %collective-permute-start.2 = (bf16[144,512]{1,0:T(8,128)(2,1)}, bf16[144,512]{1,0:T(8,128)(2,1)S(1)}, u32[]{:S(2)}, u32[]{:S(2)}) collective-permute-start(bf16[144,512]{1,0:T(8,128)(2,1)} %get-tuple-element.37), channel_id=1, source_target_pairs={{0,7},{1,6},{2,5},{3,4},{4,3},{5,2},{6,1},{7,0},{8,15},{9,14},{10,... | collective-permute-start | bytes 442376 | tf_op jit(solution)/shard_map/ppermute | solution.py:511
  22.9 1.3 %collective-permute-start.3 = (bf16[144,512]{1,0:T(8,128)(2,1)}, bf16[144,512]{1,0:T(8,128)(2,1)S(1)}, u32[]{:S(2)}, u32[]{:S(2)}) collective-permute-start(bf16[144,512]{1,0:T(8,128)(2,1)} %get-tuple-element.38), channel_id=1, source_target_pairs={{0,6},{1,7},{2,4},{3,5},{4,2},{5,3},{6,0},{7,1},{8,14},{9,15},{10,... | collective-permute-start | bytes 442376 | tf_op jit(solution)/shard_map/ppermute | solution.py:511
  24.7 2.1 %collective-permute-start.5 = (bf16[144,512]{1,0:T(8,128)(2,1)}, bf16[144,512]{1,0:T(8,128)(2,1)S(1)}, u32[]{:S(2)}, u32[]{:S(2)}) collective-permute-start(bf16[144,512]{1,0:T(8,128)(2,1)} %get-tuple-element.40), channel_id=1, source_target_pairs={{0,4},{1,5},{2,6},{3,7},{4,0},{5,1},{6,2},{7,3},{8,12},{9,13},{10,... | collective-permute-start | bytes 442376 | tf_op jit(solution)/shard_map/ppermute | solution.py:511
  27.1 13.4 %collective-permute-done.6.refs_7_ = bf16[144,512]{1,0:T(8,128)(2,1)S(1)} collective-permute-done((bf16[144,512]{1,0:T(8,128)(2,1)}, bf16[144,512]{1,0:T(8,128)(2,1)S(1)}, u32[]{:S(2)}, u32[]{:S(2)}) %collective-permute-start.6) | collective-permute-done | bytes 147488 | tf_op jit(solution)/shard_map/ppermute | solution.py:511
  40.5 0.7 constant_dynamic-update-slice_fusion.4
  41.2 4.9 %collective-permute-done.4.refs_5_ = bf16[144,512]{1,0:T(8,128)(2,1)S(1)} collective-permute-done((bf16[144,512]{1,0:T(8,128)(2,1)}, bf16[144,512]{1,0:T(8,128)(2,1)S(1)}, u32[]{:S(2)}, u32[]{:S(2)}) %collective-permute-start.4) | collective-permute-done | bytes 147488 | tf_op jit(solution)/shard_map/ppermute | solution.py:511
  46.1 3.6 %collective-permute-done.5.refs_6_ = bf16[144,512]{1,0:T(8,128)(2,1)S(1)} collective-permute-done((bf16[144,512]{1,0:T(8,128)(2,1)}, bf16[144,512]{1,0:T(8,128)(2,1)S(1)}, u32[]{:S(2)}, u32[]{:S(2)}) %collective-permute-start.5) | collective-permute-done | bytes 147488 | tf_op jit(solution)/shard_map/ppermute | solution.py:511
  49.7 1.5 %collective-permute-start.7 = (bf16[128,512]{1,0:T(8,128)(2,1)S(1)}, bf16[128,512]{1,0:T(8,128)(2,1)S(1)}, u32[]{:S(2)}, u32[]{:S(2)}) collective-permute-start(bf16[128,512]{1,0:T(8,128)(2,1)S(1)} %constant_dynamic-update-slice_fusion.refs_0_), channel_id=1, source_target_pairs={{0,8},{8,16},{16,24},{24,0},{1,9},{9,17},{17,25},{25,1},{2,10},{10... | collective-permute-start | bytes 393224 | tf_op jit(solution)/shard_map/ppermute | solution.py:522
  51.2 1.5 %collective-permute-start.8 = (bf16[128,512]{1,0:T(8,128)(2,1)S(1)}, bf16[128,512]{1,0:T(8,128)(2,1)S(1)}, u32[]{:S(2)}, u32[]{:S(2)}) collective-permute-start(bf16[128,512]{1,0:T(8,128)(2,1)S(1)} %constant_dynamic-update-slice_fusion.refs_0_), channel_id=1, source_target_pairs={{0,16},{8,24},{16,0},{24,8},{1,17},{9,25},{17,1},{25,9},{2,18},{10... | collective-permute-start | bytes 393224 | tf_op jit(solution)/shard_map/ppermute | solution.py:522
  52.7 1.4 %collective-permute-start.9 = (bf16[128,512]{1,0:T(8,128)(2,1)S(1)}, bf16[128,512]{1,0:T(8,128)(2,1)S(1)}, u32[]{:S(2)}, u32[]{:S(2)}) collective-permute-start(bf16[128,512]{1,0:T(8,128)(2,1)S(1)} %constant_dynamic-update-slice_fusion.refs_0_), channel_id=1, source_target_pairs={{0,24},{8,0},{16,8},{24,16},{1,25},{9,1},{17,9},{25,17},{2,26},{10... | collective-permute-start | bytes 393224 | tf_op jit(solution)/shard_map/ppermute | solution.py:522
  54.2 0.9 %copy-done.1 = bf16[144,512]{1,0:T(8,128)(2,1)S(1)} copy-done((bf16[144,512]{1,0:T(8,128)(2,1)S(1)}, bf16[144,512]{1,0:T(8,128)(2,1)}, u32[]{:S(2)}) %copy-start.1) | copy-done | bytes 147480
  55.1 7.6 %layer_two_0.1 = (bf16[128,512]{1,0:T(8,128)(2,1)S(1)}, bf16[128,512]{1,0:T(8,128)(2,1)S(1)}, bf16[128,512]{1,0:T(8,128)(2,1)S(1)}, bf16[128,512]{1,0:T(8,128)(2...) custom-call(s32[1,8]{1,0:T(1,128)S(1)} %copy-done.5, ...), custom_call_target="tpu_custom_call" | custom-call | flops 5905580032 | bytes 4194304 | tf_op jit(solution)/shard_map/layer_two_0/pallas_call | solution.py:323
  62.8 1.6 %collective-permute-start.10 = (bf16[128,512]{1,0:T(8,128)(2,1)S(1)}, bf16[128,512]{1,0:T(8,128)(2,1)S(1)}, u32[]{:S(2)}, u32[]{:S(2)}) collective-permute-start(bf16[128,512]{1,0:T(8,128)(2,1)S(1)} %get-tuple-element.51), channel_id=1, source_target_pairs={{7,0},{6,1},{5,2},{4,3},{3,4},{2,5},{1,6},{0,7},{15,8},{14,9},{13,... | collective-permute-start | bytes 393224 | tf_op jit(solution)/shard_map/ppermute | solution.py:511
  64.3 1.5 %collective-permute-start.11 = (bf16[128,512]{1,0:T(8,128)(2,1)S(1)}, bf16[128,512]{1,0:T(8,128)(2,1)S(1)}, u32[]{:S(2)}, u32[]{:S(2)}) collective-permute-start(bf16[128,512]{1,0:T(8,128)(2,1)S(1)} %get-tuple-element.52), channel_id=1, source_target_pairs={{6,0},{7,1},{4,2},{5,3},{2,4},{3,5},{0,6},{1,7},{14,8},{15,9},{12,... | collective-permute-start | bytes 393224 | tf_op jit(solution)/shard_map/ppermute | solution.py:511
  65.8 3.2 %collective-permute-start.13 = (bf16[128,512]{1,0:T(8,128)(2,1)S(1)}, bf16[128,512]{1,0:T(8,128)(2,1)S(1)}, u32[]{:S(2)}, u32[]{:S(2)}) collective-permute-start(bf16[128,512]{1,0:T(8,128)(2,1)S(1)} %get-tuple-element.54), channel_id=1, source_target_pairs={{4,0},{5,1},{6,2},{7,3},{0,4},{1,5},{2,6},{3,7},{12,8},{13,9},{14,... | collective-permute-start | bytes 393224 | tf_op jit(solution)/shard_map/ppermute | solution.py:511
  69.3 1.1 %collective-permute-done.10.refs_0_ = bf16[128,512]{1,0:T(8,128)(2,1)S(1)} collective-permute-done((bf16[128,512]{1,0:T(8,128)(2,1)S(1)}, bf16[128,512]{1,0:T(8,128)(2,1)S(1)}, u32[]{:S(2)}, u32[]{:S(2)}) %collective-permute-start.10) | collective-permute-done | bytes 131104 | tf_op jit(solution)/shard_map/ppermute | solution.py:511
  70.4 9.6 %collective-permute-start.15 = (bf16[128,512]{1,0:T(8,128)(2,1)S(1)}, bf16[128,512]{1,0:T(8,128)(2,1)S(1)}, u32[]{:S(2)}, u32[]{:S(2)}) collective-permute-start(bf16[128,512]{1,0:T(8,128)(2,1)S(1)} %get-tuple-element.56), channel_id=1, source_target_pairs={{2,0},{3,1},{0,2},{1,3},{6,4},{7,5},{4,6},{5,7},{10,8},{11,9},{8,1... | collective-permute-start | bytes 393224 | tf_op jit(solution)/shard_map/ppermute | solution.py:511
  80.0 5.2 %compressed.1.refs_9_ = f32[1024,512]{1,0:T(8,128)S(1)} custom-call(bf16[128,512]{1,0:T(8,128)(2,1)S(1)} %constant_dynamic-update-slice_fusion.refs_0_, bf16[128,512]{1,0:T(8,128)(2,1)S(1)} %collective-permute-done.7.refs_1_, bf16[128,512]{1,0:T(8,128)(2,1)S(1)} %collective-permute-done.8.refs_2_, bf16[128,512]{1,0:T(8,128)(2,1)S(1)} %collective-permute-done.9.refs_3_, ...), custom_call_target="tpu_custom_call" | custom-call | flops 2147483648 | bytes 8388608 | tf_op jit(solution)/shard_map/compressed/pallas_call | solution.py:404
  85.3 1.1 %collective-permute-done.13.refs_3_ = bf16[128,512]{1,0:T(8,128)(2,1)S(1)} collective-permute-done((bf16[128,512]{1,0:T(8,128)(2,1)S(1)}, bf16[128,512]{1,0:T(8,128)(2,1)S(1)}, u32[]{:S(2)}, u32[]{:S(2)}) %collective-permute-start.13) | collective-permute-done | bytes 131104 | tf_op jit(solution)/shard_map/ppermute | solution.py:511
  86.4 1.7 %collective-permute-done.15.refs_5_ = bf16[128,512]{1,0:T(8,128)(2,1)S(1)} collective-permute-done((bf16[128,512]{1,0:T(8,128)(2,1)S(1)}, bf16[128,512]{1,0:T(8,128)(2,1)S(1)}, u32[]{:S(2)}, u32[]{:S(2)}) %collective-permute-start.15) | collective-permute-done | bytes 131104 | tf_op jit(solution)/shard_map/ppermute | solution.py:511
  88.1 2.1 %last_product.1 = bf16[1024,512]{1,0:T(8,128)(2,1)} custom-call(s32[1,8]{1,0:T(1,128)S(1)} %copy-done.2, bf16[128,512]{1,0:T(8,128)(2,1)S(1)} %collective-permute-done.10.refs_0_, bf16[128,512]{1,0:T(8,128)(2,1)S(1)} %collective-permute-done.11.refs_1_, bf16[128,512]{1,0:T(8,128)(2,1)S(1)} %collective-permute-done.12.refs_2_, ...), custom_call_target="tpu_custom_call" | custom-call | flops 536870912 | bytes 4194304 | tf_op jit(solution)/shard_map/last_product/pallas_call | solution.py:464
  (38 shorter events, 1.1 us)
Async XLA Ops:
  0.0 54.2 %copy-start.3 = (bf16[512,1536]{1,0:T(8,128)(2,1)S(1)}, bf16[512,1536]{1,0:T(8,128)(2,1)}, u32[]{:S(2)}) copy-start(bf16[512,1536]{1,0:T(8,128)(2,1)} %refs_7_.3) | copy-start | bytes 4718596
  0.0 54.2 %copy-start.5 = (s32[1,8]{1,0:T(1,128)S(1)}, s32[1,8]{1,0:T(1,128)}, u32[]{:S(2)}) copy-start(s32[1,8]{1,0:T(1,128)} %refs_0_.3) | copy-start | bytes 100
  17.4 7.2 %collective-permute-start.1 = (bf16[144,512]{1,0:T(8,128)(2,1)}, bf16[144,512]{1,0:T(8,128)(2,1)S(1)}, u32[]{:S(2)}, u32[]{:S(2)}) collective-permute-start(bf16[144,512]{1,0:T(8,128)(2,1)} %get-tuple-element.36), channel_id=1, source_target_pairs={{0,1},{1,0},{2,3},{3,2},{4,5},{5,4},{6,7},{7,6},{8,9},{9,8},{10,11... | collective-permute-start | bytes 442376 | tf_op jit(solution)/shard_map/ppermute | solution.py:511
  17.9 8.9 %collective-permute-start = (bf16[144,512]{1,0:T(8,128)(2,1)}, bf16[144,512]{1,0:T(8,128)(2,1)S(1)}, u32[]{:S(2)}, u32[]{:S(2)}) collective-permute-start(bf16[144,512]{1,0:T(8,128)(2,1)} %get-tuple-element.35), channel_id=1, source_target_pairs={{0,2},{1,3},{2,0},{3,1},{4,6},{5,7},{6,4},{7,5},{8,10},{9,11},{10,... | collective-permute-start | bytes 442376 | tf_op jit(solution)/shard_map/ppermute | solution.py:511
  20.6 20.6 %collective-permute-start.2 = (bf16[144,512]{1,0:T(8,128)(2,1)}, bf16[144,512]{1,0:T(8,128)(2,1)S(1)}, u32[]{:S(2)}, u32[]{:S(2)}) collective-permute-start(bf16[144,512]{1,0:T(8,128)(2,1)} %get-tuple-element.37), channel_id=1, source_target_pairs={{0,7},{1,6},{2,5},{3,4},{4,3},{5,2},{6,1},{7,0},{8,15},{9,14},{10,... | collective-permute-start | bytes 442376 | tf_op jit(solution)/shard_map/ppermute | solution.py:511
  22.9 18.4 %collective-permute-start.3 = (bf16[144,512]{1,0:T(8,128)(2,1)}, bf16[144,512]{1,0:T(8,128)(2,1)S(1)}, u32[]{:S(2)}, u32[]{:S(2)}) collective-permute-start(bf16[144,512]{1,0:T(8,128)(2,1)} %get-tuple-element.38), channel_id=1, source_target_pairs={{0,6},{1,7},{2,4},{3,5},{4,2},{5,3},{6,0},{7,1},{8,14},{9,15},{10,... | collective-permute-start | bytes 442376 | tf_op jit(solution)/shard_map/ppermute | solution.py:511
  24.2 21.9 %collective-permute-start.4 = (bf16[144,512]{1,0:T(8,128)(2,1)}, bf16[144,512]{1,0:T(8,128)(2,1)S(1)}, u32[]{:S(2)}, u32[]{:S(2)}) collective-permute-start(bf16[144,512]{1,0:T(8,128)(2,1)} %get-tuple-element.39), channel_id=1, source_target_pairs={{0,5},{1,4},{2,7},{3,6},{4,1},{5,0},{6,3},{7,2},{8,13},{9,12},{10,... | collective-permute-start | bytes 442376 | tf_op jit(solution)/shard_map/ppermute | solution.py:511
  24.7 25.0 %collective-permute-start.5 = (bf16[144,512]{1,0:T(8,128)(2,1)}, bf16[144,512]{1,0:T(8,128)(2,1)S(1)}, u32[]{:S(2)}, u32[]{:S(2)}) collective-permute-start(bf16[144,512]{1,0:T(8,128)(2,1)} %get-tuple-element.40), channel_id=1, source_target_pairs={{0,4},{1,5},{2,6},{3,7},{4,0},{5,1},{6,2},{7,3},{8,12},{9,13},{10,... | collective-permute-start | bytes 442376 | tf_op jit(solution)/shard_map/ppermute | solution.py:511
  26.8 13.7 %collective-permute-start.6 = (bf16[144,512]{1,0:T(8,128)(2,1)}, bf16[144,512]{1,0:T(8,128)(2,1)S(1)}, u32[]{:S(2)}, u32[]{:S(2)}) collective-permute-start(bf16[144,512]{1,0:T(8,128)(2,1)} %get-tuple-element.41), channel_id=1, source_target_pairs={{0,3},{1,2},{2,1},{3,0},{4,7},{5,6},{6,5},{7,4},{8,11},{9,10},{10,... | collective-permute-start | bytes 442376 | tf_op jit(solution)/shard_map/ppermute | solution.py:511
  49.7 30.3 %copy-start = (bf16[512,512]{1,0:T(8,128)(2,1)S(1)}, bf16[512,512]{1,0:T(8,128)(2,1)}, u32[]{:S(2)}) copy-start(bf16[512,512]{1,0:T(8,128)(2,1)} %refs_8_.5) | copy-start | bytes 1572868
  49.7 13.0 %collective-permute-start.7 = (bf16[128,512]{1,0:T(8,128)(2,1)S(1)}, bf16[128,512]{1,0:T(8,128)(2,1)S(1)}, u32[]{:S(2)}, u32[]{:S(2)}) collective-permute-start(bf16[128,512]{1,0:T(8,128)(2,1)S(1)} %constant_dynamic-update-slice_fusion.refs_0_), channel_id=1, source_target_pairs={{0,8},{8,16},{16,24},{24,0},{1,9},{9,17},{17,25},{25,1},{2,10},{10... | collective-permute-start | bytes 393224 | tf_op jit(solution)/shard_map/ppermute | solution.py:522
  51.2 11.5 %collective-permute-start.8 = (bf16[128,512]{1,0:T(8,128)(2,1)S(1)}, bf16[128,512]{1,0:T(8,128)(2,1)S(1)}, u32[]{:S(2)}, u32[]{:S(2)}) collective-permute-start(bf16[128,512]{1,0:T(8,128)(2,1)S(1)} %constant_dynamic-update-slice_fusion.refs_0_), channel_id=1, source_target_pairs={{0,16},{8,24},{16,0},{24,8},{1,17},{9,25},{17,1},{25,9},{2,18},{10... | collective-permute-start | bytes 393224 | tf_op jit(solution)/shard_map/ppermute | solution.py:522
  52.7 10.0 %collective-permute-start.9 = (bf16[128,512]{1,0:T(8,128)(2,1)S(1)}, bf16[128,512]{1,0:T(8,128)(2,1)S(1)}, u32[]{:S(2)}, u32[]{:S(2)}) collective-permute-start(bf16[128,512]{1,0:T(8,128)(2,1)S(1)} %constant_dynamic-update-slice_fusion.refs_0_), channel_id=1, source_target_pairs={{0,24},{8,0},{16,8},{24,16},{1,25},{9,1},{17,9},{25,17},{2,26},{10... | collective-permute-start | bytes 393224 | tf_op jit(solution)/shard_map/ppermute | solution.py:522
  55.1 24.9 %copy-start.4 = (bf16[512,1024]{1,0:T(8,128)(2,1)S(1)}, bf16[512,1024]{1,0:T(8,128)(2,1)}, u32[]{:S(2)}) copy-start(bf16[512,1024]{1,0:T(8,128)(2,1)} %refs_6_.3) | copy-start | bytes 3145732
  55.1 24.9 %copy-start.6 = (bf16[1024,512]{1,0:T(8,128)(2,1)S(1)}, bf16[1024,512]{1,0:T(8,128)(2,1)}, u32[]{:S(2)}) copy-start(bf16[1024,512]{1,0:T(8,128)(2,1)} %get-tuple-element.64.refs_5_) | copy-start | bytes 3145732
  55.1 24.9 %copy-start.7 = (bf16[1024,512]{1,0:T(8,128)(2,1)S(1)}, bf16[1024,512]{1,0:T(8,128)(2,1)}, u32[]{:S(2)}) copy-start(bf16[1024,512]{1,0:T(8,128)(2,1)} %get-tuple-element.63.refs_4_) | copy-start | bytes 3145732
  62.8 7.7 %collective-permute-start.10 = (bf16[128,512]{1,0:T(8,128)(2,1)S(1)}, bf16[128,512]{1,0:T(8,128)(2,1)S(1)}, u32[]{:S(2)}, u32[]{:S(2)}) collective-permute-start(bf16[128,512]{1,0:T(8,128)(2,1)S(1)} %get-tuple-element.51), channel_id=1, source_target_pairs={{7,0},{6,1},{5,2},{4,3},{3,4},{2,5},{1,6},{0,7},{15,8},{14,9},{13,... | collective-permute-start | bytes 393224 | tf_op jit(solution)/shard_map/ppermute | solution.py:511
  64.3 15.7 %collective-permute-start.11 = (bf16[128,512]{1,0:T(8,128)(2,1)S(1)}, bf16[128,512]{1,0:T(8,128)(2,1)S(1)}, u32[]{:S(2)}, u32[]{:S(2)}) collective-permute-start(bf16[128,512]{1,0:T(8,128)(2,1)S(1)} %get-tuple-element.52), channel_id=1, source_target_pairs={{6,0},{7,1},{4,2},{5,3},{2,4},{3,5},{0,6},{1,7},{14,8},{15,9},{12,... | collective-permute-start | bytes 393224 | tf_op jit(solution)/shard_map/ppermute | solution.py:511
  65.8 19.5 %collective-permute-start.12 = (bf16[128,512]{1,0:T(8,128)(2,1)S(1)}, bf16[128,512]{1,0:T(8,128)(2,1)S(1)}, u32[]{:S(2)}, u32[]{:S(2)}) collective-permute-start(bf16[128,512]{1,0:T(8,128)(2,1)S(1)} %get-tuple-element.53), channel_id=1, source_target_pairs={{5,0},{4,1},{7,2},{6,3},{1,4},{0,5},{3,6},{2,7},{13,8},{12,9},{15,... | collective-permute-start | bytes 393224 | tf_op jit(solution)/shard_map/ppermute | solution.py:511
  65.8 20.6 %collective-permute-start.13 = (bf16[128,512]{1,0:T(8,128)(2,1)S(1)}, bf16[128,512]{1,0:T(8,128)(2,1)S(1)}, u32[]{:S(2)}, u32[]{:S(2)}) collective-permute-start(bf16[128,512]{1,0:T(8,128)(2,1)S(1)} %get-tuple-element.54), channel_id=1, source_target_pairs={{4,0},{5,1},{6,2},{7,3},{0,4},{1,5},{2,6},{3,7},{12,8},{13,9},{14,... | collective-permute-start | bytes 393224 | tf_op jit(solution)/shard_map/ppermute | solution.py:511
  69.0 17.4 %collective-permute-start.14 = (bf16[128,512]{1,0:T(8,128)(2,1)S(1)}, bf16[128,512]{1,0:T(8,128)(2,1)S(1)}, u32[]{:S(2)}, u32[]{:S(2)}) collective-permute-start(bf16[128,512]{1,0:T(8,128)(2,1)S(1)} %get-tuple-element.55), channel_id=1, source_target_pairs={{3,0},{2,1},{1,2},{0,3},{7,4},{6,5},{5,6},{4,7},{11,8},{10,9},{9,1... | collective-permute-start | bytes 393224 | tf_op jit(solution)/shard_map/ppermute | solution.py:511
  70.4 17.7 %collective-permute-start.15 = (bf16[128,512]{1,0:T(8,128)(2,1)S(1)}, bf16[128,512]{1,0:T(8,128)(2,1)S(1)}, u32[]{:S(2)}, u32[]{:S(2)}) collective-permute-start(bf16[128,512]{1,0:T(8,128)(2,1)S(1)} %get-tuple-element.56), channel_id=1, source_target_pairs={{2,0},{3,1},{0,2},{1,3},{6,4},{7,5},{4,6},{5,7},{10,8},{11,9},{8,1... | collective-permute-start | bytes 393224 | tf_op jit(solution)/shard_map/ppermute | solution.py:511
  80.0 8.1 %collective-permute-start.16 = (bf16[128,512]{1,0:T(8,128)(2,1)S(1)}, bf16[128,512]{1,0:T(8,128)(2,1)S(1)}, u32[]{:S(2)}, u32[]{:S(2)}) collective-permute-start(bf16[128,512]{1,0:T(8,128)(2,1)S(1)} %get-tuple-element.57), channel_id=1, source_target_pairs={{1,0},{0,1},{3,2},{2,3},{5,4},{4,5},{7,6},{6,7},{9,8},{8,9},{11,10... | collective-permute-start | bytes 393224 | tf_op jit(solution)/shard_map/ppermute | solution.py:511
  80.0 8.1 %copy-start.2 = (s32[1,8]{1,0:T(1,128)S(1)}, s32[1,8]{1,0:T(1,128)}, u32[]{:S(2)}) copy-start(s32[1,8]{1,0:T(1,128)} %pick_ref.1) | copy-start | bytes 100
  (1 other events, 0.9 us)

commit v6 on v5

--- a/solution.py
+++ b/solution.py
@@ -132,29 +132,41 @@
     pairs = width // PAIR
     blocks = count // LEAF
     copies = [
-        pltpu.make_async_copy(points, x_s, sem.at[0]),
-        pltpu.make_async_copy(w_in, in_s, sem.at[1]),
-        pltpu.make_async_copy(w_out, wo_s, sem.at[2]),
-        pltpu.make_async_copy(w_up, up_s, sem.at[3]),
-        pltpu.make_async_copy(w_down, down_s, sem.at[4]),
+        pltpu.make_async_copy(w_out, wo_s, sem.at[0]),
+        pltpu.make_async_copy(w_up, up_s, sem.at[1]),
+        pltpu.make_async_copy(w_down, down_s, sem.at[2]),
     ]
-    start_all(copies[:2])
+    thirds, balls_in = [], []
+    for i in range(3):
+        cols = pl.ds(i * width, width)
+        thirds.append(pltpu.make_async_copy(w_in.at[:, cols], in_s.at[:, cols], sem.at[3 + i]))
+    for b in range(balls):
+        at = pl.ds(b * BALL, BALL)
+        balls_in.append(pltpu.make_async_copy(points.at[at, :], x_s.at[at, :], sem.at[6 + 3 * b]))
+    balls_in[0].start()
+    start_all(thirds)
+    start_all(balls_in[1:])
     for b in range(balls):
         across = jnp.broadcast_to(ids[b : b + 1, :], (LEAF, BALL)).astype(F32)
         down = across.T
         for c in range(BALL // LEAF):
             cols = slice(c * LEAF, (c + 1) * LEAF)
             bias_s[b, :, cols] = jnp.where(down == across[:1, cols], 0.0, -1e30)
-    copies[0].wait()
     for b in range(balls):
         rows = slice(b * BALL, (b + 1) * BALL)
+        balls_in[b].wait()
         h1 = norm(x_s[rows, :], gain1[...]).astype(BF16)
+
+        def product(i):
+            if b == 0:
+                thirds[i].wait()
+            return dot(h1, in_s[:, i * width : (i + 1) * width])
+
+        q_s[rows, :] = (product(0) * SCALE).astype(BF16)
+        k_s[rows, :] = product(1).astype(BF16)
+        values = product(2).astype(BF16)
         if b == 0:
-            copies[1].wait()
-            start_all(copies[2:])
-        q_s[rows, :] = (dot(h1, in_s[:, :width]) * SCALE).astype(BF16)
-        k_s[rows, :] = dot(h1, in_s[:, width : 2 * width]).astype(BF16)
-        values = dot(h1, in_s[:, 2 * width :]).astype(BF16)
+            start_all(copies)
         for g in range(pairs):
             lay_values(v_s.at[b * pairs + g], values[:, g * PAIR : (g + 1) * PAIR])
 
@@ -174,12 +186,12 @@
     pipelined(
         [(b, g, c) for b in range(balls) for g in range(pairs) for c in range(BALL // CHUNK)], scores, mix
     )
-    copies[2].wait()
+    copies[0].wait()
     for b in range(balls):
         rows = slice(b * BALL, (b + 1) * BALL)
         y_s[rows, :] = (x_s[rows, :].astype(F32) + dot(mix_s[rows, :], wo_s[...])).astype(BF16)
-    copies[3].wait()
-    copies[4].wait()
+    copies[1].wait()
+    copies[2].wait()
     outgoing, pooled = [], []
     for b in range(balls):
         rows = slice(b * BALL, (b + 1) * BALL)
@@ -191,7 +203,7 @@
             pooled.append(jnp.sum(wide[c * CMP : (c + 1) * CMP], axis=0, keepdims=True) * CMP ** (-0.5))
         at = pl.ds(b * BALL, BALL)
         for n, (source, there) in enumerate(((z_s, z_out), (h_s, h_out))):
-            copy = pltpu.make_async_copy(source.at[at, :], there.at[at, :], sem.at[5 + 2 * b + n])
+            copy = pltpu.make_async_copy(source.at[at, :], there.at[at, :], sem.at[7 + 3 * b + n])
             copy.start()
             outgoing.append(copy)
     row = lax.broadcasted_iota(jnp.int32, p_s.shape, 0)
@@ -241,7 +253,7 @@
             pltpu.VMEM((count, width), BF16),
             pltpu.VMEM((count, width), BF16),
             pltpu.VMEM((tail, width), BF16),
-            pltpu.SemaphoreType.DMA((5 + 2 * balls,)),
+            pltpu.SemaphoreType.DMA((6 + 3 * balls,)),
             pltpu.SemaphoreType.DMA((peers * (cap + 1),)),
         ],
         compiler_params=pltpu.CompilerParams(vmem_limit_bytes=60 * MIB),
@@ -511,19 +523,28 @@
         return lax.ppermute(blocks, "pts", pattern)
 
     z, h, *sends = layer_one(peers, cap, send_pick, ball_ids, gains, points, weights)
+    sends[0] = jnp.where(recv_from[0, 0] >= 0, sends[0], jnp.zeros_like(sends[0]))
     arrived = [travel(sends[s], s, False) for s in range(peers)]
-    flow = [s for s in (2, 1, *range(peers - 1, 2, -1), 0) if s < peers]
+    flow = [*range(peers - 1, 4, -1), *(s for s in (2, 1, 4, 3, 0) if s < peers)]
     tail = sends[0].shape[0] - cap * LEAF
     first = [s for s in (1, 2, 3, 0) if s < peers]
     last = list(range(peers - 1, 3, -1))
     slab = jnp.concatenate([arrived[s][cap * LEAF :] for s in first + last])
     groups = axes[0][1]
-    turns = [[(i, (i + s) % groups) for i in range(groups)] for s in range(1, groups)]
+    doubles = groups & (groups - 1) == 0
+    turns = [[(i, i ^ 1) for i in range(groups)]] if doubles and groups > 1 else []
+    if not doubles:
+        turns = [[(i, (i + s) % groups) for i in range(groups)] for s in range(1, groups)]
     pools = [slab] + [lax.ppermute(slab, "grp", turn) for turn in turns]
     mixed = layer_two(peers, cap, flow, 0, width, recv_from, arrived, attn_in_two)
     mixed, pools = lax.optimization_barrier((mixed, pools))
     bounds = [(0, width)]
     back = [travel(mixed[s], s, True) for s in range(peers - 1, -1, -1)]
+    bit = 2
+    while doubles and bit < groups:
+        both = jnp.concatenate(pools)
+        pools = [both, lax.ppermute(both, "grp", [(i, i ^ bit) for i in range(groups)])]
+        bit *= 2
     local = points.shape[0] // CMP
     base = compressed(tail, local, pools, h, z, compress_proj, attn_in_two, attn_out_two)
     return final(peers, cap, bounds, send_pick, back, attn_out_two, base)

time: 90.7 us -> 90 us (level)
  local copies, waits for them, and re-layouts: 1.67 us -> 0.08 us
  waiting for transfers between devices: 25.9 us -> 27.2 us
  other arithmetic: 0 us -> 0.93 us
    ppermute x3 -> x1, starting transfers between devices: 4.44 us -> 1.51 us  [shards(): pools = [slab] + [lax.ppermute(slab, 'grp', turn) for turn in turns]]
    unnamed x23 -> x22, local copies, waits for them, and re-layouts: 1.67 us -> 0.07 us
    ppermute x0 -> x1, starting transfers between devices: none -> 1.58 us  [shards(): lax.ppermute(both, 'grp', [(i, i ^ bit) for i in range(groups)])]
    ppermute x14, waiting for transfers between devices: 25.9 us -> 27.2 us  [travel(): return lax.ppermute(blocks, 'pts', pattern)]
    select_n x0 -> x1, other arithmetic: none -> 0.93 us  [shards(): jnp.where(recv_from[0, 0] >= 0, sends[0], jnp.zeros_like(sends[0]))]
  transfers between devices with their start and end apart: 17 -> 16, of which waited for: 6 -> 6; matrix products, arithmetic and copies ran while one was open for 1% -> 1% of each run, Pallas kernels for 14% -> 14%
where the time goes in v6:
time: 90 us; the launch traced here: 89.8 us
  Pallas kernels  31.7 us (35%)
  starting transfers between devices  29.5 us (33%)
  waiting for transfers between devices  27.2 us (30%)
  other arithmetic  0.93 us (1%)
    ppermute x14, waiting for transfers between devices, travel(): return lax.ppermute(blocks, 'pts', pattern)  27.2 us
    ppermute x14, starting transfers between devices, travel(): return lax.ppermute(blocks, 'pts', pattern)  26.4 us
    pallas_call x1, Pallas kernels, layer_one(): pl.pallas_call(partial(layer_one_kernel, peers, cap), out_shape=[whole, w...  17.4 us
    pallas_call x1, Pallas kernels, layer_two(): pl.pallas_call(partial(layer_two_kernel, peers, cap, flow, blocks, start,...  7.64 us
    pallas_call x1, Pallas kernels, compressed(): pl.pallas_call(partial(compressed_kernel, len(pools), tail, local), out_s...  4.55 us
    pallas_call x1, Pallas kernels, final(): pl.pallas_call(partial(final_kernel, peers, cap, bounds), out_shape=jax.S...  2.12 us
  transfers between devices with their start and end apart: 16, of which 6 were waited for; matrix products, arithmetic and copies ran while one was open for 1% of the time, Pallas kernels for 14%

profile of v6, /device:TPU:0, one launch (start us, length us, event | category | flops | bytes accessed | tf_op | source)
XLA Modules:
  0.0 89.8 jit_solution(6614979771583873550)
XLA Ops:
  0.0 17.4 %layer_one.1 = (bf16[1024,512]{1,0:T(8,128)(2,1)}, bf16[1024,512]{1,0:T(8,128)(2,1)}, bf16[144,512]{1,0:T(8,128)(2,1)}, bf16[144,512]{1,0:T(8,128)(2,1)}, bf16[1...) custom-call(s32[1,8]{1,0:T(1,128)} %pick_ref.1, ...), custom_call_target="tpu_custom_call" | custom-call | flops 10737418240 | bytes 10485760 | tf_op jit(solution)/shard_map/layer_one/pallas_call | solution.py:236
  17.4 4.6 %collective-permute-start = (bf16[144,512]{1,0:T(8,128)(2,1)}, bf16[144,512]{1,0:T(8,128)(2,1)S(1)}, u32[]{:S(2)}, u32[]{:S(2)}) collective-permute-start(bf16[144,512]{1,0:T(8,128)(2,1)} %get-tuple-element.33), channel_id=1, source_target_pairs={{0,7},{1,6},{2,5},{3,4},{4,3},{5,2},{6,1},{7,0},{8,15},{9,14},{10,... | collective-permute-start | bytes 442376 | tf_op jit(solution)/shard_map/ppermute | solution.py:523
  22.0 0.7 collective-permute-start.1
  22.6 0.4 collective-permute-start.2
  23.0 3.4 %collective-permute-start.3 = (bf16[144,512]{1,0:T(8,128)(2,1)}, bf16[144,512]{1,0:T(8,128)(2,1)S(1)}, u32[]{:S(2)}, u32[]{:S(2)}) collective-permute-start(bf16[144,512]{1,0:T(8,128)(2,1)} %get-tuple-element.36), channel_id=1, source_target_pairs={{0,2},{1,3},{2,0},{3,1},{4,6},{5,7},{6,4},{7,5},{8,10},{9,11},{10,... | collective-permute-start | bytes 442376 | tf_op jit(solution)/shard_map/ppermute | solution.py:523
  26.4 0.9 %broadcast_select_fusion.refs_8_ = bf16[144,512]{1,0:T(8,128)(2,1)S(1)} fusion(bf16[144,512]{1,0:T(8,128)(2,1)} %get-tuple-element.40, pred[]{:T(512)} %bitcast.3), kind=kLoop, calls=%fused_computation | loop fusion | flops 73728 | bytes 294913 | tf_op jit(solution)/shard_map/jit(_where)/select_n | solution.py:526
  27.4 0.6 collective-permute-done.4.refs_5_
  28.0 8.1 %collective-permute-done.3.refs_4_ = bf16[144,512]{1,0:T(8,128)(2,1)S(1)} collective-permute-done((bf16[144,512]{1,0:T(8,128)(2,1)}, bf16[144,512]{1,0:T(8,128)(2,1)S(1)}, u32[]{:S(2)}, u32[]{:S(2)}) %collective-permute-start.3) | collective-permute-done | bytes 147488 | tf_op jit(solution)/shard_map/ppermute | solution.py:523
  36.1 2.1 %collective-permute-start.6 = (bf16[144,512]{1,0:T(8,128)(2,1)}, bf16[144,512]{1,0:T(8,128)(2,1)S(1)}, u32[]{:S(2)}, u32[]{:S(2)}) collective-permute-start(bf16[144,512]{1,0:T(8,128)(2,1)} %get-tuple-element.39), channel_id=1, source_target_pairs={{0,3},{1,2},{2,1},{3,0},{4,7},{5,6},{6,5},{7,4},{8,11},{9,10},{10,... | collective-permute-start | bytes 442376 | tf_op jit(solution)/shard_map/ppermute | solution.py:523
  38.2 10.4 %collective-permute-done.6.refs_7_ = bf16[144,512]{1,0:T(8,128)(2,1)S(1)} collective-permute-done((bf16[144,512]{1,0:T(8,128)(2,1)}, bf16[144,512]{1,0:T(8,128)(2,1)S(1)}, u32[]{:S(2)}, u32[]{:S(2)}) %collective-permute-start.6) | collective-permute-done | bytes 147488 | tf_op jit(solution)/shard_map/ppermute | solution.py:523
  48.7 0.0 copy-start.5
  48.7 1.5 %collective-permute-start.7 = (bf16[128,512]{1,0:T(8,128)(2,1)S(1)}, bf16[128,512]{1,0:T(8,128)(2,1)S(1)}, u32[]{:S(2)}, u32[]{:S(2)}) collective-permute-start(bf16[128,512]{1,0:T(8,128)(2,1)S(1)} %constant_dynamic-update-slice_fusion), channel_id=1, source_target_pairs={{0,8},{8,0},{16,24},{24,16},{1,9},{9,1},{17,25},{25,17},{2,10},{10... | collective-permute-start | bytes 393224 | tf_op jit(solution)/shard_map/ppermute | solution.py:538
  50.3 7.6 %layer_two_0.1 = (bf16[128,512]{1,0:T(8,128)(2,1)S(1)}, bf16[128,512]{1,0:T(8,128)(2,1)S(1)}, bf16[128,512]{1,0:T(8,128)(2,1)S(1)}, bf16[128,512]{1,0:T(8,128)(2...) custom-call(s32[1,8]{1,0:T(1,128)S(1)} %copy-done.4, ...), custom_call_target="tpu_custom_call" | custom-call | flops 5905580032 | bytes 4194304 | tf_op jit(solution)/shard_map/layer_two_0/pallas_call | solution.py:335
  57.9 1.6 %collective-permute-start.15 = (bf16[256,512]{1,0:T(8,128)(2,1)S(1)}, bf16[256,512]{1,0:T(8,128)(2,1)S(1)}, u32[]{:S(2)}, u32[]{:S(2)}) collective-permute-start(bf16[256,512]{1,0:T(8,128)(2,1)S(1)} %constant_dynamic-update-slice_fusion.8.refs_0_), channel_id=1, source_target_pairs={{0,16},{8,24},{16,0},{24,8},{1,17},{9,25},{17,1},{25,9},{2,18},{10... | collective-permute-start | bytes 786440 | tf_op jit(solution)/shard_map/ppermute | solution.py:546
  59.5 1.4 %collective-permute-start.8 = (bf16[128,512]{1,0:T(8,128)(2,1)S(1)}, bf16[128,512]{1,0:T(8,128)(2,1)S(1)}, u32[]{:S(2)}, u32[]{:S(2)}) collective-permute-start(bf16[128,512]{1,0:T(8,128)(2,1)S(1)} %get-tuple-element.49), channel_id=1, source_target_pairs={{7,0},{6,1},{5,2},{4,3},{3,4},{2,5},{1,6},{0,7},{15,8},{14,9},{13,... | collective-permute-start | bytes 393224 | tf_op jit(solution)/shard_map/ppermute | solution.py:523
  60.9 1.9 %collective-permute-start.9 = (bf16[128,512]{1,0:T(8,128)(2,1)S(1)}, bf16[128,512]{1,0:T(8,128)(2,1)S(1)}, u32[]{:S(2)}, u32[]{:S(2)}) collective-permute-start(bf16[128,512]{1,0:T(8,128)(2,1)S(1)} %get-tuple-element.50), channel_id=1, source_target_pairs={{6,0},{7,1},{4,2},{5,3},{2,4},{3,5},{0,6},{1,7},{14,8},{15,9},{12,... | collective-permute-start | bytes 393224 | tf_op jit(solution)/shard_map/ppermute | solution.py:523
  62.7 3.0 %collective-permute-start.11 = (bf16[128,512]{1,0:T(8,128)(2,1)S(1)}, bf16[128,512]{1,0:T(8,128)(2,1)S(1)}, u32[]{:S(2)}, u32[]{:S(2)}) collective-permute-start(bf16[128,512]{1,0:T(8,128)(2,1)S(1)} %get-tuple-element.52), channel_id=1, source_target_pairs={{4,0},{5,1},{6,2},{7,3},{0,4},{1,5},{2,6},{3,7},{12,8},{13,9},{14,... | collective-permute-start | bytes 393224 | tf_op jit(solution)/shard_map/ppermute | solution.py:523
  65.7 1.5 %collective-permute-done.8.refs_0_ = bf16[128,512]{1,0:T(8,128)(2,1)S(1)} collective-permute-done((bf16[128,512]{1,0:T(8,128)(2,1)S(1)}, bf16[128,512]{1,0:T(8,128)(2,1)S(1)}, u32[]{:S(2)}, u32[]{:S(2)}) %collective-permute-start.8) | collective-permute-done | bytes 131104 | tf_op jit(solution)/shard_map/ppermute | solution.py:523
  67.2 2.7 %collective-permute-done.9.refs_1_ = bf16[128,512]{1,0:T(8,128)(2,1)S(1)} collective-permute-done((bf16[128,512]{1,0:T(8,128)(2,1)S(1)}, bf16[128,512]{1,0:T(8,128)(2,1)S(1)}, u32[]{:S(2)}, u32[]{:S(2)}) %collective-permute-start.9) | collective-permute-done | bytes 131104 | tf_op jit(solution)/shard_map/ppermute | solution.py:523
  70.0 7.7 %collective-permute-start.13 = (bf16[128,512]{1,0:T(8,128)(2,1)S(1)}, bf16[128,512]{1,0:T(8,128)(2,1)S(1)}, u32[]{:S(2)}, u32[]{:S(2)}) collective-permute-start(bf16[128,512]{1,0:T(8,128)(2,1)S(1)} %get-tuple-element.54), channel_id=1, source_target_pairs={{2,0},{3,1},{0,2},{1,3},{6,4},{7,5},{4,6},{5,7},{10,8},{11,9},{8,1... | collective-permute-start | bytes 393224 | tf_op jit(solution)/shard_map/ppermute | solution.py:523
  77.6 1.5 %collective-permute-start.14 = (bf16[128,512]{1,0:T(8,128)(2,1)S(1)}, bf16[128,512]{1,0:T(8,128)(2,1)S(1)}, u32[]{:S(2)}, u32[]{:S(2)}) collective-permute-start(bf16[128,512]{1,0:T(8,128)(2,1)S(1)} %get-tuple-element.55), channel_id=1, source_target_pairs={{1,0},{0,1},{3,2},{2,3},{5,4},{4,5},{7,6},{6,7},{9,8},{8,9},{11,10... | collective-permute-start | bytes 393224 | tf_op jit(solution)/shard_map/ppermute | solution.py:523
  79.1 4.6 %compressed.1.refs_9_ = f32[1024,512]{1,0:T(8,128)S(1)} custom-call(bf16[256,512]{1,0:T(8,128)(2,1)S(1)} %constant_dynamic-update-slice_fusion.8.refs_0_, bf16[256,512]{1,0:T(8,128)(2,1)S(1)} %collective-permute-done.15.refs_1_, bf16[1024,512]{1,0:T(8,128)(2,1)S(1)} %copy-done.6, bf16[1024,512]{1,0:T(8,128)(2,1)S(1)} %copy-done.5, ...), custom_call_target="tpu_custom_call" | custom-call | flops 2147483648 | bytes 8388608 | tf_op jit(solution)/shard_map/compressed/pallas_call | solution.py:416
  83.7 3.8 %collective-permute-done.13.refs_5_ = bf16[128,512]{1,0:T(8,128)(2,1)S(1)} collective-permute-done((bf16[128,512]{1,0:T(8,128)(2,1)S(1)}, bf16[128,512]{1,0:T(8,128)(2,1)S(1)}, u32[]{:S(2)}, u32[]{:S(2)}) %collective-permute-start.13) | collective-permute-done | bytes 131104 | tf_op jit(solution)/shard_map/ppermute | solution.py:523
  87.5 2.1 %last_product.1 = bf16[1024,512]{1,0:T(8,128)(2,1)} custom-call(s32[1,8]{1,0:T(1,128)S(1)} %copy-done.1, bf16[128,512]{1,0:T(8,128)(2,1)S(1)} %collective-permute-done.8.refs_0_, bf16[128,512]{1,0:T(8,128)(2,1)S(1)} %collective-permute-done.9.refs_1_, bf16[128,512]{1,0:T(8,128)(2,1)S(1)} %collective-permute-done.10.refs_2_, ...), custom_call_target="tpu_custom_call" | custom-call | flops 536870912 | bytes 4194304 | tf_op jit(solution)/shard_map/last_product/pallas_call | solution.py:476
  (37 shorter events, 0.1 us)
Async XLA Ops:
  0.0 26.4 %copy-start.4 = (s32[1,8]{1,0:T(1,128)S(1)}, s32[1,8]{1,0:T(1,128)}, u32[]{:S(2)}) copy-start(s32[1,8]{1,0:T(1,128)} %refs_0_.3) | copy-start | bytes 100
  0.0 50.2 %copy-start.2 = (bf16[512,1536]{1,0:T(8,128)(2,1)S(1)}, bf16[512,1536]{1,0:T(8,128)(2,1)}, u32[]{:S(2)}) copy-start(bf16[512,1536]{1,0:T(8,128)(2,1)} %refs_5_.3) | copy-start | bytes 4718596
  17.4 31.2 %collective-permute-start = (bf16[144,512]{1,0:T(8,128)(2,1)}, bf16[144,512]{1,0:T(8,128)(2,1)S(1)}, u32[]{:S(2)}, u32[]{:S(2)}) collective-permute-start(bf16[144,512]{1,0:T(8,128)(2,1)} %get-tuple-element.33), channel_id=1, source_target_pairs={{0,7},{1,6},{2,5},{3,4},{4,3},{5,2},{6,1},{7,0},{8,15},{9,14},{10,... | collective-permute-start | bytes 442376 | tf_op jit(solution)/shard_map/ppermute | solution.py:523
  22.0 26.7 %collective-permute-start.1 = (bf16[144,512]{1,0:T(8,128)(2,1)}, bf16[144,512]{1,0:T(8,128)(2,1)S(1)}, u32[]{:S(2)}, u32[]{:S(2)}) collective-permute-start(bf16[144,512]{1,0:T(8,128)(2,1)} %get-tuple-element.34), channel_id=1, source_target_pairs={{0,6},{1,7},{2,4},{3,5},{4,2},{5,3},{6,0},{7,1},{8,14},{9,15},{10,... | collective-permute-start | bytes 442376 | tf_op jit(solution)/shard_map/ppermute | solution.py:523
  22.6 26.0 %collective-permute-start.2 = (bf16[144,512]{1,0:T(8,128)(2,1)}, bf16[144,512]{1,0:T(8,128)(2,1)S(1)}, u32[]{:S(2)}, u32[]{:S(2)}) collective-permute-start(bf16[144,512]{1,0:T(8,128)(2,1)} %get-tuple-element.35), channel_id=1, source_target_pairs={{0,5},{1,4},{2,7},{3,6},{4,1},{5,0},{6,3},{7,2},{8,13},{9,12},{10,... | collective-permute-start | bytes 442376 | tf_op jit(solution)/shard_map/ppermute | solution.py:523
  23.0 13.1 %collective-permute-start.3 = (bf16[144,512]{1,0:T(8,128)(2,1)}, bf16[144,512]{1,0:T(8,128)(2,1)S(1)}, u32[]{:S(2)}, u32[]{:S(2)}) collective-permute-start(bf16[144,512]{1,0:T(8,128)(2,1)} %get-tuple-element.36), channel_id=1, source_target_pairs={{0,2},{1,3},{2,0},{3,1},{4,6},{5,7},{6,4},{7,5},{8,10},{9,11},{10,... | collective-permute-start | bytes 442376 | tf_op jit(solution)/shard_map/ppermute | solution.py:523
  26.4 1.6 %collective-permute-start.4 = (bf16[144,512]{1,0:T(8,128)(2,1)}, bf16[144,512]{1,0:T(8,128)(2,1)S(1)}, u32[]{:S(2)}, u32[]{:S(2)}) collective-permute-start(bf16[144,512]{1,0:T(8,128)(2,1)} %get-tuple-element.37), channel_id=1, source_target_pairs={{0,1},{1,0},{2,3},{3,2},{4,5},{5,4},{6,7},{7,6},{8,9},{9,8},{10,11... | collective-permute-start | bytes 442376 | tf_op jit(solution)/shard_map/ppermute | solution.py:523
  28.0 20.7 %collective-permute-start.5 = (bf16[144,512]{1,0:T(8,128)(2,1)}, bf16[144,512]{1,0:T(8,128)(2,1)S(1)}, u32[]{:S(2)}, u32[]{:S(2)}) collective-permute-start(bf16[144,512]{1,0:T(8,128)(2,1)} %get-tuple-element.38), channel_id=1, source_target_pairs={{0,4},{1,5},{2,6},{3,7},{4,0},{5,1},{6,2},{7,3},{8,12},{9,13},{10,... | collective-permute-start | bytes 442376 | tf_op jit(solution)/shard_map/ppermute | solution.py:523
  36.1 12.5 %collective-permute-start.6 = (bf16[144,512]{1,0:T(8,128)(2,1)}, bf16[144,512]{1,0:T(8,128)(2,1)S(1)}, u32[]{:S(2)}, u32[]{:S(2)}) collective-permute-start(bf16[144,512]{1,0:T(8,128)(2,1)} %get-tuple-element.39), channel_id=1, source_target_pairs={{0,3},{1,2},{2,1},{3,0},{4,7},{5,6},{6,5},{7,4},{8,11},{9,10},{10,... | collective-permute-start | bytes 442376 | tf_op jit(solution)/shard_map/ppermute | solution.py:523
  48.7 30.4 %copy-start = (bf16[512,512]{1,0:T(8,128)(2,1)S(1)}, bf16[512,512]{1,0:T(8,128)(2,1)}, u32[]{:S(2)}) copy-start(bf16[512,512]{1,0:T(8,128)(2,1)} %refs_8_.3) | copy-start | bytes 1572868
  48.7 30.4 %copy-start.3 = (bf16[512,1024]{1,0:T(8,128)(2,1)S(1)}, bf16[512,1024]{1,0:T(8,128)(2,1)}, u32[]{:S(2)}) copy-start(bf16[512,1024]{1,0:T(8,128)(2,1)} %refs_4_.1) | copy-start | bytes 3145732
  48.7 30.4 %copy-start.5 = (bf16[1024,512]{1,0:T(8,128)(2,1)S(1)}, bf16[1024,512]{1,0:T(8,128)(2,1)}, u32[]{:S(2)}) copy-start(bf16[1024,512]{1,0:T(8,128)(2,1)} %get-tuple-element.60.refs_3_) | copy-start | bytes 3145732
  48.7 30.4 %copy-start.6 = (bf16[1024,512]{1,0:T(8,128)(2,1)S(1)}, bf16[1024,512]{1,0:T(8,128)(2,1)}, u32[]{:S(2)}) copy-start(bf16[1024,512]{1,0:T(8,128)(2,1)} %get-tuple-element.59.refs_2_) | copy-start | bytes 3145732
  48.7 9.2 %collective-permute-start.7 = (bf16[128,512]{1,0:T(8,128)(2,1)S(1)}, bf16[128,512]{1,0:T(8,128)(2,1)S(1)}, u32[]{:S(2)}, u32[]{:S(2)}) collective-permute-start(bf16[128,512]{1,0:T(8,128)(2,1)S(1)} %constant_dynamic-update-slice_fusion), channel_id=1, source_target_pairs={{0,8},{8,0},{16,24},{24,16},{1,9},{9,1},{17,25},{25,17},{2,10},{10... | collective-permute-start | bytes 393224 | tf_op jit(solution)/shard_map/ppermute | solution.py:538
  57.9 19.7 %collective-permute-start.15 = (bf16[256,512]{1,0:T(8,128)(2,1)S(1)}, bf16[256,512]{1,0:T(8,128)(2,1)S(1)}, u32[]{:S(2)}, u32[]{:S(2)}) collective-permute-start(bf16[256,512]{1,0:T(8,128)(2,1)S(1)} %constant_dynamic-update-slice_fusion.8.refs_0_), channel_id=1, source_target_pairs={{0,16},{8,24},{16,0},{24,8},{1,17},{9,25},{17,1},{25,9},{2,18},{10... | collective-permute-start | bytes 786440 | tf_op jit(solution)/shard_map/ppermute | solution.py:546
  59.5 7.7 %collective-permute-start.8 = (bf16[128,512]{1,0:T(8,128)(2,1)S(1)}, bf16[128,512]{1,0:T(8,128)(2,1)S(1)}, u32[]{:S(2)}, u32[]{:S(2)}) collective-permute-start(bf16[128,512]{1,0:T(8,128)(2,1)S(1)} %get-tuple-element.49), channel_id=1, source_target_pairs={{7,0},{6,1},{5,2},{4,3},{3,4},{2,5},{1,6},{0,7},{15,8},{14,9},{13,... | collective-permute-start | bytes 393224 | tf_op jit(solution)/shard_map/ppermute | solution.py:523
  60.9 9.1 %collective-permute-start.9 = (bf16[128,512]{1,0:T(8,128)(2,1)S(1)}, bf16[128,512]{1,0:T(8,128)(2,1)S(1)}, u32[]{:S(2)}, u32[]{:S(2)}) collective-permute-start(bf16[128,512]{1,0:T(8,128)(2,1)S(1)} %get-tuple-element.50), channel_id=1, source_target_pairs={{6,0},{7,1},{4,2},{5,3},{2,4},{3,5},{0,6},{1,7},{14,8},{15,9},{12,... | collective-permute-start | bytes 393224 | tf_op jit(solution)/shard_map/ppermute | solution.py:523
  62.7 21.0 %collective-permute-start.10 = (bf16[128,512]{1,0:T(8,128)(2,1)S(1)}, bf16[128,512]{1,0:T(8,128)(2,1)S(1)}, u32[]{:S(2)}, u32[]{:S(2)}) collective-permute-start(bf16[128,512]{1,0:T(8,128)(2,1)S(1)} %get-tuple-element.51), channel_id=1, source_target_pairs={{5,0},{4,1},{7,2},{6,3},{1,4},{0,5},{3,6},{2,7},{13,8},{12,9},{15,... | collective-permute-start | bytes 393224 | tf_op jit(solution)/shard_map/ppermute | solution.py:523
  62.7 21.0 %collective-permute-start.11 = (bf16[128,512]{1,0:T(8,128)(2,1)S(1)}, bf16[128,512]{1,0:T(8,128)(2,1)S(1)}, u32[]{:S(2)}, u32[]{:S(2)}) collective-permute-start(bf16[128,512]{1,0:T(8,128)(2,1)S(1)} %get-tuple-element.52), channel_id=1, source_target_pairs={{4,0},{5,1},{6,2},{7,3},{0,4},{1,5},{2,6},{3,7},{12,8},{13,9},{14,... | collective-permute-start | bytes 393224 | tf_op jit(solution)/shard_map/ppermute | solution.py:523
  67.2 16.5 %collective-permute-start.12 = (bf16[128,512]{1,0:T(8,128)(2,1)S(1)}, bf16[128,512]{1,0:T(8,128)(2,1)S(1)}, u32[]{:S(2)}, u32[]{:S(2)}) collective-permute-start(bf16[128,512]{1,0:T(8,128)(2,1)S(1)} %get-tuple-element.53), channel_id=1, source_target_pairs={{3,0},{2,1},{1,2},{0,3},{7,4},{6,5},{5,6},{4,7},{11,8},{10,9},{9,1... | collective-permute-start | bytes 393224 | tf_op jit(solution)/shard_map/ppermute | solution.py:523
  70.0 17.5 %collective-permute-start.13 = (bf16[128,512]{1,0:T(8,128)(2,1)S(1)}, bf16[128,512]{1,0:T(8,128)(2,1)S(1)}, u32[]{:S(2)}, u32[]{:S(2)}) collective-permute-start(bf16[128,512]{1,0:T(8,128)(2,1)S(1)} %get-tuple-element.54), channel_id=1, source_target_pairs={{2,0},{3,1},{0,2},{1,3},{6,4},{7,5},{4,6},{5,7},{10,8},{11,9},{8,1... | collective-permute-start | bytes 393224 | tf_op jit(solution)/shard_map/ppermute | solution.py:523
  77.6 9.9 %collective-permute-start.14 = (bf16[128,512]{1,0:T(8,128)(2,1)S(1)}, bf16[128,512]{1,0:T(8,128)(2,1)S(1)}, u32[]{:S(2)}, u32[]{:S(2)}) collective-permute-start(bf16[128,512]{1,0:T(8,128)(2,1)S(1)} %get-tuple-element.55), channel_id=1, source_target_pairs={{1,0},{0,1},{3,2},{2,3},{5,4},{4,5},{7,6},{6,7},{9,8},{8,9},{11,10... | collective-permute-start | bytes 393224 | tf_op jit(solution)/shard_map/ppermute | solution.py:523
  79.1 8.4 %copy-start.1 = (s32[1,8]{1,0:T(1,128)S(1)}, s32[1,8]{1,0:T(1,128)}, u32[]{:S(2)}) copy-start(s32[1,8]{1,0:T(1,128)} %pick_ref.1) | copy-start | bytes 100

commit v7 on v6

--- a/solution.py
+++ b/solution.py
@@ -444,9 +444,9 @@
     )(*pools, h, z, w_comp, w_in, w_out)
 
 
-def final_kernel(peers, cap, bounds, pick_ref, *refs):
+def final_kernel(peers, cap, flow, bounds, pick_ref, *refs):
     parts = len(bounds)
-    back = [refs[p * peers : (p + 1) * peers][::-1] for p in range(parts)]
+    back = [dict(zip(flow, refs[p * peers : (p + 1) * peers])) for p in range(parts)]
     w_out, base, out, m_s, o_s, out_sem = refs[parts * peers :]
     blocks = base.shape[0] // LEAF
     me = lax.axis_index("pts").astype(jnp.int32)
@@ -471,10 +471,10 @@
     wait_all(outgoing)
 
 
-def final(peers, cap, bounds, pick, back, w_out, base):
+def final(peers, cap, flow, bounds, pick, back, w_out, base):
     rows, width = base.shape
     return pl.pallas_call(
-        partial(final_kernel, peers, cap, bounds),
+        partial(final_kernel, peers, cap, flow, bounds),
         out_shape=jax.ShapeDtypeStruct((rows, width), BF16),
         in_specs=[SMEM] + [VMEM] * (peers * len(bounds) + 2),
         out_specs=ANY,
@@ -525,7 +525,8 @@
     z, h, *sends = layer_one(peers, cap, send_pick, ball_ids, gains, points, weights)
     sends[0] = jnp.where(recv_from[0, 0] >= 0, sends[0], jnp.zeros_like(sends[0]))
     arrived = [travel(sends[s], s, False) for s in range(peers)]
-    flow = [*range(peers - 1, 4, -1), *(s for s in (2, 1, 4, 3, 0) if s < peers)]
+    flow = [*range(peers - 1, 5, -1), *(s for s in (3, 2, 1, 5, 4, 0) if s < peers)]
+    home = [*range(peers - 1, 4, -1), *(s for s in (2, 1, 4, 3, 0) if s < peers)]
     tail = sends[0].shape[0] - cap * LEAF
     first = [s for s in (1, 2, 3, 0) if s < peers]
     last = list(range(peers - 1, 3, -1))
@@ -539,15 +540,18 @@
     mixed = layer_two(peers, cap, flow, 0, width, recv_from, arrived, attn_in_two)
     mixed, pools = lax.optimization_barrier((mixed, pools))
     bounds = [(0, width)]
-    back = [travel(mixed[s], s, True) for s in range(peers - 1, -1, -1)]
+    back = {s: travel(mixed[s], s, True) for s in home}
     bit = 2
     while doubles and bit < groups:
         both = jnp.concatenate(pools)
         pools = [both, lax.ppermute(both, "grp", [(i, i ^ bit) for i in range(groups)])]
         bit *= 2
     local = points.shape[0] // CMP
+    soon = [back[s] for s in (1, 2) if s < peers]
+    z, soon = lax.optimization_barrier((z, soon))
+    back.update(zip((1, 2), soon))
     base = compressed(tail, local, pools, h, z, compress_proj, attn_in_two, attn_out_two)
-    return final(peers, cap, bounds, send_pick, back, attn_out_two, base)
+    return final(peers, cap, home, bounds, send_pick, [back[s] for s in home], attn_out_two, base)
 
 
 def solution(mesh):

time: 90 us -> 88.9 us (0.988)
  transfers between devices with their start and end apart: 16 -> 16, of which waited for: 6 -> 7; matrix products, arithmetic and copies ran while one was open for 1% -> 1% of each run, Pallas kernels for 14% -> 14%
where the time goes in v7:
time: 88.9 us; the launch traced here: 88.7 us
  Pallas kernels  31.7 us (36%)
  starting transfers between devices  28.7 us (32%)
  waiting for transfers between devices  27 us (30%)
  other arithmetic  0.93 us (1%)
    ppermute x14, waiting for transfers between devices, travel(): return lax.ppermute(blocks, 'pts', pattern)  27 us
    ppermute x14, starting transfers between devices, travel(): return lax.ppermute(blocks, 'pts', pattern)  25.6 us
    pallas_call x1, Pallas kernels, layer_one(): pl.pallas_call(partial(layer_one_kernel, peers, cap), out_shape=[whole, w...  17.4 us
    pallas_call x1, Pallas kernels, layer_two(): pl.pallas_call(partial(layer_two_kernel, peers, cap, flow, blocks, start,...  7.64 us
    pallas_call x1, Pallas kernels, compressed(): pl.pallas_call(partial(compressed_kernel, len(pools), tail, local), out_s...  4.55 us
    pallas_call x1, Pallas kernels, final(): pl.pallas_call(partial(final_kernel, peers, cap, flow, bounds), out_shape...  2.12 us
  transfers between devices with their start and end apart: 16, of which 7 were waited for; matrix products, arithmetic and copies ran while one was open for 1% of the time, Pallas kernels for 14%

profile of v7, /device:TPU:0, one launch (start us, length us, event | category | flops | bytes accessed | tf_op | source)
XLA Modules:
  0.0 88.7 jit_solution(446411813453132780)
XLA Ops:
  0.0 17.4 %layer_one.1 = (bf16[1024,512]{1,0:T(8,128)(2,1)}, bf16[1024,512]{1,0:T(8,128)(2,1)}, bf16[144,512]{1,0:T(8,128)(2,1)}, bf16[144,512]{1,0:T(8,128)(2,1)}, bf16[1...) custom-call(s32[1,8]{1,0:T(1,128)} %pick_ref.1, ...), custom_call_target="tpu_custom_call" | custom-call | flops 10737418240 | bytes 10485760 | tf_op jit(solution)/shard_map/layer_one/pallas_call | solution.py:236
  17.4 4.6 %collective-permute-start = (bf16[144,512]{1,0:T(8,128)(2,1)}, bf16[144,512]{1,0:T(8,128)(2,1)S(1)}, u32[]{:S(2)}, u32[]{:S(2)}) collective-permute-start(bf16[144,512]{1,0:T(8,128)(2,1)} %get-tuple-element.36), channel_id=1, source_target_pairs={{0,7},{1,6},{2,5},{3,4},{4,3},{5,2},{6,1},{7,0},{8,15},{9,14},{10,... | collective-permute-start | bytes 442376 | tf_op jit(solution)/shard_map/ppermute | solution.py:523
  22.0 0.7 collective-permute-start.1
  22.6 1.7 %collective-permute-start.3 = (bf16[144,512]{1,0:T(8,128)(2,1)}, bf16[144,512]{1,0:T(8,128)(2,1)S(1)}, u32[]{:S(2)}, u32[]{:S(2)}) collective-permute-start(bf16[144,512]{1,0:T(8,128)(2,1)} %get-tuple-element.39), channel_id=1, source_target_pairs={{0,2},{1,3},{2,0},{3,1},{4,6},{5,7},{6,4},{7,5},{8,10},{9,11},{10,... | collective-permute-start | bytes 442376 | tf_op jit(solution)/shard_map/ppermute | solution.py:523
  24.5 0.9 %broadcast_select_fusion.refs_8_ = bf16[144,512]{1,0:T(8,128)(2,1)S(1)} fusion(bf16[144,512]{1,0:T(8,128)(2,1)} %get-tuple-element.43, pred[]{:T(512)} %bitcast.3), kind=kLoop, calls=%fused_computation | loop fusion | flops 73728 | bytes 294913 | tf_op jit(solution)/shard_map/jit(_where)/select_n | solution.py:526
  25.5 0.4 collective-permute-done.4.refs_5_
  25.9 1.9 %collective-permute-start.5 = (bf16[144,512]{1,0:T(8,128)(2,1)}, bf16[144,512]{1,0:T(8,128)(2,1)S(1)}, u32[]{:S(2)}, u32[]{:S(2)}) collective-permute-start(bf16[144,512]{1,0:T(8,128)(2,1)} %get-tuple-element.41), channel_id=1, source_target_pairs={{0,5},{1,4},{2,7},{3,6},{4,1},{5,0},{6,3},{7,2},{8,13},{9,12},{10,... | collective-permute-start | bytes 442376 | tf_op jit(solution)/shard_map/ppermute | solution.py:523
  27.7 9.5 %collective-permute-done.3.refs_4_ = bf16[144,512]{1,0:T(8,128)(2,1)S(1)} collective-permute-done((bf16[144,512]{1,0:T(8,128)(2,1)}, bf16[144,512]{1,0:T(8,128)(2,1)S(1)}, u32[]{:S(2)}, u32[]{:S(2)}) %collective-permute-start.3) | collective-permute-done | bytes 147488 | tf_op jit(solution)/shard_map/ppermute | solution.py:523
  37.3 3.3 %collective-permute-start.6 = (bf16[144,512]{1,0:T(8,128)(2,1)}, bf16[144,512]{1,0:T(8,128)(2,1)S(1)}, u32[]{:S(2)}, u32[]{:S(2)}) collective-permute-start(bf16[144,512]{1,0:T(8,128)(2,1)} %get-tuple-element.42), channel_id=1, source_target_pairs={{0,4},{1,5},{2,6},{3,7},{4,0},{5,1},{6,2},{7,3},{8,12},{9,13},{10,... | collective-permute-start | bytes 442376 | tf_op jit(solution)/shard_map/ppermute | solution.py:523
  40.6 1.4 %collective-permute-done.5.refs_6_ = bf16[144,512]{1,0:T(8,128)(2,1)S(1)} collective-permute-done((bf16[144,512]{1,0:T(8,128)(2,1)}, bf16[144,512]{1,0:T(8,128)(2,1)S(1)}, u32[]{:S(2)}, u32[]{:S(2)}) %collective-permute-start.5) | collective-permute-done | bytes 147488 | tf_op jit(solution)/shard_map/ppermute | solution.py:523
  42.0 6.4 %collective-permute-done.6.refs_7_ = bf16[144,512]{1,0:T(8,128)(2,1)S(1)} collective-permute-done((bf16[144,512]{1,0:T(8,128)(2,1)}, bf16[144,512]{1,0:T(8,128)(2,1)S(1)}, u32[]{:S(2)}, u32[]{:S(2)}) %collective-permute-start.6) | collective-permute-done | bytes 147488 | tf_op jit(solution)/shard_map/ppermute | solution.py:523
  48.4 1.6 %collective-permute-start.7 = (bf16[128,512]{1,0:T(8,128)(2,1)S(1)}, bf16[128,512]{1,0:T(8,128)(2,1)S(1)}, u32[]{:S(2)}, u32[]{:S(2)}) collective-permute-start(bf16[128,512]{1,0:T(8,128)(2,1)S(1)} %constant_dynamic-update-slice_fusion), channel_id=1, source_target_pairs={{0,8},{8,0},{16,24},{24,16},{1,9},{9,1},{17,25},{25,17},{2,10},{10... | collective-permute-start | bytes 393224 | tf_op jit(solution)/shard_map/ppermute | solution.py:539
  50.0 7.6 %layer_two_0.1 = (bf16[128,512]{1,0:T(8,128)(2,1)S(1)}, bf16[128,512]{1,0:T(8,128)(2,1)S(1)}, bf16[128,512]{1,0:T(8,128)(2,1)S(1)}, bf16[128,512]{1,0:T(8,128)(2...) custom-call(s32[1,8]{1,0:T(1,128)S(1)} %copy-done.4, ...), custom_call_target="tpu_custom_call" | custom-call | flops 5905580032 | bytes 4194304 | tf_op jit(solution)/shard_map/layer_two_0/pallas_call | solution.py:335
  57.7 1.6 %collective-permute-start.15 = (bf16[256,512]{1,0:T(8,128)(2,1)S(1)}, bf16[256,512]{1,0:T(8,128)(2,1)S(1)}, u32[]{:S(2)}, u32[]{:S(2)}) collective-permute-start(bf16[256,512]{1,0:T(8,128)(2,1)S(1)} %constant_dynamic-update-slice_fusion.8.refs_0_), channel_id=1, source_target_pairs={{0,16},{8,24},{16,0},{24,8},{1,17},{9,25},{17,1},{25,9},{2,18},{10... | collective-permute-start | bytes 786440 | tf_op jit(solution)/shard_map/ppermute | solution.py:547
  59.6 2.8 %collective-permute-start.8 = (bf16[128,512]{1,0:T(8,128)(2,1)S(1)}, bf16[128,512]{1,0:T(8,128)(2,1)S(1)}, u32[]{:S(2)}, u32[]{:S(2)}) collective-permute-start(bf16[128,512]{1,0:T(8,128)(2,1)S(1)} %get-tuple-element.52), channel_id=1, source_target_pairs={{7,0},{6,1},{5,2},{4,3},{3,4},{2,5},{1,6},{0,7},{15,8},{14,9},{13,... | collective-permute-start | bytes 393224 | tf_op jit(solution)/shard_map/ppermute | solution.py:523
  62.5 0.8 collective-permute-start.9
  63.3 1.1 %collective-permute-start.10 = (bf16[128,512]{1,0:T(8,128)(2,1)S(1)}, bf16[128,512]{1,0:T(8,128)(2,1)S(1)}, u32[]{:S(2)}, u32[]{:S(2)}) collective-permute-start(bf16[128,512]{1,0:T(8,128)(2,1)S(1)} %get-tuple-element.54), channel_id=1, source_target_pairs={{5,0},{4,1},{7,2},{6,3},{1,4},{0,5},{3,6},{2,7},{13,8},{12,9},{15,... | collective-permute-start | bytes 393224 | tf_op jit(solution)/shard_map/ppermute | solution.py:523
  64.4 0.8 collective-permute-done.12.refs_3_
  65.2 6.8 %collective-permute-start.13 = (bf16[128,512]{1,0:T(8,128)(2,1)S(1)}, bf16[128,512]{1,0:T(8,128)(2,1)S(1)}, u32[]{:S(2)}, u32[]{:S(2)}) collective-permute-start(bf16[128,512]{1,0:T(8,128)(2,1)S(1)} %get-tuple-element.60), channel_id=1, source_target_pairs={{4,0},{5,1},{6,2},{7,3},{0,4},{1,5},{2,6},{3,7},{12,8},{13,9},{14,... | collective-permute-start | bytes 393224 | tf_op jit(solution)/shard_map/ppermute | solution.py:523
  72.0 1.5 %collective-permute-start.14 = (bf16[128,512]{1,0:T(8,128)(2,1)S(1)}, bf16[128,512]{1,0:T(8,128)(2,1)S(1)}, u32[]{:S(2)}, u32[]{:S(2)}) collective-permute-start(bf16[128,512]{1,0:T(8,128)(2,1)S(1)} %get-tuple-element.61), channel_id=1, source_target_pairs={{3,0},{2,1},{1,2},{0,3},{7,4},{6,5},{5,6},{4,7},{11,8},{10,9},{9,1... | collective-permute-start | bytes 393224 | tf_op jit(solution)/shard_map/ppermute | solution.py:523
  73.5 4.6 %compressed.1.refs_9_ = f32[1024,512]{1,0:T(8,128)S(1)} custom-call(bf16[256,512]{1,0:T(8,128)(2,1)S(1)} %constant_dynamic-update-slice_fusion.8.refs_0_, bf16[256,512]{1,0:T(8,128)(2,1)S(1)} %collective-permute-done.15.refs_1_, bf16[1024,512]{1,0:T(8,128)(2,1)S(1)} %copy-done.6, bf16[1024,512]{1,0:T(8,128)(2,1)S(1)} %copy-done.5, ...), custom_call_target="tpu_custom_call" | custom-call | flops 2147483648 | bytes 8388608 | tf_op jit(solution)/shard_map/compressed/pallas_call | solution.py:416
  78.1 5.2 %collective-permute-done.10.refs_2_ = bf16[128,512]{1,0:T(8,128)(2,1)S(1)} collective-permute-done((bf16[128,512]{1,0:T(8,128)(2,1)S(1)}, bf16[128,512]{1,0:T(8,128)(2,1)S(1)}, u32[]{:S(2)}, u32[]{:S(2)}) %collective-permute-start.10) | collective-permute-done | bytes 131104 | tf_op jit(solution)/shard_map/ppermute | solution.py:523
  83.3 3.2 %collective-permute-done.13.refs_5_ = bf16[128,512]{1,0:T(8,128)(2,1)S(1)} collective-permute-done((bf16[128,512]{1,0:T(8,128)(2,1)S(1)}, bf16[128,512]{1,0:T(8,128)(2,1)S(1)}, u32[]{:S(2)}, u32[]{:S(2)}) %collective-permute-start.13) | collective-permute-done | bytes 131104 | tf_op jit(solution)/shard_map/ppermute | solution.py:523
  86.5 2.1 %last_product.1 = bf16[1024,512]{1,0:T(8,128)(2,1)} custom-call(s32[1,8]{1,0:T(1,128)S(1)} %copy-done.1, bf16[128,512]{1,0:T(8,128)(2,1)S(1)} %collective-permute-done.8.refs_0_, bf16[128,512]{1,0:T(8,128)(2,1)S(1)} %collective-permute-done.9.refs_1_, bf16[128,512]{1,0:T(8,128)(2,1)S(1)} %collective-permute-done.10.refs_2_, ...), custom_call_target="tpu_custom_call" | custom-call | flops 536870912 | bytes 4194304 | tf_op jit(solution)/shard_map/last_product/pallas_call | solution.py:476
  (37 shorter events, 0.7 us)
Async XLA Ops:
  0.0 24.5 %copy-start.4 = (s32[1,8]{1,0:T(1,128)S(1)}, s32[1,8]{1,0:T(1,128)}, u32[]{:S(2)}) copy-start(s32[1,8]{1,0:T(1,128)} %refs_0_.3) | copy-start | bytes 100
  0.0 50.0 %copy-start.2 = (bf16[512,1536]{1,0:T(8,128)(2,1)S(1)}, bf16[512,1536]{1,0:T(8,128)(2,1)}, u32[]{:S(2)}) copy-start(bf16[512,1536]{1,0:T(8,128)(2,1)} %refs_5_.3) | copy-start | bytes 4718596
  17.4 23.1 %collective-permute-start = (bf16[144,512]{1,0:T(8,128)(2,1)}, bf16[144,512]{1,0:T(8,128)(2,1)S(1)}, u32[]{:S(2)}, u32[]{:S(2)}) collective-permute-start(bf16[144,512]{1,0:T(8,128)(2,1)} %get-tuple-element.36), channel_id=1, source_target_pairs={{0,7},{1,6},{2,5},{3,4},{4,3},{5,2},{6,1},{7,0},{8,15},{9,14},{10,... | collective-permute-start | bytes 442376 | tf_op jit(solution)/shard_map/ppermute | solution.py:523
  22.0 18.6 %collective-permute-start.1 = (bf16[144,512]{1,0:T(8,128)(2,1)}, bf16[144,512]{1,0:T(8,128)(2,1)S(1)}, u32[]{:S(2)}, u32[]{:S(2)}) collective-permute-start(bf16[144,512]{1,0:T(8,128)(2,1)} %get-tuple-element.37), channel_id=1, source_target_pairs={{0,6},{1,7},{2,4},{3,5},{4,2},{5,3},{6,0},{7,1},{8,14},{9,15},{10,... | collective-permute-start | bytes 442376 | tf_op jit(solution)/shard_map/ppermute | solution.py:523
  22.6 17.9 %collective-permute-start.2 = (bf16[144,512]{1,0:T(8,128)(2,1)}, bf16[144,512]{1,0:T(8,128)(2,1)S(1)}, u32[]{:S(2)}, u32[]{:S(2)}) collective-permute-start(bf16[144,512]{1,0:T(8,128)(2,1)} %get-tuple-element.38), channel_id=1, source_target_pairs={{0,3},{1,2},{2,1},{3,0},{4,7},{5,6},{6,5},{7,4},{8,11},{9,10},{10,... | collective-permute-start | bytes 442376 | tf_op jit(solution)/shard_map/ppermute | solution.py:523
  22.6 14.6 %collective-permute-start.3 = (bf16[144,512]{1,0:T(8,128)(2,1)}, bf16[144,512]{1,0:T(8,128)(2,1)S(1)}, u32[]{:S(2)}, u32[]{:S(2)}) collective-permute-start(bf16[144,512]{1,0:T(8,128)(2,1)} %get-tuple-element.39), channel_id=1, source_target_pairs={{0,2},{1,3},{2,0},{3,1},{4,6},{5,7},{6,4},{7,5},{8,10},{9,11},{10,... | collective-permute-start | bytes 442376 | tf_op jit(solution)/shard_map/ppermute | solution.py:523
  24.3 1.6 %collective-permute-start.4 = (bf16[144,512]{1,0:T(8,128)(2,1)}, bf16[144,512]{1,0:T(8,128)(2,1)S(1)}, u32[]{:S(2)}, u32[]{:S(2)}) collective-permute-start(bf16[144,512]{1,0:T(8,128)(2,1)} %get-tuple-element.40), channel_id=1, source_target_pairs={{0,1},{1,0},{2,3},{3,2},{4,5},{5,4},{6,7},{7,6},{8,9},{9,8},{10,11... | collective-permute-start | bytes 442376 | tf_op jit(solution)/shard_map/ppermute | solution.py:523
  25.9 16.1 %collective-permute-start.5 = (bf16[144,512]{1,0:T(8,128)(2,1)}, bf16[144,512]{1,0:T(8,128)(2,1)S(1)}, u32[]{:S(2)}, u32[]{:S(2)}) collective-permute-start(bf16[144,512]{1,0:T(8,128)(2,1)} %get-tuple-element.41), channel_id=1, source_target_pairs={{0,5},{1,4},{2,7},{3,6},{4,1},{5,0},{6,3},{7,2},{8,13},{9,12},{10,... | collective-permute-start | bytes 442376 | tf_op jit(solution)/shard_map/ppermute | solution.py:523
  37.3 11.1 %collective-permute-start.6 = (bf16[144,512]{1,0:T(8,128)(2,1)}, bf16[144,512]{1,0:T(8,128)(2,1)S(1)}, u32[]{:S(2)}, u32[]{:S(2)}) collective-permute-start(bf16[144,512]{1,0:T(8,128)(2,1)} %get-tuple-element.42), channel_id=1, source_target_pairs={{0,4},{1,5},{2,6},{3,7},{4,0},{5,1},{6,2},{7,3},{8,12},{9,13},{10,... | collective-permute-start | bytes 442376 | tf_op jit(solution)/shard_map/ppermute | solution.py:523
  48.4 25.1 %copy-start = (bf16[512,512]{1,0:T(8,128)(2,1)S(1)}, bf16[512,512]{1,0:T(8,128)(2,1)}, u32[]{:S(2)}) copy-start(bf16[512,512]{1,0:T(8,128)(2,1)} %refs_8_.3) | copy-start | bytes 1572868
  48.4 25.1 %copy-start.3 = (bf16[512,1024]{1,0:T(8,128)(2,1)S(1)}, bf16[512,1024]{1,0:T(8,128)(2,1)}, u32[]{:S(2)}) copy-start(bf16[512,1024]{1,0:T(8,128)(2,1)} %refs_4_.1) | copy-start | bytes 3145732
  48.4 25.1 %copy-start.5 = (bf16[1024,512]{1,0:T(8,128)(2,1)S(1)}, bf16[1024,512]{1,0:T(8,128)(2,1)}, u32[]{:S(2)}) copy-start(bf16[1024,512]{1,0:T(8,128)(2,1)} %get-tuple-element.66.refs_3_) | copy-start | bytes 3145732
  48.4 25.1 %copy-start.6 = (bf16[1024,512]{1,0:T(8,128)(2,1)S(1)}, bf16[1024,512]{1,0:T(8,128)(2,1)}, u32[]{:S(2)}) copy-start(bf16[1024,512]{1,0:T(8,128)(2,1)} %get-tuple-element.65.refs_2_) | copy-start | bytes 3145732
  48.4 9.2 %collective-permute-start.7 = (bf16[128,512]{1,0:T(8,128)(2,1)S(1)}, bf16[128,512]{1,0:T(8,128)(2,1)S(1)}, u32[]{:S(2)}, u32[]{:S(2)}) collective-permute-start(bf16[128,512]{1,0:T(8,128)(2,1)S(1)} %constant_dynamic-update-slice_fusion), channel_id=1, source_target_pairs={{0,8},{8,0},{16,24},{24,16},{1,9},{9,1},{17,25},{25,17},{2,10},{10... | collective-permute-start | bytes 393224 | tf_op jit(solution)/shard_map/ppermute | solution.py:539
  57.7 14.3 %collective-permute-start.15 = (bf16[256,512]{1,0:T(8,128)(2,1)S(1)}, bf16[256,512]{1,0:T(8,128)(2,1)S(1)}, u32[]{:S(2)}, u32[]{:S(2)}) collective-permute-start(bf16[256,512]{1,0:T(8,128)(2,1)S(1)} %constant_dynamic-update-slice_fusion.8.refs_0_), channel_id=1, source_target_pairs={{0,16},{8,24},{16,0},{24,8},{1,17},{9,25},{17,1},{25,9},{2,18},{10... | collective-permute-start | bytes 786440 | tf_op jit(solution)/shard_map/ppermute | solution.py:547
  59.3 4.0 %collective-permute-start.11 = (bf16[128,512]{1,0:T(8,128)(2,1)S(1)}, bf16[128,512]{1,0:T(8,128)(2,1)S(1)}, u32[]{:S(2)}, u32[]{:S(2)}) collective-permute-start(bf16[128,512]{1,0:T(8,128)(2,1)S(1)} %get-tuple-element.56), channel_id=1, source_target_pairs={{1,0},{0,1},{3,2},{2,3},{5,4},{4,5},{7,6},{6,7},{9,8},{8,9},{11,10... | collective-permute-start | bytes 393224 | tf_op jit(solution)/shard_map/ppermute | solution.py:523
  59.3 5.9 %collective-permute-start.12 = (bf16[128,512]{1,0:T(8,128)(2,1)S(1)}, bf16[128,512]{1,0:T(8,128)(2,1)S(1)}, u32[]{:S(2)}, u32[]{:S(2)}) collective-permute-start(bf16[128,512]{1,0:T(8,128)(2,1)S(1)} %get-tuple-element.57), channel_id=1, source_target_pairs={{2,0},{3,1},{0,2},{1,3},{6,4},{7,5},{4,6},{5,7},{10,8},{11,9},{8,1... | collective-permute-start | bytes 393224 | tf_op jit(solution)/shard_map/ppermute | solution.py:523
  59.6 18.4 %collective-permute-start.8 = (bf16[128,512]{1,0:T(8,128)(2,1)S(1)}, bf16[128,512]{1,0:T(8,128)(2,1)S(1)}, u32[]{:S(2)}, u32[]{:S(2)}) collective-permute-start(bf16[128,512]{1,0:T(8,128)(2,1)S(1)} %get-tuple-element.52), channel_id=1, source_target_pairs={{7,0},{6,1},{5,2},{4,3},{3,4},{2,5},{1,6},{0,7},{15,8},{14,9},{13,... | collective-permute-start | bytes 393224 | tf_op jit(solution)/shard_map/ppermute | solution.py:523
  62.5 15.6 %collective-permute-start.9 = (bf16[128,512]{1,0:T(8,128)(2,1)S(1)}, bf16[128,512]{1,0:T(8,128)(2,1)S(1)}, u32[]{:S(2)}, u32[]{:S(2)}) collective-permute-start(bf16[128,512]{1,0:T(8,128)(2,1)S(1)} %get-tuple-element.53), channel_id=1, source_target_pairs={{6,0},{7,1},{4,2},{5,3},{2,4},{3,5},{0,6},{1,7},{14,8},{15,9},{12,... | collective-permute-start | bytes 393224 | tf_op jit(solution)/shard_map/ppermute | solution.py:523
  63.3 20.0 %collective-permute-start.10 = (bf16[128,512]{1,0:T(8,128)(2,1)S(1)}, bf16[128,512]{1,0:T(8,128)(2,1)S(1)}, u32[]{:S(2)}, u32[]{:S(2)}) collective-permute-start(bf16[128,512]{1,0:T(8,128)(2,1)S(1)} %get-tuple-element.54), channel_id=1, source_target_pairs={{5,0},{4,1},{7,2},{6,3},{1,4},{0,5},{3,6},{2,7},{13,8},{12,9},{15,... | collective-permute-start | bytes 393224 | tf_op jit(solution)/shard_map/ppermute | solution.py:523
  65.2 21.3 %collective-permute-start.13 = (bf16[128,512]{1,0:T(8,128)(2,1)S(1)}, bf16[128,512]{1,0:T(8,128)(2,1)S(1)}, u32[]{:S(2)}, u32[]{:S(2)}) collective-permute-start(bf16[128,512]{1,0:T(8,128)(2,1)S(1)} %get-tuple-element.60), channel_id=1, source_target_pairs={{4,0},{5,1},{6,2},{7,3},{0,4},{1,5},{2,6},{3,7},{12,8},{13,9},{14,... | collective-permute-start | bytes 393224 | tf_op jit(solution)/shard_map/ppermute | solution.py:523
  72.0 14.5 %collective-permute-start.14 = (bf16[128,512]{1,0:T(8,128)(2,1)S(1)}, bf16[128,512]{1,0:T(8,128)(2,1)S(1)}, u32[]{:S(2)}, u32[]{:S(2)}) collective-permute-start(bf16[128,512]{1,0:T(8,128)(2,1)S(1)} %get-tuple-element.61), channel_id=1, source_target_pairs={{3,0},{2,1},{1,2},{0,3},{7,4},{6,5},{5,6},{4,7},{11,8},{10,9},{9,1... | collective-permute-start | bytes 393224 | tf_op jit(solution)/shard_map/ppermute | solution.py:523
  73.5 13.0 %copy-start.1 = (s32[1,8]{1,0:T(1,128)S(1)}, s32[1,8]{1,0:T(1,128)}, u32[]{:S(2)}) copy-start(s32[1,8]{1,0:T(1,128)} %pick_ref.1) | copy-start | bytes 100
